TPU v7x, 128 devices: a whole 4x4x4 slice. The times are simulated.
128 devices in a mesh: seq: 8 (over z, x_hi), fsdp: 16 (over y, x_lo, core).
Axes of the slice: x: 4 (x_hi: 2, x_lo: 2; x = x_hi * 2 + x_lo), y: 4, z: 4, core: 2. Of those that a mesh axis runs over, the one named last changes fastest.
Arguments:
- tokens: bfloat16 [16, 1024, 1024], P('fsdp', 'seq'), may hold values from -6 to 6
- segments: int32 [16, 1024], P('fsdp'), may hold values from 0 to 3, as said below
- norm_input: bfloat16 [1024], P('fsdp'), may hold values from 0.25 to 1.75
- w_query: bfloat16 [1024, 2048], P('fsdp'), may hold values from -0.1875 to 0.1875
- w_key: bfloat16 [1024, 1024], P('fsdp'), may hold values from -0.1875 to 0.1875
- w_value: bfloat16 [1024, 1024], P('fsdp'), may hold values from -0.1875 to 0.1875
- norm_query: bfloat16 [128], P('fsdp'), may hold values from 0.25 to 1.75
- norm_key: bfloat16 [128], P('fsdp'), may hold values from 0.25 to 1.75
- w_output: bfloat16 [2048, 1024], P(None, 'fsdp'), may hold values from -1 to 1
- norm_post: bfloat16 [1024], P('fsdp'), may hold values from 0.25 to 1.75
- w_gate: bfloat16 [1024, 3072], P('fsdp'), may hold values from -0.1875 to 0.1875
- w_up: bfloat16 [1024, 3072], P('fsdp'), may hold values from -0.1875 to 0.1875
- w_down: bfloat16 [3072, 1024], P(None, 'fsdp'), may hold values from -0.109375 to 0.109375
- cotangent: bfloat16 [16, 1024, 1024], P('fsdp', 'seq'), may hold values from -6 to 6
Outputs:
- output: bfloat16 [16, 1024, 1024], P('fsdp', 'seq')
- grad_tokens: float32 [16, 1024, 1024], P('fsdp', 'seq')
- grad_norm_input: float32 [1024], P('fsdp')
- grad_query: float32 [1024, 2048], P('fsdp')
- grad_key: float32 [1024, 1024], P('fsdp')
- grad_value: float32 [1024, 1024], P('fsdp')
- grad_norm_query: float32 [128], P('fsdp')
- grad_norm_key: float32 [128], P('fsdp')
- grad_output: float32 [2048, 1024], P(None, 'fsdp')
- grad_norm_post: float32 [1024], P('fsdp')
- grad_gate: float32 [1024, 3072], P('fsdp')
- grad_up: float32 [1024, 3072], P('fsdp')
- grad_down: float32 [3072, 1024], P(None, 'fsdp')
Inputs may be any that keep to these rules, and one draw needn't show every extreme that they name: `segments`: ids never fall along a sequence; tokens of one sequence with equal ids belong to one document.
All inputs are finite; a program needn't handle non-finite values.
Results may differ from a plain program's by a relative error of at most 0.025.
Values may be sent and summed in bfloat16 or wider, within the bound.
No kernel may reach another device: no remote copies, remote signals or barrier semaphores. Data moves between devices by JAX's collectives and lax.ppermute only.
A program may use at most 192 MiB of HBM per device.

v0:
```python
import math

import jax
import jax.numpy as jnp
from jax import lax
from jax.sharding import PartitionSpec as P

HEAD = 128
FF = 3072
QBLOCK = 512
Q_WIDTH = 2048
KV_WIDTH = 1024


EPSILON = 1e-06
THETA = 1000000.0
NEGATIVE = -1e30


def normalize(values, gain):
    return values * lax.rsqrt(jnp.mean(values * values, axis=-1, keepdims=True) + EPSILON) * gain


def rotation(positions):
    exponent = jnp.arange(0, HEAD, 2, dtype=jnp.float32) / HEAD
    frequency = jnp.power(jnp.float32(THETA), -exponent)
    angles = positions.astype(jnp.float32)[:, None] * frequency[None, :]
    angles = jnp.concatenate([angles, angles], axis=-1)
    return (jnp.cos(angles)[:, None, :], jnp.sin(angles)[:, None, :])


def rotate(values, cosine, sine):
    half = values.shape[-1] // 2
    turned = jnp.concatenate([-values[..., half:], values[..., :half]], axis=-1)
    return values * cosine + turned * sine


def contract(left, right):
    return lax.dot_general(
        left, right, (((1,), (1,)), ((), ())), preferred_element_type=jnp.float32
    )


def outer_rows(left, right):
    return lax.dot_general(
        left, right, (((0,), (0,)), ((), ())), preferred_element_type=jnp.float32
    )


def gated(gate, up_part):
    return gate * jax.nn.sigmoid(gate) * up_part


def per_device(
    tokens,
    segments,
    norm_input,
    w_query,
    w_key,
    w_value,
    norm_query,
    norm_key,
    w_output,
    norm_post,
    w_gate,
    w_up,
    w_down,
    cotangent,
):
    sequence = tokens[0]
    local_rows = sequence.shape[0]
    length = local_rows * lax.axis_size("seq")
    offset = lax.axis_index("seq") * local_rows
    doc_ids = segments[0]
    scale = 1.0 / math.sqrt(HEAD)
    cosine, sine = rotation(offset + jnp.arange(local_rows, dtype=jnp.int32))
    attn_set = (
        lax.all_gather(norm_input, "fsdp", axis=0, tiled=True),
        lax.all_gather(w_query, "fsdp", axis=0, tiled=True),
        lax.all_gather(w_key, "fsdp", axis=0, tiled=True),
        lax.all_gather(w_value, "fsdp", axis=0, tiled=True),
        lax.all_gather(norm_query, "fsdp", axis=0, tiled=True),
        lax.all_gather(norm_key, "fsdp", axis=0, tiled=True),
        lax.all_gather(w_output, "fsdp", axis=1, tiled=True),
    )
    gain_input, query_weight, key_weight, value_weight, gain_query, gain_key, output_weight = (
        attn_set
    )
    widened = sequence.astype(jnp.float32)
    normed = normalize(widened, gain_input).astype(jnp.bfloat16)
    query_raw = jnp.dot(normed, query_weight, preferred_element_type=jnp.float32)
    key_raw = jnp.dot(normed, key_weight, preferred_element_type=jnp.float32)
    values_low = jnp.dot(normed, value_weight, preferred_element_type=jnp.float32).astype(
        jnp.bfloat16
    )

    def head_path(raw, gain):
        shaped = raw.reshape(local_rows, raw.shape[1] // HEAD, HEAD)
        return rotate(normalize(shaped, gain), cosine, sine)

    query_rot = head_path(query_raw, gain_query).astype(jnp.bfloat16)
    key_rot = head_path(key_raw, gain_key).astype(jnp.bfloat16)
    query_heads, key_heads, value_heads = (
        lax.all_to_all(query_rot, "seq", split_axis=1, concat_axis=0, tiled=True),
        lax.all_to_all(key_rot, "seq", split_axis=1, concat_axis=0, tiled=True),
        lax.all_to_all(
            values_low.reshape(local_rows, -1, HEAD), "seq", split_axis=1, concat_axis=0, tiled=True
        ),
    )
    kv_local = key_heads.shape[1]
    grouped = query_heads.shape[1] // kv_local
    query_grouped = query_heads.reshape(length, kv_local, grouped, HEAD)
    columns = jnp.arange(length, dtype=jnp.int32)
    block_starts = jnp.arange(length // QBLOCK, dtype=jnp.int32) * QBLOCK

    def block_scores(begin):
        rows_query = lax.dynamic_slice_in_dim(query_grouped, begin, QBLOCK, 0)
        rows_ids = lax.dynamic_slice_in_dim(doc_ids, begin, QBLOCK, 0)
        positions = begin + jnp.arange(QBLOCK, dtype=jnp.int32)
        allowed = (positions[:, None] >= columns[None, :]) & (rows_ids[:, None] == doc_ids[None, :])
        raw = (
            jnp.einsum("qhgd,khd->hgqk", rows_query, key_heads, preferred_element_type=jnp.float32)
            * scale
        )
        return (jnp.where(allowed, raw, NEGATIVE), rows_query)

    def forward_block(begin):
        score, rows_query = block_scores(begin)
        highest = jnp.max(score, axis=-1, keepdims=True)
        expo_term = jnp.exp(score - highest)
        denominator = jnp.sum(expo_term, axis=-1, keepdims=True)
        prob_low = (expo_term / denominator).astype(jnp.bfloat16)
        mixed_part = jnp.einsum(
            "hgqk,khd->qhgd", prob_low, value_heads, preferred_element_type=jnp.float32
        )
        return (mixed_part.astype(jnp.bfloat16), highest + jnp.log(denominator))

    mixed_blocks, log_totals = lax.map(forward_block, block_starts)
    mixed_heads = mixed_blocks.reshape(length, kv_local * grouped, HEAD)
    mixed_tokens = lax.all_to_all(
        mixed_heads, "seq", split_axis=0, concat_axis=1, tiled=True
    ).reshape(local_rows, -1)
    hidden = widened + jnp.dot(mixed_tokens, output_weight, preferred_element_type=jnp.float32)
    mlp_set = (
        lax.all_gather(norm_post, "fsdp", axis=0, tiled=True),
        lax.all_gather(w_gate, "fsdp", axis=0, tiled=True),
        lax.all_gather(w_up, "fsdp", axis=0, tiled=True),
        lax.all_gather(w_down, "fsdp", axis=1, tiled=True),
    )
    gain_post, gate_weight, up_weight, down_weight = mlp_set
    normed_post = normalize(hidden, gain_post).astype(jnp.bfloat16)
    gate = jnp.dot(normed_post, gate_weight, preferred_element_type=jnp.float32)
    up_part = jnp.dot(normed_post, up_weight, preferred_element_type=jnp.float32)
    inner = gated(gate, up_part).astype(jnp.bfloat16)
    result = (hidden + jnp.dot(inner, down_weight, preferred_element_type=jnp.float32)).astype(
        jnp.bfloat16
    )
    back_attn = (
        lax.all_gather(norm_input, "fsdp", axis=0, tiled=True),
        lax.all_gather(w_query, "fsdp", axis=0, tiled=True),
        lax.all_gather(w_key, "fsdp", axis=0, tiled=True),
        lax.all_gather(w_value, "fsdp", axis=0, tiled=True),
        lax.all_gather(norm_query, "fsdp", axis=0, tiled=True),
        lax.all_gather(norm_key, "fsdp", axis=0, tiled=True),
        lax.all_gather(w_output, "fsdp", axis=1, tiled=True),
    )
    back_mlp = (
        lax.all_gather(norm_post, "fsdp", axis=0, tiled=True),
        lax.all_gather(w_gate, "fsdp", axis=0, tiled=True),
        lax.all_gather(w_up, "fsdp", axis=0, tiled=True),
        lax.all_gather(w_down, "fsdp", axis=1, tiled=True),
    )
    (
        gain_input_b,
        query_weight_b,
        key_weight_b,
        value_weight_b,
        gain_query_b,
        gain_key_b,
        output_weight_b,
    ) = back_attn
    gain_post_b, gate_weight_b, up_weight_b, down_weight_b = back_mlp
    incoming_low = cotangent[0]
    incoming = incoming_low.astype(jnp.float32)
    inner_grad = contract(incoming_low, down_weight_b)
    unused_out, gate_pull = jax.vjp(gated, gate, up_part)
    gate_grad, up_grad = gate_pull(inner_grad)
    gate_grad = gate_grad.astype(jnp.bfloat16)
    up_grad = up_grad.astype(jnp.bfloat16)
    post_grad = contract(gate_grad, gate_weight_b) + contract(up_grad, up_weight_b)
    unused_post, post_pull = jax.vjp(normalize, hidden, gain_post_b)
    hidden_part, gain_post_grad = post_pull(post_grad)
    hidden_grad = incoming + hidden_part
    left_rows = normed_post
    back_rows = incoming_low
    mlp_share = lax.psum_scatter(
        jnp.concatenate(
            [
                outer_rows(left_rows, gate_grad),
                outer_rows(left_rows, up_grad),
                outer_rows(back_rows, inner),
            ],
            axis=1,
        ).astype(jnp.bfloat16),
        "fsdp",
        scatter_dimension=0,
        tiled=True,
    )
    proj_grad = hidden_grad.astype(jnp.bfloat16)
    mixed_grad = (
        contract(proj_grad, output_weight_b).astype(jnp.bfloat16).reshape(local_rows, -1, HEAD)
    )
    mixed_grad_heads = lax.all_to_all(mixed_grad, "seq", split_axis=1, concat_axis=0, tiled=True)
    mixed_grad_grouped = mixed_grad_heads.reshape(length, kv_local, grouped, HEAD)

    def backward_block(carried, item):
        begin, log_total = item
        score, rows_query = block_scores(begin)
        weights_now = jnp.exp(score - log_total)
        rows_grad = lax.dynamic_slice_in_dim(mixed_grad_grouped, begin, QBLOCK, 0)
        weight_grad = jnp.einsum(
            "qhgd,khd->hgqk", rows_grad, value_heads, preferred_element_type=jnp.float32
        )
        score_grad = (
            weights_now * (weight_grad - jnp.sum(weights_now * weight_grad, axis=-1, keepdims=True))
        ).astype(jnp.bfloat16)
        query_part = (
            jnp.einsum("hgqk,khd->qhgd", score_grad, key_heads, preferred_element_type=jnp.float32)
            * scale
        )
        key_sum = (
            carried[0]
            + jnp.einsum(
                "hgqk,qhgd->khd", score_grad, rows_query, preferred_element_type=jnp.float32
            )
            * scale
        )
        value_sum = carried[1] + jnp.einsum(
            "hgqk,qhgd->khd",
            weights_now.astype(jnp.bfloat16),
            rows_grad,
            preferred_element_type=jnp.float32,
        )
        return ((key_sum, value_sum), query_part)

    zero_heads = jnp.zeros((length, kv_local, HEAD), jnp.float32)
    (key_grad, value_grad), query_blocks = lax.scan(
        backward_block, (zero_heads, zero_heads), (block_starts, log_totals)
    )
    query_back, key_back, value_back = (
        lax.all_to_all(
            query_blocks.reshape(length, -1, HEAD).astype(jnp.bfloat16),
            "seq",
            split_axis=0,
            concat_axis=1,
            tiled=True,
        ),
        lax.all_to_all(
            key_grad.astype(jnp.bfloat16), "seq", split_axis=0, concat_axis=1, tiled=True
        ),
        lax.all_to_all(
            value_grad.astype(jnp.bfloat16), "seq", split_axis=0, concat_axis=1, tiled=True
        ),
    )
    unused_query, query_pull = jax.vjp(head_path, query_raw, gain_query_b)
    query_raw_grad, gain_query_grad = query_pull(query_back.astype(jnp.float32))
    unused_key, key_pull = jax.vjp(head_path, key_raw, gain_key_b)
    key_raw_grad, gain_key_grad = key_pull(key_back.astype(jnp.float32))
    query_raw_low = query_raw_grad.astype(jnp.bfloat16)
    key_raw_low = key_raw_grad.astype(jnp.bfloat16)
    value_flat = value_back.reshape(local_rows, -1)
    normed_grad = (
        contract(query_raw_low, query_weight_b)
        + contract(key_raw_low, key_weight_b)
        + contract(value_flat, value_weight_b)
    )
    unused_normed, input_pull = jax.vjp(normalize, widened, gain_input_b)
    input_part, gain_input_grad = input_pull(normed_grad)
    tokens_grad = (hidden_grad + input_part)[None]
    gain_shares = (
        lax.psum_scatter(
            gain_input_grad.astype(jnp.float32), "fsdp", scatter_dimension=0, tiled=True
        ),
        lax.psum_scatter(
            gain_query_grad.astype(jnp.float32), "fsdp", scatter_dimension=0, tiled=True
        ),
        lax.psum_scatter(
            gain_key_grad.astype(jnp.float32), "fsdp", scatter_dimension=0, tiled=True
        ),
        lax.psum_scatter(
            gain_post_grad.astype(jnp.float32), "fsdp", scatter_dimension=0, tiled=True
        ),
    )
    left_rows = normed
    back_rows = proj_grad
    attn_share = lax.psum_scatter(
        jnp.concatenate(
            [
                outer_rows(left_rows, query_raw_low),
                outer_rows(left_rows, key_raw_low),
                outer_rows(left_rows, value_flat),
                outer_rows(back_rows, mixed_tokens),
            ],
            axis=1,
        ).astype(jnp.bfloat16),
        "fsdp",
        scatter_dimension=0,
        tiled=True,
    )
    summed = (
        lax.psum(attn_share, "seq").astype(jnp.float32),
        lax.psum(mlp_share, "seq").astype(jnp.float32),
        lax.psum(gain_shares[0].astype(jnp.bfloat16), "seq").astype(jnp.float32),
        lax.psum(gain_shares[1].astype(jnp.bfloat16), "seq").astype(jnp.float32),
        lax.psum(gain_shares[2].astype(jnp.bfloat16), "seq").astype(jnp.float32),
        lax.psum(gain_shares[3].astype(jnp.bfloat16), "seq").astype(jnp.float32),
    )
    attn_total, mlp_total, input_gain_total, query_gain_total, key_gain_total, post_gain_total = (
        summed
    )
    query_total = attn_total[:, :Q_WIDTH]
    key_total = attn_total[:, Q_WIDTH : Q_WIDTH + KV_WIDTH]
    value_total = attn_total[:, Q_WIDTH + KV_WIDTH : Q_WIDTH + 2 * KV_WIDTH]
    output_total = attn_total[:, Q_WIDTH + 2 * KV_WIDTH :].T
    gate_total = mlp_total[:, :FF]
    up_total = mlp_total[:, FF : 2 * FF]
    down_total = mlp_total[:, 2 * FF :].T
    return (
        result[None],
        tokens_grad,
        input_gain_total,
        query_total,
        key_total,
        value_total,
        query_gain_total,
        key_gain_total,
        output_total,
        post_gain_total,
        gate_total,
        up_total,
        down_total,
    )


def solution(mesh):
    in_specs = (
        P("fsdp", "seq", None),
        P("fsdp", None),
        P("fsdp"),
        P("fsdp", None),
        P("fsdp", None),
        P("fsdp", None),
        P("fsdp"),
        P("fsdp"),
        P(None, "fsdp"),
        P("fsdp"),
        P("fsdp", None),
        P("fsdp", None),
        P(None, "fsdp"),
        P("fsdp", "seq", None),
    )
    out_specs = (
        P("fsdp", "seq", None),
        P("fsdp", "seq", None),
        P("fsdp"),
        P("fsdp", None),
        P("fsdp", None),
        P("fsdp", None),
        P("fsdp"),
        P("fsdp"),
        P(None, "fsdp"),
        P("fsdp"),
        P("fsdp", None),
        P("fsdp", None),
        P(None, "fsdp"),
    )
    return jax.shard_map(
        per_device, mesh=mesh, in_specs=in_specs, out_specs=out_specs, check_vma=False
    )
```

profile of v0, /device:TPU:0, one launch (start us, length us, event | category | flops | bytes accessed | tf_op | source)
XLA Modules:
  0.0 899.0 jit_solution(9296535210944418807)
XLA Ops:
  17.9 31.2 %all-reduce.13 = (bf16[1024]{0:T(1024)(128)(2,1)S(1)}, bf16[128]{0:T(256)(128)(2,1)S(1)}, bf16[128]{0:T(256)(128)(2,1)S(1)}, bf16[1024]{0:T(1024)(128)(2,1)S(1)}) all-reduce(bf16[1024]{0:T(1024)(128)(2,1)S(1)} %dynamic-update-slice, bf16[128]{0:T(256)(128)(2,1)S(1)} %dynamic-update-slice.1, ...), channel_id=1, replica_groups=mesh['seq'=8,'fsdp'=16] {'fsdp'}, use_global_device_ids=true, to_apply=%add.4 | all-reduce | flops 2304 | bytes 9216
  50.7 2.9 copy.100
  56.1 7.4 all-to-all-start.1
  63.5 24.5 %all-gather.8.cloned.1.call-done = bf16[1024,2048]{1,0:T(8,128)(2,1)} async-done(((bf16[64,2048]{1,0:T(8,128)(2,1)}), bf16[1024,2048]{1,0:T(8,128)(2,1)}) %all-gather.8.cloned.1.call-update) | async-done | bytes 4194320 | tf_op jit(solution)/shard_map/all_gather | solution.py:79
  88.0 6.4 copy.98
  94.4 3.6 multiply_reduce_fusion.2
  100.1 6.5 all-to-all-start
  106.5 18.3 %all-gather.12.cloned.1.call-done = bf16[1024,1024]{1,0:T(8,128)(2,1)} async-done(((bf16[64,1024]{1,0:T(8,128)(2,1)}), bf16[1024,1024]{1,0:T(8,128)(2,1)}) %all-gather.12.cloned.1.call-update) | async-done | bytes 2097168 | tf_op jit(solution)/shard_map/all_gather | solution.py:81
  124.8 2.1 fusion.75
  127.7 6.9 all-to-all-start.2
  136.3 10.2 %all-to-all-done.2 = bf16[128,8,128]{2,0,1:T(8,128)(2,1)} async-done(((bf16[128,8,128]{2,0,1:T(8,128)(2,1)}), bf16[128,8,128]{2,0,1:T(8,128)(2,1)}, u32[]{:S(2)}, u32[]{:S(2)}) %all-to-all-start.2) | async-done | bytes 262176 | tf_op jit(solution)/shard_map/all_to_all | solution.py:106
  146.5 21.9 %while.28 = (s32[]{:T(128)}, bf16[2,512,1,2,128]{4,1,0,3,2:T(8,128)(2,1)S(1)}, f32[2,1,2,512,1]{3,2,4,1,0:T(2,128)}, s32[2]{0:T(128)}, s32[1024]{0:T(1024)S(1)},...) while((s32[]{:T(128)}, ...), condition=%wide.region_6.7_spmd.clone, body=%wide.region_3.6_spmd.clone.sunk | while | flops 551157248 | bytes 15775935 | solution.py:138
  150.9 2.1 fusion.198
  154.2 2.6 fusion.200
  161.9 2.1 fusion.198
  165.2 2.6 fusion.200
  169.8 4.0 all-to-all-start.3
  173.7 14.9 %all-to-all-done.3 = bf16[1024,2,128]{2,1,0:T(2,128)(2,1)S(1)} async-done(((bf16[1024,2,128]{2,1,0:T(2,128)(2,1)}), bf16[1024,2,128]{2,1,0:T(2,128)(2,1)S(1)}, u32[]{:S(2)}, u32[]{:S(2)}) %all-to-all-start.3) | async-done | bytes 524320 | tf_op jit(solution)/shard_map/all_to_all | solution.py:140
  189.0 4.0 multiply_reduce_fusion.7
  193.2 16.5 %all-gather.16.cloned.1.call-done = bf16[1024,3072]{1,0:T(8,128)(2,1)} async-done(((bf16[64,3072]{1,0:T(8,128)(2,1)}), bf16[1024,3072]{1,0:T(8,128)(2,1)}) %all-gather.16.cloned.1.call-update) | async-done | bytes 6291472 | tf_op jit(solution)/shard_map/all_gather | solution.py:146
  209.8 5.0 fusion.135
  214.7 38.9 %all-gather.18.cloned.1.call-done = bf16[1024,3072]{1,0:T(8,128)(2,1)} async-done(((bf16[64,3072]{1,0:T(8,128)(2,1)}), bf16[1024,3072]{1,0:T(8,128)(2,1)}) %all-gather.18.cloned.1.call-update) | async-done | bytes 6291472 | tf_op jit(solution)/shard_map/all_gather | solution.py:147
  253.6 4.9 fusion.136
  258.5 40.0 %all-gather.20.cloned.1.call-done = bf16[3072,1024]{0,1:T(8,128)(2,1)} async-done(((bf16[3072,64]{0,1:T(8,128)(2,1)}), bf16[3072,1024]{0,1:T(8,128)(2,1)}) %all-gather.20.cloned.1.call-update) | async-done | bytes 6291472 | tf_op jit(solution)/shard_map/all_gather | solution.py:148
  298.6 6.4 multiply_convert_fusion
  305.0 5.6 fusion.137
  310.6 2.9 multiply_reduce_fusion.3
  315.5 7.0 all-to-all-start.4
  322.6 11.9 %all-to-all-done.4 = bf16[128,16,128]{2,0,1:T(8,128)(2,1)S(1)} async-done(((bf16[128,16,128]{2,0,1:T(8,128)(2,1)}), bf16[128,16,128]{2,0,1:T(8,128)(2,1)S(1)}, u32[]{:S(2)}, u32[]{:S(2)}) %all-to-all-start.4) | async-done | bytes 524320 | tf_op jit(solution)/shard_map/all_to_all | solution.py:213
  335.3 39.0 %while.29 = (s32[]{:T(128)}, f32[1024,1,128]{0,2,1:T(8,128)}, f32[1024,1,128]{0,2,1:T(8,128)}, bf16[2,512,1,2,128]{4,1,0,3,2:T(8,128)(2,1)}, s32[2]{0:T(128)}, /...) while((s32[]{:T(128)}, f32[1024,1,128]{0,2,1:T(8,128)}, ...), condition=%wide.region_11.12_spmd.clone, body=%wide.region_9.11_spmd.clone.sunk | while | flops 1360264704 | bytes 59025728 | solution.py:247
  338.5 1.7 fusion.209
  342.2 2.7 fusion.211
  346.3 2.3 fusion.213
  348.5 4.5 fusion.214
  357.9 1.7 fusion.209
  361.6 2.7 fusion.211
  365.6 2.4 fusion.213
  368.1 4.6 fusion.214
  377.7 3.4 all-to-all-start.7
  384.0 5.8 all-to-all-done.7
  389.9 3.4 all-to-all-start.6
  393.3 3.3 convolution_convert_fusion.2
  398.5 3.6 all-to-all-done.6
  402.0 3.6 all-to-all-start.5
  407.8 2.2 convolution_convert_fusion.5
  410.8 2.2 convolution_convert_fusion.6
  413.0 2.8 all-to-all-done.5
  417.0 1.6 copy.112
  419.6 1.4 convolution_convert_fusion.3
  422.8 11.6 %pad_maximum_fusion.1 = bf16[1024,6144]{1,0:T(8,128)(2,1)} fusion(bf16[1024,2048]{1,0:T(8,128)(2,1)S(1)} %copy-done.7, bf16[1024,1024]{1,0:T(8,128)(2,1)S(1)} %copy-done.14, bf16[1024,1024]{1,0:T(8,128)(2,1)S(1)} %copy-done.15, bf16[1024,2048]{1,0:T(8,128)(2,1)S(1)} %convolution_convert_fusion.3), kind=kLoop, calls=%fused_computation.70 | loop fusion | flops 50331648 | bytes 25165824 | tf_op jit(solution)/shard_map/concatenate | solution.py:297
  435.6 1.8 convolution_convert_fusion
  437.5 1.8 convolution_convert_fusion.1
  439.3 1.8 convert_bitcast_fusion
  441.1 16.6 %pad_maximum_fusion = bf16[1024,9216]{1,0:T(8,128)(2,1)} fusion(bf16[1024,3072]{1,0:T(8,128)(2,1)S(1)} %convert_bitcast_fusion, bf16[1024,3072]{1,0:T(8,128)(2,1)S(1)} %convolution_convert_fusion, bf16[1024,3072]{1,0:T(8,128)(2,1)S(1)} %convolution_convert_fusion.1), kind=kLoop, calls=%fused_computation.69 | loop fusion | flops 56623104 | bytes 37748736 | tf_op jit(solution)/shard_map/concatenate | solution.py:197
  459.2 114.0 %reduce-scatter.3.cloned.1.call-done = bf16[64,6144]{1,0:T(8,128)(2,1)} async-done(((bf16[1024,6144]{1,0:T(8,128)(2,1)}), bf16[64,6144]{1,0:T(8,128)(2,1)}) %reduce-scatter.3.cloned.1.call-update) | async-done | bytes 786448 | tf_op jit(solution)/shard_map/reduce_scatter | solution.py:296
  573.2 204.7 %reduce-scatter.5.cloned.1.call-done = bf16[64,9216]{1,0:T(8,128)(2,1)} async-done(((bf16[1024,9216]{1,0:T(8,128)(2,1)}), bf16[64,9216]{1,0:T(8,128)(2,1)}) %reduce-scatter.5.cloned.1.call-update) | async-done | bytes 1179664 | tf_op jit(solution)/shard_map/reduce_scatter | solution.py:196
  778.0 5.8 fusion.76
  786.0 1.7 fusion.89
  787.7 55.2 %all-reduce.12 = (bf16[1024]{0:T(1024)(128)(2,1)S(1)}, bf16[128]{0:T(256)(128)(2,1)S(1)}, bf16[128]{0:T(256)(128)(2,1)S(1)}, bf16[1024]{0:T(1024)(128)(2,1)S(1)}) all-reduce(bf16[1024]{0:T(1024)(128)(2,1)S(1)} %get-tuple-element.207, bf16[128]{0:T(256)(128)(2,1)S(1)} %get-tuple-element.201, ...), channel_id=2, replica_groups=mesh['seq'=8,'fsdp'=16] {'fsdp'}, use_global_device_ids=true, to_apply=%region_16.17.clone | all-reduce | flops 2304 | bytes 9216
  843.2 26.5 %all-reduce.14 = (bf16[64]{0:T(256)(128)(2,1)S(1)}, bf16[8]{0:T(256)(128)(2,1)S(1)}, bf16[8]{0:T(256)(128)(2,1)S(1)}, bf16[64]{0:T(256)(128)(2,1)S(1)}) all-reduce(bf16[64]{0:T(256)(128)(2,1)S(1)} %dynamic-slice.19, bf16[8]{0:T(256)(128)(2,1)S(1)} %dynamic-slice.18, ...), channel_id=1, replica_groups=mesh['seq'=8,'fsdp'=16] {'seq'}, use_global_device_ids=true, to_apply=%region_17.18 | all-reduce | flops 144 | bytes 576 | tf_op jit(solution)/shard_map/psum | solution.py:313
  872.7 11.7 %all-reduce.18.cloned.1.call-done = (bf16[64,6144]{1,0:T(8,128)(2,1)}, bf16[64,9216]{1,0:T(8,128)(2,1)}) async-done(((bf16[64,6144]{1,0:T(8,128)(2,1)}, bf16[64,9216]{1,0:T(8,128)(2,1)}), (bf16[64,6144]{1,0:T(8,128)(2,1)}, bf16[64,9216]{1,0:T(8,128)(2,1)})) %all-reduce.18.cloned.1.call-update) | async-done | bytes 1966096 | tf_op jit(solution)/shard_map/psum | solution.py:311
  884.4 1.9 slice.48
  886.2 1.8 fusion.132
  890.3 1.5 fusion.130
  (254 shorter events, 67.1 us)
Async XLA Ops:
  7.2 46.4 %copy-start.2 = (bf16[1,128,1024]{2,1,0:T(8,128)(2,1)S(1)}, bf16[1,128,1024]{2,1,0:T(8,128)(2,1)}, u32[]{:S(2)}) copy-start(bf16[1,128,1024]{2,1,0:T(8,128)(2,1)} %param.18) | copy-start | bytes 786436
  7.2 43.5 %all-gather.10.cloned.1.call-start = ((), (), s32[]{:S(2)}) async-start(), calls=%async_computation.11 | async-start | bytes 2228224 | tf_op jit(solution)/shard_map/all_gather | solution.py:80
  7.9 80.1 %all-gather.8.cloned.1.call-start = ((), (), s32[]{:S(2)}) async-start(), calls=%async_computation.10 | async-start | bytes 4456448 | tf_op jit(solution)/shard_map/all_gather | solution.py:79
  8.7 116.1 %all-gather.12.cloned.1.call-start = ((), (), s32[]{:S(2)}) async-start(), calls=%async_computation.12 | async-start | bytes 2228224 | tf_op jit(solution)/shard_map/all_gather | solution.py:81
  9.4 179.6 %all-gather.14.cloned.1.call-start = ((), (), s32[]{:S(2)}) async-start(), calls=%async_computation.13 | async-start | bytes 4456448 | tf_op jit(solution)/shard_map/all_gather | solution.py:84
  10.0 199.8 %all-gather.16.cloned.1.call-start = ((), (), s32[]{:S(2)}) async-start(), calls=%async_computation.14 | async-start | bytes 6684672 | tf_op jit(solution)/shard_map/all_gather | solution.py:146
  10.6 243.0 %all-gather.18.cloned.1.call-start = ((), (), s32[]{:S(2)}) async-start(), calls=%async_computation.15 | async-start | bytes 6684672 | tf_op jit(solution)/shard_map/all_gather | solution.py:147
  11.1 287.4 %all-gather.20.cloned.1.call-start = ((), (), s32[]{:S(2)}) async-start(), calls=%async_computation.16 | async-start | bytes 6684672 | tf_op jit(solution)/shard_map/all_gather | solution.py:148
  49.2 49.4 %copy-start.44 = (f32[128]{0:T(128)}, f32[128]{0:T(128)S(1)}, u32[]{:S(2)}) copy-start(f32[128]{0:T(128)S(1)} %convert_element_type.214) | copy-start | bytes 1540
  49.2 5.4 copy-start.46
  50.7 2.9 copy-start.50
  50.7 74.1 %copy-start.38 = (f32[128]{0:T(128)}, f32[128]{0:T(128)S(1)}, u32[]{:S(2)}) copy-start(f32[128]{0:T(128)S(1)} %fusion.121) | copy-start | bytes 1540
  54.4 40.0 %copy-start.41 = (f32[128,8]{0,1:T(8,128)}, f32[128,8]{0,1:T(8,128)S(1)}, u32[]{:S(2)}) copy-start(f32[128,8]{0,1:T(8,128)S(1)} %get-tuple-element.292) | copy-start | bytes 12292
  56.1 44.0 %all-to-all-start.1 = ((bf16[128,8,128]{0,2,1:T(8,128)(2,1)}), bf16[128,8,128]{0,2,1:T(8,128)(2,1)S(1)}, u32[]{:S(2)}, u32[]{:S(2)}) async-start(bf16[128,8,128]{0,2,1:T(8,128)(2,1)} %fusion.99), calls=%async_computation.1 | async-start | bytes 524288 | tf_op jit(solution)/shard_map/all_to_all | solution.py:105
  99.0 47.5 %copy-start.30 = (s32[1,1024]{1,0:T(1,128)S(1)}, s32[1,1024]{1,0:T(1,128)}, u32[]{:S(2)}) copy-start(s32[1,1024]{1,0:T(1,128)} %param.19) | copy-start | bytes 12292
  100.1 27.6 %all-to-all-start = ((bf16[128,16,128]{0,2,1:T(8,128)(2,1)}), bf16[128,16,128]{0,2,1:T(8,128)(2,1)S(1)}, u32[]{:S(2)}, u32[]{:S(2)}) async-start(bf16[128,16,128]{0,2,1:T(8,128)(2,1)} %fusion.79), calls=%async_computation | async-start | bytes 1048576 | tf_op jit(solution)/shard_map/all_to_all | solution.py:104
  127.7 18.8 %all-to-all-start.2 = ((bf16[128,8,128]{2,0,1:T(8,128)(2,1)}), bf16[128,8,128]{2,0,1:T(8,128)(2,1)}, u32[]{:S(2)}, u32[]{:S(2)}) async-start(bf16[128,8,128]{2,0,1:T(8,128)(2,1)} %bitcast.340), calls=%async_computation.2 | async-start | bytes 524288 | tf_op jit(solution)/shard_map/all_to_all | solution.py:106
  169.8 18.9 %all-to-all-start.3 = ((bf16[1024,2,128]{2,1,0:T(2,128)(2,1)}), bf16[1024,2,128]{2,1,0:T(2,128)(2,1)S(1)}, u32[]{:S(2)}, u32[]{:S(2)}) async-start(bf16[1024,2,128]{2,1,0:T(2,128)(2,1)} %copy.104), calls=%async_computation.3 | async-start | bytes 1048576 | tf_op jit(solution)/shard_map/all_to_all | solution.py:140
  189.0 25.7 %copy-start.20 = (bf16[128,8,2,128]{0,3,2,1:T(8,128)(2,1)}, bf16[128,8,2,128]{0,3,2,1:T(8,128)(2,1)S(1)}, u32[]{:S(2)}) copy-start(bf16[128,8,2,128]{0,3,2,1:T(8,128)(2,1)S(1)} %copy.106) | copy-start | bytes 1572868
  193.1 21.6 %copy-start.52 = (f32[128]{0:T(128)}, f32[128]{0:T(128)S(1)}, u32[]{:S(2)}) copy-start(f32[128]{0:T(128)S(1)} %get-tuple-element.294) | copy-start | bytes 1540
  193.1 120.5 %copy-start.10 = (f32[128,1024]{1,0:T(8,128)}, f32[128,1024]{1,0:T(8,128)S(1)}, u32[]{:S(2)}) copy-start(f32[128,1024]{1,0:T(8,128)S(1)} %get-tuple-element.295) | copy-start | bytes 1572868
  193.1 21.6 %copy-start.47 = (f32[128]{0:T(128)}, f32[128]{0:T(128)S(1)}, u32[]{:S(2)}) copy-start(f32[128]{0:T(128)S(1)} %fusion.122) | copy-start | bytes 1540
  214.7 83.8 %copy-start.28 = (bf16[1,128,1024]{2,1,0:T(8,128)(2,1)S(1)}, bf16[1,128,1024]{2,1,0:T(8,128)(2,1)}, u32[]{:S(2)}) copy-start(bf16[1,128,1024]{2,1,0:T(8,128)(2,1)} %param.31) | copy-start | bytes 786436
  305.0 5.6 copy-start.22
  305.0 8.6 copy-start.24
  305.0 5.6 copy-start.1
  305.0 5.6 copy-start.48
  310.6 3.0 copy-start.53
  310.6 3.1 copy-start.5
  313.8 21.6 %copy-start.12 = (f32[128,1024]{1,0:T(8,128)}, f32[128,1024]{1,0:T(8,128)S(1)}, u32[]{:S(2)}) copy-start(f32[128,1024]{1,0:T(8,128)S(1)} %fusion.94) | copy-start | bytes 1572868
  315.5 19.0 %all-to-all-start.4 = ((bf16[128,16,128]{2,0,1:T(8,128)(2,1)}), bf16[128,16,128]{2,0,1:T(8,128)(2,1)S(1)}, u32[]{:S(2)}, u32[]{:S(2)}) async-start(bf16[128,16,128]{2,0,1:T(8,128)(2,1)} %bitcast.339), calls=%async_computation.4 | async-start | bytes 1048576 | tf_op jit(solution)/shard_map/all_to_all | solution.py:213
  340.2 4.7 copy-start
  348.5 4.5 copy-start.31
  359.5 4.7 copy-start
  368.1 4.6 copy-start.31
  374.3 19.0 %copy-start.13 = (f32[128,1024]{1,0:T(8,128)S(1)}, f32[128,1024]{1,0:T(8,128)}, u32[]{:S(2)}) copy-start(f32[128,1024]{1,0:T(8,128)} %copy-done.12) | copy-start | bytes 1572868
  374.3 19.0 %copy-start.21 = (bf16[128,8,2,128]{0,3,2,1:T(8,128)(2,1)S(1)}, bf16[128,8,2,128]{0,3,2,1:T(8,128)(2,1)}, u32[]{:S(2)}) copy-start(bf16[128,8,2,128]{0,3,2,1:T(8,128)(2,1)} %copy-done.20) | copy-start | bytes 1572868
  377.7 12.1 %all-to-all-start.7 = ((bf16[8,2,8192]{2,1,0:T(2,128)(2,1)}), bf16[8,2,8192]{2,1,0:T(2,128)(2,1)S(1)}, u32[]{:S(2)}, u32[]{:S(2)}) async-start(bf16[8,2,8192]{2,1,0:T(2,128)(2,1)} %reshape.439), calls=%async_computation.7 | async-start | bytes 524288 | tf_op jit(solution)/shard_map/all_to_all | solution.py:261
  381.2 15.4 %copy-start.33 = (bf16[2,512,1,2,128]{4,1,0,3,2:T(8,128)(2,1)S(1)}, bf16[2,512,1,2,128]{4,1,0,3,2:T(8,128)(2,1)}, u32[]{:S(2)}) copy-start(bf16[2,512,1,2,128]{4,1,0,3,2:T(8,128)(2,1)} %get-tuple-element.137) | copy-start | bytes 1572868
  389.9 12.1 %all-to-all-start.6 = ((bf16[8,2,8192]{2,1,0:T(2,128)(2,1)}), bf16[8,2,8192]{2,1,0:T(2,128)(2,1)S(1)}, u32[]{:S(2)}, u32[]{:S(2)}) async-start(bf16[8,2,8192]{2,1,0:T(2,128)(2,1)} %reshape.441), calls=%async_computation.6 | async-start | bytes 524288 | tf_op jit(solution)/shard_map/all_to_all | solution.py:258
  396.6 9.8 %copy-start.9 = (f32[128,8,128]{0,2,1:T(8,128)S(1)}, f32[128,8,128]{0,2,1:T(8,128)}, u32[]{:S(2)}) copy-start(f32[128,8,128]{0,2,1:T(8,128)} %copy-done.8) | copy-start | bytes 1572868
  398.2 9.5 %copy-start.42 = (f32[128,8]{0,1:T(8,128)S(1)}, f32[128,8]{0,1:T(8,128)}, u32[]{:S(2)}) copy-start(f32[128,8]{0,1:T(8,128)} %copy-done.41) | copy-start | bytes 12292
  398.3 9.6 %copy-start.39 = (f32[128]{0:T(128)S(1)}, f32[128]{0:T(128)}, u32[]{:S(2)}) copy-start(f32[128]{0:T(128)} %copy-done.38) | copy-start | bytes 1540
  398.4 11.5 %copy-start.26 = (bf16[128,8,1,128]{0,3,1,2:T(8,128)(2,1)}, bf16[128,8,1,128]{0,3,1,2:T(8,128)(2,1)S(1)}, u32[]{:S(2)}) copy-start(bf16[128,8,1,128]{0,3,1,2:T(8,128)(2,1)S(1)} %copy.117) | copy-start | bytes 786436
  402.0 13.8 %all-to-all-start.5 = ((bf16[1024,2,128]{2,1,0:T(2,128)(2,1)}), bf16[1024,2,128]{2,1,0:T(2,128)(2,1)S(1)}, u32[]{:S(2)}, u32[]{:S(2)}) async-start(bf16[1024,2,128]{2,1,0:T(2,128)(2,1)} %copy.110), calls=%async_computation.5 | async-start | bytes 1048576 | tf_op jit(solution)/shard_map/all_to_all | solution.py:251
  405.6 167.6 %reduce-scatter.3.cloned.1.call-start = ((), (), s32[]{:S(2)}) async-start(), calls=%async_computation.17 | async-start | bytes 13369344 | tf_op jit(solution)/shard_map/reduce_scatter | solution.py:296
  415.9 2.9 copy-start.4
  415.9 2.9 copy-start.35
  415.9 2.9 copy-start.45
  419.6 2.6 copy-start.7
  419.6 3.2 copy-start.14
  434.5 343.4 %reduce-scatter.5.cloned.1.call-start = ((), (), s32[]{:S(2)}) async-start(), calls=%async_computation.18 | async-start | bytes 20054016 | tf_op jit(solution)/shard_map/reduce_scatter | solution.py:196
  437.4 1.9 copy-start.19
  437.4 1.9 copy-start.29
  457.8 320.1 %copy-start.11 = (f32[128,1024]{1,0:T(8,128)S(1)}, f32[128,1024]{1,0:T(8,128)}, u32[]{:S(2)}) copy-start(f32[128,1024]{1,0:T(8,128)} %copy-done.10) | copy-start | bytes 1572868
  457.8 426.5 %all-reduce.18.cloned.1.call-start = ((), (), s32[]{:S(2)}) async-start(), calls=%async_computation.19 | async-start | bytes 3932160 | tf_op jit(solution)/shard_map/psum | solution.py:311
  777.9 5.9 copy-start.17
  777.9 5.9 copy-start.27
  777.9 6.7 copy-start.16
  783.8 2.2 copy-start.6
  784.7 3.0 copy-start.43
  784.7 3.0 copy-start.49
  784.7 87.0 %copy-start.51 = (f32[128]{0:T(128)S(1)}, f32[128]{0:T(128)}, u32[]{:S(2)}) copy-start(f32[128]{0:T(128)} %copy-done.50) | copy-start | bytes 1540
  884.4 5.8 copy-start.18
  (11 other events, 11.3 us)
Sparse Core Ops, SparseCore 0:
  9.7 36.5 all-gather.9
  48.0 39.9 all-gather.7
  89.7 35.0 all-gather.11
  126.4 38.2 all-gather.13
  166.3 43.4 all-gather.15
  211.3 42.2 all-gather.17
  255.3 43.1 all-gather.19
  434.6 138.5 reduce-scatter.2
  575.6 202.2 reduce-scatter.4
  780.3 103.9 all-reduce.17
where the time goes:
time: 910 us; the launch traced here: 899 us
  waiting for transfers between devices  522 us (57%)
  blocking collectives  113 us (12%)
  matrix products  93.4 us (10%)
  other arithmetic  56.5 us (6%)
  local copies, waits for them, and re-layouts  44.8 us (5%)
  starting transfers between devices  43 us (5%)
  between operations  18.2 us (2%)
    reduce_scatter x1, waiting for transfers between devices, per_device(): lax.psum_scatter(jnp.concatenate([outer_rows(left_rows, gate_grad), outer...  205 us
    reduce_scatter x1, waiting for transfers between devices, per_device(): lax.psum_scatter(jnp.concatenate([outer_rows(left_rows, query_raw_low), o...  114 us
    unnamed x2, blocking collectives  86.4 us
    all_gather x1, waiting for transfers between devices, per_device(): lax.all_gather(w_down, 'fsdp', axis=1, tiled=True)  40 us
    all_gather x1, waiting for transfers between devices, per_device(): lax.all_gather(w_up, 'fsdp', axis=0, tiled=True)  38.9 us
    psum x1, blocking collectives, per_device(): lax.psum(gain_shares[0].astype(jnp.bfloat16), 'seq').astype(jnp.float32)  26.5 us
    all_gather x1, waiting for transfers between devices, per_device(): lax.all_gather(w_query, 'fsdp', axis=0, tiled=True)  24.5 us
    dot_general x7, matrix products, contract(): lax.dot_general(left, right, (((1,), (1,)), ((), ())), preferred_element_...  19.1 us
  transfers between devices with their start and end apart: 18, of which 14 were waited for; matrix products, arithmetic and copies ran while one was open for 12% of the time, Pallas kernels for 0%

commit v1 on v0

v1 whole, which is shorter than its diff:
```python
import functools
import math

import jax
import jax.numpy as jnp
import numpy as np
from jax import lax
from jax.experimental import pallas as pl
from jax.experimental.pallas import tpu as pltpu
from jax.sharding import PartitionSpec as P

HEAD = 128
D = 1024
FF = 3072
LENGTH = 1024
ROWS = 128
N_SEQ = 8
N_FSDP = 16
Z = 4
OWN = D // N_FSDP
FF_Z = FF // Z
UNIT = 512
BLOCK = 256
EXTRA = 16
SHARE = 2 * UNIT + HEAD
MEGA = 1 << 20
GRANT = 60

EPSILON = 1e-06
THETA = 1000000.0
NEGATIVE = -1e30
SCALE = 1.0 / math.sqrt(HEAD)

PIECES = (
    (0, 0, 0, 0),
    (1, 0, 1, 0),
    (2, 0, 3, 0),
    (2, 1, 2, 0),
    (3, 0, 0, 1),
    (4, 0, 3, 1),
    (5, 0, 1, 1),
    (5, 1, 2, 1),
)
KEPT = ((0, 0), (1, 0), (0, 1), (3, 1))


def exchange(values, axis, bits):
    size = N_SEQ if axis == "seq" else N_FSDP
    return lax.ppermute(values, axis, [(i, i ^ bits) for i in range(size)])


swap_x_hi = functools.partial(exchange, axis="seq", bits=1)
swap_z_a = functools.partial(exchange, axis="seq", bits=2)
swap_z_b = functools.partial(exchange, axis="seq", bits=6)
swap_core = functools.partial(exchange, axis="fsdp", bits=1)
swap_x_lo = functools.partial(exchange, axis="fsdp", bits=2)
swap_chip = functools.partial(exchange, axis="fsdp", bits=3)
swap_y_a = functools.partial(exchange, axis="fsdp", bits=4)
swap_y_b = functools.partial(exchange, axis="fsdp", bits=12)


def after(values, *others):
    return lax.optimization_barrier((values, *others))[0]


def gather4(zero, one, swap_a, swap_b):
    zero_1 = swap_a(zero)
    one_1 = swap_b(one)
    zero_2 = swap_b(jnp.concatenate([zero, zero_1], axis=0))
    one_2 = swap_a(jnp.concatenate([one, one_1], axis=0))
    return zero, zero_1, zero_2, one, one_1, one_2


def halves(rows):
    middle = rows.shape[0] // 2
    return rows[:middle], rows[middle:]


def scatter4(first_0, first_1, block, swap_a, swap_b, between=None):
    got_0, got_1 = swap_b(first_0), swap_a(first_1)
    if between is not None:
        got_0, got_1 = after((got_0, got_1), between)
    n = got_0.shape[0] // 2
    last_0 = swap_a((block(1, 0) + got_0[n:].astype(jnp.float32)).astype(jnp.bfloat16))
    last_1 = swap_b((block(3, 1) + got_1[n:].astype(jnp.float32)).astype(jnp.bfloat16))
    return got_0, got_1, last_0, last_1


def total4(block, got_0, got_1, last_0, last_1):
    n = got_0.shape[0] // 2
    mine_0 = block(0, 0) + got_0[:n].astype(jnp.float32) + last_0.astype(jnp.float32)
    mine_1 = block(0, 1) + got_1[:n].astype(jnp.float32) + last_1.astype(jnp.float32)
    return mine_0, mine_1


def rotation():
    frequency = THETA ** -(np.arange(0, HEAD, 2, dtype=np.float64) / HEAD)
    angles = np.arange(LENGTH, dtype=np.float64)[:, None] * frequency[None, :]
    return jnp.asarray(np.concatenate([np.cos(angles), np.sin(angles)], axis=1).astype(np.float32))


def turns(table):
    turned = pltpu.roll(table, HEAD // 2, 1)
    low = lax.broadcasted_iota(jnp.int32, table.shape, 1) < HEAD // 2
    return jnp.where(low, table, turned), jnp.where(low, -turned, table)


def contract(left, right):
    return lax.dot_general(
        left, right, (((1,), (1,)), ((), ())), preferred_element_type=jnp.float32
    )


def outer_rows(left, right):
    return lax.dot_general(
        left, right, (((0,), (0,)), ((), ())), preferred_element_type=jnp.float32
    )


def product(left, right):
    return jnp.dot(left, right, preferred_element_type=jnp.float32)


def inverse_norm(values):
    return lax.rsqrt(jnp.mean(values * values, axis=-1, keepdims=True) + EPSILON)


def allowed_scores(scores, first_key, begin):
    first = first_key[:, begin : begin + BLOCK]
    place = (BLOCK, BLOCK)
    key, query = lax.broadcasted_iota(jnp.int32, place, 0), lax.broadcasted_iota(jnp.int32, place, 1)
    diagonal = jnp.where((key <= query) & (key + begin >= first), scores[begin:], NEGATIVE)
    if begin == 0:
        return [(0, diagonal)]
    key = lax.broadcasted_iota(jnp.int32, (begin, BLOCK), 0)
    return [(0, jnp.where(key >= first, scores[:begin], NEGATIVE)), (begin, diagonal)]


def front_kernel(
    at, x0, x1, x2, x3, x4, x5, w0, w1, w2, w3, w4, w5, first_key, table,
    normed, raw, heads, mixed, turned, log_total, gains, weight, value_t,
):
    z, x_hi, y, x_lo, core = at[0], at[1], at[2], at[3], at[4]
    weights, tokens = (w0, w1, w2, w3, w4, w5), (x0, x1, x2, x3, x4, x5)
    extra = jnp.zeros((EXTRA, UNIT), jnp.float32)
    for array, step, relative, color in PIECES:
        for other in range(2):
            first = (2 * step + other) * (OWN + EXTRA)
            owner = 4 * (y ^ relative) + 2 * (x_lo ^ color) + (core ^ other)
            weight[pl.ds(pl.multiple_of(owner * OWN, OWN), OWN), :] = weights[array][
                first : first + OWN, :
            ]
            extra += weights[array][first + OWN : first + OWN + EXTRA, :].astype(jnp.float32)
    gain = jnp.concatenate([extra[0:1], extra[1:2]], axis=1)
    gains[...] = jnp.zeros(gains.shape, jnp.float32)
    gains[0:1, :] = gain
    gains[1:2, :] = jnp.concatenate([extra[2:3], extra[3:4]], axis=1)
    gains[2:3, 0:UNIT] = extra[4:5]
    for array, step, relative, color in PIECES:
        values = tokens[array][step * ROWS : (step + 1) * ROWS, :].astype(jnp.float32)
        place = (2 * (z ^ relative) + (x_hi ^ color)) * ROWS
        normed[pl.ds(pl.multiple_of(place, ROWS), ROWS), :] = (
            values * inverse_norm(values) * gain
        ).astype(jnp.bfloat16)
    normed.send()
    weight.send()
    gain_query, gain_key = extra[4:5, :HEAD], extra[4:5, HEAD : 2 * HEAD]
    for begin in range(0, LENGTH, BLOCK):
        rows = slice(begin, begin + BLOCK)
        projected = product(normed[rows, :], weight[...])
        cosine, sine = turns(table[rows, :])
        raw[rows, :] = projected[:, : 3 * HEAD]
        for head, head_gain in enumerate((gain_query, gain_query, gain_key)):
            part = projected[:, head * HEAD : (head + 1) * HEAD]
            part = part * inverse_norm(part) * head_gain
            part = part * cosine + pltpu.roll(part, HEAD // 2, 1) * sine
            heads[rows, head * HEAD : (head + 1) * HEAD] = part.astype(jnp.bfloat16)
        value = projected[:, 3 * HEAD :]
        heads[rows, 3 * HEAD :] = value.astype(jnp.bfloat16)
        value_t[:, rows] = value.T.astype(jnp.bfloat16)
    raw.send()
    heads.send()
    key = slice(2 * HEAD, 3 * HEAD)
    for begin in range(0, LENGTH, BLOCK):
        rows, end = slice(begin, begin + BLOCK), begin + BLOCK
        for head in range(2):
            columns = slice(head * HEAD, (head + 1) * HEAD)
            scores = contract(heads[:end, key], heads[rows, columns]) * SCALE
            parts = allowed_scores(scores, first_key, begin)
            highest = functools.reduce(
                jnp.maximum, [jnp.max(s, axis=0, keepdims=True) for _, s in parts]
            )
            total, result = 0.0, 0.0
            for first, s in parts:
                weights_now = jnp.exp(s - highest)
                total += jnp.sum(weights_now, axis=0, keepdims=True)
                result += product(
                    value_t[:, first : first + s.shape[0]], weights_now.astype(jnp.bfloat16)
                )
            log_total[head : head + 1, rows] = highest + jnp.log(total)
            result = (result / total).T.astype(jnp.bfloat16)
            mixed[rows, columns] = result
            for part in range(2):
                turned[part ^ x_hi, (begin // BLOCK) ^ z, :, columns] = result[
                    part * ROWS : (part + 1) * ROWS
                ]


def back_kernel(
    at, raw, heads, log_total, grad, first_key, table, gains, weight,
    back, gain_grads, first_0, first_1, keep, key_t, key_sum, value_sum, query_sum, turned,
):
    key, value = slice(2 * HEAD, 3 * HEAD), slice(3 * HEAD, 4 * HEAD)
    key_t[...] = heads[:, key].astype(jnp.float32).T.astype(jnp.bfloat16)
    key_sum[...] = jnp.zeros_like(key_sum)
    value_sum[...] = jnp.zeros_like(value_sum)
    for begin in range(0, LENGTH, BLOCK):
        rows, end = slice(begin, begin + BLOCK), begin + BLOCK
        for head in range(2):
            columns = slice(head * HEAD, (head + 1) * HEAD)
            query, rows_grad = heads[rows, columns], grad[rows, columns]
            scores = contract(heads[:end, key], query) * SCALE
            prob_grad = contract(heads[:end, value], rows_grad)
            log_now = log_total[head : head + 1, rows]
            parts, mean = [], 0.0
            for first, s in allowed_scores(scores, first_key, begin):
                prob = jnp.exp(s - log_now)
                pulled = prob_grad[first : first + s.shape[0]]
                mean += jnp.sum(prob * pulled, axis=0, keepdims=True)
                parts.append((first, prob, pulled))
            query_part = 0.0
            for first, prob, pulled in parts:
                keys = slice(first, first + prob.shape[0])
                score_grad = (prob * (pulled - mean)).astype(jnp.bfloat16)
                value_sum[keys, :] += product(prob.astype(jnp.bfloat16), rows_grad)
                key_sum[keys, :] += product(score_grad, query)
                query_part += product(key_t[:, keys], score_grad)
            query_sum[rows, columns] = query_part.T
    back[:, value] = value_sum[...].astype(jnp.bfloat16)
    gain_grads[...] = jnp.zeros(gain_grads.shape, jnp.float32)
    for head in range(3):
        columns = slice(head * HEAD, (head + 1) * HEAD)
        which = 0 if head < 2 else 1
        gain = gains[2:3, which * HEAD : (which + 1) * HEAD]
        for begin in range(0, LENGTH, BLOCK):
            rows = slice(begin, begin + BLOCK)
            cosine, sine = turns(table[rows, :])
            pulled = (query_sum[rows, columns] if head < 2 else key_sum[rows, :]) * SCALE
            pulled = pulled.astype(jnp.bfloat16).astype(jnp.float32)
            pulled = pulled * cosine - pltpu.roll(pulled, HEAD // 2, 1) * sine
            part = raw[rows, columns]
            inverse = inverse_norm(part)
            unit = part * inverse
            gain_grads[which : which + 1, :] += jnp.sum(pulled * unit, axis=0, keepdims=True)
            pulled = pulled * gain
            mean = jnp.mean(unit * pulled, axis=-1, keepdims=True)
            back[rows, columns] = (inverse * (pulled - unit * mean)).astype(jnp.bfloat16)

    back.send()
    z, x_hi = at[0], at[1]
    for relative in range(Z):
        for color in range(2):
            place = (2 * (z ^ relative) + (x_hi ^ color)) * ROWS
            begin = (2 * relative + color) * ROWS
            turned[begin : begin + ROWS, :] = back[pl.ds(pl.multiple_of(place, ROWS), ROWS), :]
    send_order(contract(turned[...], weight[...]), first_0, first_1, keep)


def grad_kernel(
    at, normed, back, gain_grads, p0, p1, p2, p3, p4, p5, mixed_mine, mixed_other,
    mine, theirs, share, proj, mixed, done,
):
    y, x_lo, core = at[2], at[3], at[4]
    ordered((p0, p1, p2, p3, p4, p5), proj)
    mixed[:, : 2 * HEAD] = mixed_mine[...]
    mixed[:, 2 * HEAD :] = mixed_other[...]
    lane = lax.broadcasted_iota(jnp.int32, (OWN, HEAD), 1)
    line = lax.broadcasted_iota(jnp.int32, (OWN, HEAD), 0)
    each = HEAD // N_FSDP
    for begin in range(0, D, BLOCK):
        goal = slice(begin, begin + BLOCK)
        attn = outer_rows(normed[:, goal], back[...]).astype(jnp.bfloat16)
        output = outer_rows(proj[:, goal], mixed[...]).astype(jnp.bfloat16)
        for part in range(BLOCK // OWN):
            owner = begin // OWN + part
            query_gain = pltpu.roll(gain_grads[0:1, :], (HEAD - each * owner) % HEAD, 1)
            key_gain = pltpu.roll(gain_grads[1:2, :], (HEAD + each - each * owner) % HEAD, 1)
            head_gains = jnp.where(lane < each, query_gain, key_gain)
            head_gains = jnp.where((line == 0) & (lane < 2 * each), head_gains, 0.0)
            rows = slice(part * OWN, (part + 1) * OWN)
            place = ((owner % 2) ^ core, (owner // 4) ^ y, ((owner // 2) % 2) ^ x_lo)
            share[(*place, slice(None), slice(0, UNIT))] = attn[rows]
            share[(*place, slice(None), slice(UNIT, 2 * UNIT))] = output[rows]
            share[(*place, slice(None), slice(2 * UNIT, SHARE))] = head_gains.astype(jnp.bfloat16)
    copies = [
        pltpu.make_async_copy(share.at[i], goal, done.at[i]) for i, goal in ((1, theirs), (0, mine))
    ]
    for copy in copies:
        copy.start()
    for copy in copies:
        copy.wait()


def out_kernel(mixed, tokens, gains, later, hidden, upper, lower, rows, weights, arrived):
    whole = fetch(later, weights, arrived, [(0, 2 * D)])
    for head in range(N_SEQ):
        rows[:, head * 2 * HEAD : (head + 1) * 2 * HEAD] = mixed[head]
    values = tokens[...].astype(jnp.float32) + contract(rows[...], whole[0]()[...])
    hidden[...] = values
    values = (values * inverse_norm(values) * gains[1:2, :]).astype(jnp.bfloat16)
    upper[...] = values[: ROWS // 2]
    lower[...] = values[ROWS // 2 :]


def mid_kernel(
    keep, got_0, got_1, last_0, last_1, hidden, incoming, gains, later,
    hidden_grad, upper, lower, mixed_grad, weights, arrived,
):
    parts = fetch(later, weights, arrived, [(i * 2 * HEAD, 2 * HEAD) for i in range(N_SEQ)])
    half = ROWS // 2
    total_0 = keep[:half, :] + got_0[:half, :].astype(jnp.float32) + last_0[...].astype(jnp.float32)
    total_1 = keep[2 * half : 3 * half, :] + got_1[:half, :].astype(jnp.float32)
    total_1 = total_1 + last_1[...].astype(jnp.float32)
    pulled = jnp.concatenate([total_0, total_1], axis=0) * gains[1:2, :]
    inverse = inverse_norm(hidden[...])
    unit = hidden[...] * inverse
    mean = jnp.mean(unit * pulled, axis=-1, keepdims=True)
    grad = incoming[...].astype(jnp.float32) + inverse * (pulled - unit * mean)
    hidden_grad[...] = grad
    grad = grad.astype(jnp.bfloat16)
    upper[...] = grad[:half]
    lower[...] = grad[half:]
    for head in range(N_SEQ):
        mixed_grad[head] = product(grad, parts[head]()[...]).astype(jnp.bfloat16)


def ordered(pieces, place):
    half = pieces[0].shape[0]
    for array, step, relative, color in PIECES:
        begin = (2 * relative + color) * half
        place[begin : begin + half, :] = pieces[array][step * half : (step + 1) * half, :]


def send_order(values, first_0, first_1, keep):
    half = values.shape[0] // 8

    def block(relative, color):
        begin = (2 * relative + color) * half
        return values[begin : begin + half]

    first_0[:half, :] = block(3, 0).astype(jnp.bfloat16)
    first_0[half:, :] = block(2, 0).astype(jnp.bfloat16)
    first_1[:half, :] = block(1, 1).astype(jnp.bfloat16)
    first_1[half:, :] = block(2, 1).astype(jnp.bfloat16)
    for i, (relative, color) in enumerate(KEPT):
        keep[i * half : (i + 1) * half, :] = block(relative, color)


def kept(values):
    half = values.shape[0] // 4

    def block(relative, color):
        i = KEPT.index((relative, color))
        return values[i * half : (i + 1) * half]

    return block


def mlp_kernel(
    n0, n1, n2, n3, n4, n5, c0, c1, c2, c3, c4, c5, later,
    rows, incoming, both_grad, inner, first_0, first_1, keep, weights, arrived,
):
    steps = range(0, FF_Z, BLOCK)
    parts = fetch(
        later, weights, arrived,
        [(i * FF_Z + begin, BLOCK) for begin in steps for i in range(3)], 2 * D,
    )
    ordered((n0, n1, n2, n3, n4, n5), rows)
    ordered((c0, c1, c2, c3, c4, c5), incoming)
    rows.send()
    incoming.send()
    for i, begin in enumerate(steps):
        columns, second = slice(begin, begin + BLOCK), slice(FF_Z + begin, FF_Z + begin + BLOCK)
        gate = product(rows[...], parts[3 * i]()[...])
        up = product(rows[...], parts[3 * i + 1]()[...])
        inner_grad = product(incoming[...], parts[3 * i + 2]()[...])
        sigmoid = jax.nn.sigmoid(gate)
        swish = gate * sigmoid
        inner[:, columns] = (swish * up).astype(jnp.bfloat16)
        both_grad[:, columns] = (
            inner_grad * up * sigmoid * (1.0 + gate * (1.0 - sigmoid))
        ).astype(jnp.bfloat16)
        both_grad[:, second] = (inner_grad * swish).astype(jnp.bfloat16)
    send_order(contract(both_grad[...], weights[:, : 2 * FF_Z]), first_0, first_1, keep)


def mlp_grad_kernel(
    rows, incoming, both_grad, inner, later,
    share, first_0, first_1, keep, weights, arrived,
):
    whole = fetch(later, weights, arrived, [(0, FF_Z)], 2 * D + 2 * FF_Z)
    for begin in range(0, D, BLOCK):
        goal = slice(begin, begin + BLOCK)
        share[goal, : 2 * FF_Z] = outer_rows(rows[:, goal], both_grad[...]).astype(jnp.bfloat16)
        share[goal, 2 * FF_Z :] = outer_rows(incoming[:, goal], inner[...]).astype(jnp.bfloat16)
        share.send(goal)
    send_order(contract(inner[...], whole[0]()[...]), first_0, first_1, keep)


def last_kernel(
    at, p0, p1, p2, p3, p4, p5, w_gate, w_up, w_query, w_key, w_value, norm_post, norm_input,
    gate, up, down_t, query, key, value, output_t, post_grad, input_grad, gain_grads,
):
    z, x_hi = at[0], at[1]
    pieces = (p0, p1, p2, p3, p4, p5)
    half, middle = OWN // 2, SHARE - FF_Z
    gain_total = jnp.zeros((8, HEAD), jnp.float32)
    for array, step, relative, color in PIECES:
        begin = 2 * step * OWN
        part = pieces[array][begin : begin + OWN, :].astype(jnp.float32)
        place, theirs = z ^ relative, x_hi ^ color
        head = 2 * place + theirs
        one = pl.ds(pl.multiple_of(head * HEAD, HEAD), HEAD)
        two = pl.ds(pl.multiple_of(head * 2 * HEAD, 2 * HEAD), 2 * HEAD)
        query[:, two] = part[:, : 2 * HEAD]
        key[:, one] = part[:, 2 * HEAD : 3 * HEAD]
        value[:, one] = part[:, 3 * HEAD : 4 * HEAD]
        for other in range(2):
            goal = (2 * place + (theirs ^ other)) * 2 * HEAD
            goal = pl.ds(pl.multiple_of(goal, 2 * HEAD), 2 * HEAD)
            first = UNIT + other * 2 * HEAD
            share = part[:, first : first + 2 * HEAD]
            output_t[:, goal] = share if color == 0 else output_t[:, goal] + share
        gain_total += part[0:8, 2 * UNIT :]
        left = pieces[array][begin + OWN : begin + OWN + half, :].astype(jnp.float32)
        right = pieces[array][begin + OWN + half : begin + 2 * OWN, :].astype(jnp.float32)
        rows = slice(color * half, (color + 1) * half)
        start = place * FF_Z
        columns = pl.ds(pl.multiple_of(start, FF_Z), FF_Z)
        gate[rows, columns] = left[:, :FF_Z]
        up[rows, pl.ds(pl.multiple_of(start, FF_Z), middle)] = left[:, FF_Z:]
        up[rows, pl.ds(pl.multiple_of(start + middle, middle), middle)] = right[:, :middle]
        down_t[rows, columns] = right[:, middle:]
    for result in (gate, up, down_t, query, key, value, output_t):
        result.send()
    gain_grads[...] = gain_total

    def paired(*pairs):
        return functools.reduce(
            jnp.add,
            [
                jnp.sum(grad[...] * weight[...].astype(jnp.float32), axis=1, keepdims=True)
                for grad, weight in pairs
            ],
        )

    post_grad[...] = paired((gate, w_gate), (up, w_up)) / norm_post[...]
    input_grad[...] = paired((query, w_query), (key, w_key), (value, w_value)) / norm_input[...]


class Reading:
    def __init__(self, copy, place):
        self.copy, self.place, self.shape = copy, place, place.shape
        copy.start()

    def __getitem__(self, index):
        return self()[index]

    def __call__(self):
        if self.copy is not None:
            self.copy.wait()
            self.copy = None
        return self.place


class Writing:
    def __init__(self, place, goal, semaphores):
        self.place, self.goal, self.semaphores, self.copies = place, goal, semaphores, []
        self.shape = place.shape

    def __getitem__(self, index):
        return self.place[index]

    def __setitem__(self, index, values):
        self.place[index] = values

    def send(self, rows=slice(None)):
        copy = pltpu.make_async_copy(self.place.at[rows], self.goal.at[rows], next(self.semaphores))
        copy.start()
        self.copies.append(copy)


def fetch(source, place, arrived, parts, begin=0):
    result = []
    for i, (first, size) in enumerate(parts):
        part = place.at[:, pl.ds(first, size)]
        copy = pltpu.make_async_copy(source.at[:, pl.ds(begin + first, size)], part, arrived.at[i])
        result.append(Reading(copy, part))
    return result


def kernel_call(kernel, inputs, outs, limit, scratch=(), flops=0, raw=(), raw_outs=0):
    modes = ["scalar" if x.ndim == 1 else "raw" if i in raw else "copy" for i, x in enumerate(inputs)]
    n_in, n_out = len(inputs), len(outs)
    buffers = [pltpu.VMEM(x.shape, x.dtype) for x, m in zip(inputs, modes) if m == "copy"]
    out_buffers = [pltpu.VMEM(shape, dtype) for shape, dtype in outs[raw_outs:]]
    n_sent = 24

    def body(*refs):
        ins, results, rest = refs[:n_in], refs[n_in : n_in + n_out], refs[n_in + n_out :]
        places, rest = iter(rest[: len(buffers)]), rest[len(buffers) :]
        out_places, rest = rest[: len(out_buffers)], rest[len(out_buffers) :]
        (arrived, sent), rest = rest[:2], rest[2:]
        semaphores = iter([sent.at[i] for i in range(n_sent)])
        args = []
        for i, (ref, mode) in enumerate(zip(ins, modes)):
            if mode == "copy":
                place = next(places)
                ref = Reading(pltpu.make_async_copy(ref, place, arrived.at[i]), place)
            args.append(ref)
        writes = [Writing(p, g, semaphores) for p, g in zip(out_places, results[raw_outs:])]
        kernel(*args, *results[:raw_outs], *writes, *rest)
        for read in args:
            if isinstance(read, Reading):
                read()
        for write in writes:
            if not write.copies:
                write.send()
        for write in writes:
            for copy in write.copies:
                copy.wait()

    anywhere, scalars = pl.BlockSpec(memory_space=pltpu.HBM), pl.BlockSpec(memory_space=pltpu.SMEM)
    return pl.pallas_call(
        body,
        out_shape=[jax.ShapeDtypeStruct(shape, dtype) for shape, dtype in outs],
        in_specs=[scalars if m == "scalar" else anywhere for m in modes],
        out_specs=[anywhere] * n_out,
        scratch_shapes=[
            *buffers,
            *out_buffers,
            pltpu.SemaphoreType.DMA((n_in,)),
            pltpu.SemaphoreType.DMA((n_sent,)),
            *(x if not isinstance(x, tuple) else pltpu.VMEM(*x) for x in scratch),
        ],
        compiler_params=pltpu.CompilerParams(vmem_limit_bytes=GRANT * MEGA),
        cost_estimate=pl.CostEstimate(flops=flops, bytes_accessed=8 * MEGA, transcendentals=0),
    )(*inputs)


def per_device(
    tokens,
    segments,
    norm_input,
    w_query,
    w_key,
    w_value,
    norm_query,
    norm_key,
    w_output,
    norm_post,
    w_gate,
    w_up,
    w_down,
    cotangent,
):
    bf16, f32 = jnp.bfloat16, jnp.float32
    s, f = lax.axis_index("seq"), lax.axis_index("fsdp")
    z, x_hi = s // 2, s % 2
    at = jnp.stack([z, x_hi, f // 4, (f // 2) % 2, f % 2]).astype(jnp.int32)
    sequence = tokens[0]
    table = rotation()
    ids = segments[0]
    first_key = jnp.sum((ids[None, :] < ids[:, None]).astype(jnp.int32), axis=1).reshape(1, LENGTH)

    token_pieces = gather4(sequence, swap_x_hi(sequence), swap_z_a, swap_z_b)

    def spread(values):
        wide = jnp.tile(values, N_FSDP)
        owner = jnp.arange(wide.shape[0], dtype=jnp.int32) // values.shape[0]
        return jnp.where(owner == f, wide, jnp.zeros_like(wide))

    def my_columns(values, width):
        return lax.dynamic_slice_in_dim(values, s * width, width, 1)

    rest = jnp.zeros((UNIT - 2 * HEAD,), bf16)
    extra = jnp.concatenate(
        [spread(norm_input), spread(norm_post), spread(norm_query), spread(norm_key), rest]
    ).reshape(5, UNIT)
    extra = jnp.pad(extra, ((0, EXTRA - 5), (0, 0)))
    my_unit = jnp.concatenate(
        [my_columns(w_query, 2 * HEAD), my_columns(w_key, HEAD), my_columns(w_value, HEAD)], axis=1
    )
    piece = lax.optimization_barrier(jnp.concatenate([my_unit, extra], axis=0))
    pair = jnp.concatenate([piece, swap_core(piece)], axis=0)
    other_pair = jnp.concatenate([swap_x_lo(piece), swap_chip(piece)], axis=0)
    pair, other_pair = lax.optimization_barrier((pair, other_pair))
    unit_pieces = gather4(pair, other_pair, swap_y_a, swap_y_b)

    def slice_z(values):
        return lax.dynamic_slice_in_dim(values, z * FF_Z, FF_Z, 1)

    later = jnp.concatenate(
        [w_output.T, slice_z(w_gate), slice_z(w_up), slice_z(w_down.T)], axis=1
    )
    later = lax.all_gather(later, "fsdp", axis=0, tiled=True)

    incoming = after(cotangent[0], (token_pieces[1], token_pieces[4]))
    cotangent_z = gather4(*halves(incoming), swap_z_a, swap_z_b)
    token_pieces = after(token_pieces, cotangent_z)

    normed, raw, heads, mixed, turned, log_total, gains, weight = kernel_call(
        front_kernel,
        (at, *token_pieces, *unit_pieces, first_key, table),
        (
            ((LENGTH, D), bf16),
            ((LENGTH, 3 * HEAD), f32),
            ((LENGTH, UNIT), bf16),
            ((LENGTH, 2 * HEAD), bf16),
            ((2, Z, ROWS, 2 * HEAD), bf16),
            ((8, LENGTH), f32),
            ((8, D), f32),
            ((D, UNIT), bf16),
        ),
        28,
        scratch=(((HEAD, LENGTH), bf16),),
        flops=4 * 10**9,
    )

    mixed_tokens = lax.all_to_all(
        mixed.reshape(N_SEQ, ROWS, 2 * HEAD), "seq", split_axis=0, concat_axis=0, tiled=True
    )
    half_rows = ((ROWS // 2, D), bf16)
    hidden, upper, lower = kernel_call(
        out_kernel,
        (mixed_tokens, sequence, gains, later),
        (((ROWS, D), f32), half_rows, half_rows),
        16,
        scratch=(((ROWS, 2 * D), bf16), ((D, 2 * D), bf16), pltpu.SemaphoreType.DMA((1,))),
        flops=10**9,
        raw=(3,),
    )
    turned = after(turned, upper).reshape(2, Z * ROWS, 2 * HEAD)
    mixed_mine, mixed_other = turned[0], swap_x_hi(turned[1])
    normed_post_z = gather4(upper, lower, swap_z_a, swap_z_b)
    sent = (((ROWS, D), bf16), ((ROWS, D), bf16), ((2 * ROWS, D), f32))
    rows_z, incoming_z, both_grad, inner, first_0, first_1, keep = kernel_call(
        mlp_kernel,
        (*normed_post_z, *cotangent_z, later),
        (
            ((Z * ROWS, D), bf16),
            ((Z * ROWS, D), bf16),
            ((Z * ROWS, 2 * FF_Z), bf16),
            ((Z * ROWS, FF_Z), bf16),
            *sent,
        ),
        28,
        scratch=(((D, 3 * FF_Z), bf16), pltpu.SemaphoreType.DMA((9,))),
        flops=4 * 10**9,
        raw=(12,),
    )
    mlp_share, down_0, down_1, down_keep = kernel_call(
        mlp_grad_kernel,
        (rows_z, incoming_z, both_grad, inner, later),
        (((D, 3 * FF_Z), bf16), *sent),
        24,
        scratch=(((D, FF_Z), bf16), pltpu.SemaphoreType.DMA((1,))),
        flops=4 * 10**9,
        raw=(4,),
    )
    got_0, got_1, last_0, last_1 = scatter4(
        first_0, first_1, kept(keep), swap_z_a, swap_z_b, mlp_share
    )
    mlp_share = lax.psum_scatter(mlp_share, "fsdp", scatter_dimension=0, tiled=True)
    hidden_grad, upper, lower, mixed_grad = kernel_call(
        mid_kernel,
        (keep, got_0, got_1, last_0, last_1, hidden, cotangent[0], gains, later),
        (((ROWS, D), f32), half_rows, half_rows, ((N_SEQ, ROWS, 2 * HEAD), bf16)),
        16,
        scratch=(((D, 2 * D), bf16), pltpu.SemaphoreType.DMA((8,))),
        flops=10**9,
        raw=(8,),
    )
    mixed_grad = lax.all_to_all(mixed_grad, "seq", split_axis=0, concat_axis=0, tiled=True)
    proj_grad_z = gather4(upper, lower, swap_z_a, swap_z_b)
    down_0, down_1 = after((down_0, down_1), upper)
    down_got_0, down_got_1, down_last_0, down_last_1 = scatter4(
        down_0, down_1, kept(down_keep), swap_z_a, swap_z_b
    )
    mixed_grad = after(mixed_grad, (down_got_0, down_got_1))

    back, gain_grads, dx_0, dx_1, dx_keep = kernel_call(
        back_kernel,
        (at, raw, heads, log_total, mixed_grad.reshape(LENGTH, 2 * HEAD), first_key, table, gains, weight),
        (
            ((LENGTH, UNIT), bf16),
            ((8, HEAD), f32),
            ((2 * ROWS, D), bf16),
            ((2 * ROWS, D), bf16),
            ((4 * ROWS, D), f32),
        ),
        30,
        scratch=(
            ((HEAD, LENGTH), bf16),
            ((LENGTH, HEAD), f32),
            ((LENGTH, HEAD), f32),
            ((LENGTH, 2 * HEAD), f32),
            ((LENGTH, UNIT), bf16),
        ),
        flops=4 * 10**9,
    )
    share, share_sent = kernel_call(
        grad_kernel,
        (at, normed, back, gain_grads, *proj_grad_z, mixed_mine, mixed_other),
        (((Z, 2, OWN, SHARE), bf16), ((Z, 2, OWN, SHARE), bf16)),
        20,
        scratch=(
            ((2, Z, 2, OWN, SHARE), bf16),
            ((Z * ROWS, D), bf16),
            ((Z * ROWS, UNIT), bf16),
            pltpu.SemaphoreType.DMA((2,)),
        ),
        flops=4 * 10**9,
        raw_outs=2,
    )
    share = share.reshape(D // 2, SHARE)
    other_share = swap_core(share_sent.reshape(D // 2, SHARE))

    def share_block(relative, color):
        begin = (2 * relative + color) * OWN
        mine, other = share[begin : begin + OWN], other_share[begin : begin + OWN]
        return mine.astype(f32) + other.astype(f32)

    def share_pair(one, two):
        return jnp.concatenate([share_block(*one), share_block(*two)], axis=0).astype(bf16)

    share_0, share_1 = total4(
        share_block,
        *scatter4(
            share_pair((3, 0), (2, 0)), share_pair((1, 1), (2, 1)), share_block, swap_y_a, swap_y_b
        ),
    )
    attn_share = (share_0 + swap_x_lo(share_1.astype(bf16)).astype(f32)).astype(bf16)

    mine = jnp.concatenate([attn_share, mlp_share[:, :SHARE], mlp_share[:, SHARE:]], axis=0)
    mine = lax.optimization_barrier(mine)
    other = swap_x_hi(mine)
    mlp_sum = (mine[OWN:].astype(f32) + other[OWN:].astype(f32)).astype(bf16)
    half = OWN // 2
    zero = jnp.concatenate([mine[:OWN], mlp_sum[:half], mlp_sum[OWN : OWN + half]], axis=0)
    one = jnp.concatenate([other[:OWN], mlp_sum[half:OWN], mlp_sum[OWN + half :]], axis=0)
    zero, one = lax.optimization_barrier((zero, one))
    last_pieces = gather4(zero, one, swap_z_a, swap_z_b)

    normed_grad, other_grad = total4(
        kept(dx_keep), *scatter4(dx_0, dx_1, kept(dx_keep), swap_z_a, swap_z_b)
    )
    normed_grad = normed_grad + swap_x_hi(other_grad.astype(bf16)).astype(f32)
    normed_grad = normed_grad * gains[0:1]
    widened = sequence.astype(f32)
    inverse = inverse_norm(widened)
    unit_input = widened * inverse
    tokens_grad = hidden_grad + inverse * (
        normed_grad - unit_input * jnp.mean(unit_input * normed_grad, axis=-1, keepdims=True)
    )

    down_last = after((down_last_0, down_last_1), last_pieces)
    down = total4(kept(down_keep), down_got_0, down_got_1, *down_last)
    result = (hidden + jnp.concatenate(down, axis=0)).astype(bf16)

    (
        gate_total,
        up_total,
        down_total,
        query_total,
        key_total,
        value_total,
        output_total,
        post_gain_total,
        input_gain_total,
        head_gain_total,
    ) = kernel_call(
        last_kernel,
        (
            at, *last_pieces, w_gate, w_up, w_query, w_key, w_value,
            norm_post.astype(f32).reshape(OWN, 1), norm_input.astype(f32).reshape(OWN, 1),
        ),
        (
            ((OWN, FF), f32),
            ((OWN, FF), f32),
            ((OWN, FF), f32),
            ((OWN, 2 * D), f32),
            ((OWN, D), f32),
            ((OWN, D), f32),
            ((OWN, 2 * D), f32),
            ((OWN, 1), f32),
            ((OWN, 1), f32),
            ((8, HEAD), f32),
        ),
        16,
    )
    return (
        result[None],
        tokens_grad[None],
        input_gain_total.reshape(OWN),
        query_total,
        key_total,
        value_total,
        head_gain_total[0, :8],
        head_gain_total[0, 8:16],
        output_total.T,
        post_gain_total.reshape(OWN),
        gate_total,
        up_total,
        down_total.T,
    )


def solution(mesh):
    rows, columns, tokens = P("fsdp", None), P(None, "fsdp"), P("fsdp", "seq", None)
    in_specs = (
        tokens, rows, P("fsdp"), rows, rows, rows, P("fsdp"), P("fsdp"), columns, P("fsdp"),
        rows, rows, columns, tokens,
    )
    out_specs = (
        tokens, tokens, P("fsdp"), rows, rows, rows, P("fsdp"), P("fsdp"), columns, P("fsdp"),
        rows, rows, columns,
    )
    return jax.shard_map(
        per_device, mesh=mesh, in_specs=in_specs, out_specs=out_specs, check_vma=False
    )
```

time: 910 us -> 304 us (0.33)
  the two profiles are of different devices: /device:TPU:0 before, /device:TPU:2 now
where the time goes in v1:
time: 304 us; the launch traced here: 298 us
  waiting for transfers between devices  87.2 us (29%)
  starting transfers between devices  71 us (23%)
  Pallas kernels  69.5 us (23%)
  other arithmetic  22.8 us (8%)
  local copies, waits for them, and re-layouts  16.9 us (6%)
  between operations  15.5 us (5%)
  blocking collectives  15.4 us (5%)
    ppermute x49, waiting for transfers between devices, exchange(): return lax.ppermute(values, axis, [(i, i ^ bits) for i in range(size)])  83.1 us
    pallas_call x8, Pallas kernels, kernel_call(): pl.pallas_call(body, out_shape=[jax.ShapeDtypeStruct(shape, dtype) for sh...  69.5 us
    ppermute x49, starting transfers between devices, exchange(): return lax.ppermute(values, axis, [(i, i ^ bits) for i in range(size)])  65.4 us
    all_to_all x1, blocking collectives, per_device(): lax.all_to_all(mixed.reshape(N_SEQ, ROWS, 2 * HEAD), 'seq', split_axis=0,...  15.4 us
    unnamed x134, local copies, waits for them, and re-layouts  7.84 us
  transfers between devices with their start and end apart: 52, of which 26 were waited for; matrix products, arithmetic and copies ran while one was open for 8% of the time, Pallas kernels for 13%

profile of v1, /device:TPU:2, one launch (start us, length us, event | category | flops | bytes accessed | tf_op | source)
XLA Modules:
  0.0 298.2 jit_solution(13190744132830167781)
XLA Ops:
  9.2 1.8 pad_maximum_fusion.2
  14.4 1.6 collective-permute-start.10
  16.0 2.1 collective-permute-start.2
  18.1 2.7 collective-permute-done.10
  20.9 1.7 collective-permute-start.12
  22.5 1.9 collective-permute-start
  24.4 4.7 %collective-permute-done.2.refs_4_ = bf16[128,1024]{1,0:T(8,128)(2,1)S(1)} collective-permute-done((bf16[128,1024]{1,0:T(8,128)(2,1)S(1)}, bf16[128,1024]{1,0:T(8,128)(2,1)S(1)}, u32[]{:S(2)}, u32[]{:S(2)}) %collective-permute-start.2) | collective-permute-done | bytes 262176 | tf_op jit(solution)/shard_map/ppermute | solution.py:49
  29.1 5.1 %collective-permute-start.3 = (bf16[128,1024]{1,0:T(8,128)(2,1)S(1)}, bf16[128,1024]{1,0:T(8,128)(2,1)S(1)}, u32[]{:S(2)}, u32[]{:S(2)}) collective-permute-start(bf16[128,1024]{1,0:T(8,128)(2,1)S(1)} %collective-permute-done.2.refs_4_), channel_id=1, source_target_pairs={{0,96},{16,112},{32,64},{48,80},{64,32},{80,48},{96,0},{112,16},{1... | collective-permute-start | bytes 786440 | tf_op jit(solution)/shard_map/ppermute | solution.py:49
  34.2 3.3 %collective-permute-start.14 = (bf16[160,512]{1,0:T(8,128)(2,1)S(1)}, bf16[160,512]{1,0:T(8,128)(2,1)S(1)}, u32[]{:S(2)}, u32[]{:S(2)}) collective-permute-start(bf16[160,512]{1,0:T(8,128)(2,1)S(1)} %pad_maximum_fusion.19.refs_10_), channel_id=1, source_target_pairs={{0,12},{1,13},{2,14},{3,15},{4,8},{5,9},{6,10},{7,11},{8,4},{9,5},... | collective-permute-start | bytes 491528 | tf_op jit(solution)/shard_map/ppermute | solution.py:49
  38.1 2.4 collective-permute-done.3.refs_5_
  40.6 3.8 %collective-permute-start.7 = (bf16[64,1024]{1,0:T(8,128)(2,1)S(1)}, bf16[64,1024]{1,0:T(8,128)(2,1)S(1)}, u32[]{:S(2)}, u32[]{:S(2)}) collective-permute-start(bf16[64,1024]{1,0:T(8,128)(2,1)S(1)} %get-tuple-element.159.refs_9_), channel_id=1, source_target_pairs={{0,96},{16,112},{32,64},{48,80},{64,32},{80,48},{96,0},{112,16},{1... | collective-permute-start | bytes 393224 | tf_op jit(solution)/shard_map/ppermute | solution.py:49
  44.4 2.1 collective-permute-start.4
  46.6 7.0 %collective-permute-done.7.refs_10_ = bf16[64,1024]{1,0:T(8,128)(2,1)S(1)} collective-permute-done((bf16[64,1024]{1,0:T(8,128)(2,1)S(1)}, bf16[64,1024]{1,0:T(8,128)(2,1)S(1)}, u32[]{:S(2)}, u32[]{:S(2)}) %collective-permute-start.7) | collective-permute-done | bytes 131104 | tf_op jit(solution)/shard_map/ppermute | solution.py:49
  54.5 3.0 %collective-permute-start.6 = (bf16[128,1024]{1,0:T(8,128)(2,1)S(1)}, bf16[128,1024]{1,0:T(8,128)(2,1)S(1)}, u32[]{:S(2)}, u32[]{:S(2)}) collective-permute-start(bf16[128,1024]{1,0:T(8,128)(2,1)S(1)} %pad_maximum_fusion.12), channel_id=1, source_target_pairs={{0,96},{16,112},{32,64},{48,80},{64,32},{80,48},{96,0},{112,16},{1... | collective-permute-start | bytes 786440 | tf_op jit(solution)/shard_map/ppermute | solution.py:49
  58.2 1.2 convert_reduce_fusion
  59.5 2.3 collective-permute-done.8.refs_11_
  62.6 6.1 %collective-permute-done.15.refs_12_ = bf16[320,512]{1,0:T(8,128)(2,1)} collective-permute-done((bf16[320,512]{1,0:T(8,128)(2,1)S(1)}, bf16[320,512]{1,0:T(8,128)(2,1)}, u32[]{:S(2)}, u32[]{:S(2)}) %collective-permute-start.15) | collective-permute-done | bytes 327712 | tf_op jit(solution)/shard_map/ppermute | solution.py:49
  68.6 12.0 %shard_map.246 = (bf16[1024,1024]{1,0:T(8,128)(2,1)}, f32[1024,384]{1,0:T(8,128)}, bf16[1024,512]{1,0:T(8,128)(2,1)}, bf16[1024,256]{1,0:T(8,128)(2,1)}, bf16[2,...) custom-call(s32[5]{0:T(128)} %stack.23.refs_0_, ...), custom_call_target="tpu_custom_call" | custom-call | flops 4000000000 | bytes 8388608 | tf_op jit(solution)/shard_map/pallas_call | solution.py:534
  80.6 15.4 %all_to_all.10.refs_0_ = bf16[8,128,256]{2,1,0:T(8,128)(2,1)} all-to-all(bf16[8,128,256]{2,1,0:T(8,128)(2,1)} %bitcast.50), channel_id=1, replica_groups=mesh['seq'=8,'fsdp'=16] {'seq'}, dimensions={0} | all-to-all | bytes 1048576 | tf_op jit(solution)/shard_map/all_to_all | solution.py:630
  96.1 5.2 %shard_map.247 = (f32[128,1024]{1,0:T(8,128)}, bf16[64,1024]{1,0:T(8,128)(2,1)}, bf16[64,1024]{1,0:T(8,128)(2,1)}) custom-call(bf16[8,128,256]{2,1,0:T(8,128)(2,1)} %all_to_all.10.refs_0_, bf16[128,1024]{1,0:T(8,128)(2,1)} %bitcast.39, f32[8,1024]{1,0:T(8,128)} %get-tuple-element.85.refs_2_.refs_7_, ...), custom_call_target="tpu_custom_call" | custom-call | flops 1000000000 | bytes 8388608 | tf_op jit(solution)/shard_map/pallas_call | solution.py:534
  102.4 5.3 %collective-permute-done.18.refs_4_ = bf16[64,1024]{1,0:T(8,128)(2,1)S(1)} collective-permute-done((bf16[64,1024]{1,0:T(8,128)(2,1)}, bf16[64,1024]{1,0:T(8,128)(2,1)S(1)}, u32[]{:S(2)}, u32[]{:S(2)}) %collective-permute-start.18) | collective-permute-done | bytes 131104 | tf_op jit(solution)/shard_map/ppermute | solution.py:49
  109.8 2.1 collective-permute-start.17
  111.9 3.3 %collective-permute-done.19.refs_5_ = bf16[128,1024]{1,0:T(8,128)(2,1)S(1)} collective-permute-done((bf16[128,1024]{1,0:T(8,128)(2,1)S(1)}, bf16[128,1024]{1,0:T(8,128)(2,1)S(1)}, u32[]{:S(2)}, u32[]{:S(2)}) %collective-permute-start.19) | collective-permute-done | bytes 262176 | tf_op jit(solution)/shard_map/ppermute | solution.py:49
  115.2 2.5 collective-permute-done.17.refs_2_
  118.4 12.9 %shard_map.248 = (bf16[512,1024]{1,0:T(8,128)(2,1)}, bf16[512,1024]{1,0:T(8,128)(2,1)}, bf16[512,1536]{1,0:T(8,128)(2,1)}, bf16[512,768]{1,0:T(8,128)(2,1)}, bf1...) custom-call(bf16[64,1024]{1,0:T(8,128)(2,1)} %get-tuple-element.87.refs_0_, ...), custom_call_target="tpu_custom_call" | custom-call | flops 4000000000 | bytes 8388608 | tf_op jit(solution)/shard_map/pallas_call | solution.py:534
  131.3 7.3 %shard_map.249 = (bf16[1024,2304]{1,0:T(8,128)(2,1)}, bf16[128,1024]{1,0:T(8,128)(2,1)}, bf16[128,1024]{1,0:T(8,128)(2,1)}, f32[256,1024]{1,0:T(8,128)}) custom-call(bf16[512,1024]{1,0:T(8,128)(2,1)} %get-tuple-element.89.refs_0_, bf16[512,1024]{1,0:T(8,128)(2,1)} %get-tuple-element.90.refs_1_, bf16[512,1536]{1,0:T(8,128)(2,1)} %get-tuple-element.91.refs_2_, ...), custom_call_target="tpu_custom_call" | custom-call | flops 4000000000 | bytes 8388608 | tf_op jit(solution)/shard_map/pallas_call | solution.py:534
  139.5 1.8 collective-permute-start.20
  141.4 5.9 %collective-permute-done.20.refs_1_ = bf16[128,1024]{1,0:T(8,128)(2,1)S(1)} collective-permute-done((bf16[128,1024]{1,0:T(8,128)(2,1)S(1)}, bf16[128,1024]{1,0:T(8,128)(2,1)S(1)}, u32[]{:S(2)}, u32[]{:S(2)}) %collective-permute-start.20) | collective-permute-done | bytes 262176 | tf_op jit(solution)/shard_map/ppermute | solution.py:49
  147.8 1.5 collective-permute-start.23
  149.3 4.8 %collective-permute-done.23.refs_4_ = bf16[64,1024]{1,0:T(8,128)(2,1)S(1)} collective-permute-done((bf16[64,1024]{1,0:T(8,128)(2,1)S(1)}, bf16[64,1024]{1,0:T(8,128)(2,1)S(1)}, u32[]{:S(2)}, u32[]{:S(2)}) %collective-permute-start.23) | collective-permute-done | bytes 131104 | tf_op jit(solution)/shard_map/ppermute | solution.py:49
  154.9 6.9 %shard_map.250 = (f32[128,1024]{1,0:T(8,128)}, bf16[64,1024]{1,0:T(8,128)(2,1)}, bf16[64,1024]{1,0:T(8,128)(2,1)}, bf16[8,128,256]{2,1,0:T(8,128)(2,1)}) custom-call(f32[256,1024]{1,0:T(8,128)} %get-tuple-element.96.refs_0_, bf16[128,1024]{1,0:T(8,128)(2,1)} %copy-done.18, bf16[128,1024]{1,0:T(8,128)(2,1)} %copy-done.19, bf16[64,1024]{1,0:T(8,128)(2,1)} %copy-done.35, ...), custom_call_target="tpu_custom_call" | custom-call | flops 1000000000 | bytes 8388608 | tf_op jit(solution)/shard_map/pallas_call | solution.py:534
  162.0 5.5 %all-to-all-start.1 = ((bf16[8,128,256]{2,1,0:T(8,128)(2,1)}), bf16[8,128,256]{2,1,0:T(8,128)(2,1)S(1)}, u32[]{:S(2)}, u32[]{:S(2)}) async-start(bf16[8,128,256]{2,1,0:T(8,128)(2,1)} %get-tuple-element.109), calls=%async_computation.1 | async-start | bytes 1048576 | tf_op jit(solution)/shard_map/all_to_all | solution.py:684
  167.5 3.2 %collective-permute-start.30 = (bf16[64,1024]{1,0:T(8,128)(2,1)}, bf16[64,1024]{1,0:T(8,128)(2,1)S(1)}, u32[]{:S(2)}, u32[]{:S(2)}) collective-permute-start(bf16[64,1024]{1,0:T(8,128)(2,1)} %get-tuple-element.114.refs_7_), channel_id=1, source_target_pairs={{0,96},{16,112},{32,64},{48,80},{64,32},{80,48},{96,0},{112,16},{1... | collective-permute-start | bytes 393224 | tf_op jit(solution)/shard_map/ppermute | solution.py:49
  172.6 3.0 collective-permute-start.32
  175.6 1.9 collective-permute-start.31
  177.5 2.8 collective-permute-start.29
  180.9 4.1 %all-to-all-done.1 = bf16[8,128,256]{2,1,0:T(8,128)(2,1)S(1)} async-done(((bf16[8,128,256]{2,1,0:T(8,128)(2,1)}), bf16[8,128,256]{2,1,0:T(8,128)(2,1)S(1)}, u32[]{:S(2)}, u32[]{:S(2)}) %all-to-all-start.1) | async-done | bytes 524320 | tf_op jit(solution)/shard_map/all_to_all | solution.py:684
  185.9 13.4 %shard_map.251 = (bf16[1024,512]{1,0:T(8,128)(2,1)}, f32[8,128]{1,0:T(8,128)}, bf16[256,1024]{1,0:T(8,128)(2,1)}, bf16[256,1024]{1,0:T(8,128)(2,1)}, f32[512,1024]{1,0:T(8,128)}) custom-call(s32[5]{0:T(128)} %stack.23.refs_0_, f32[1024,384]{1,0:T(8,128)} %get-tuple-element.106.refs_1_, bf16[1024,512]{1,0:T(8,128)(2,1)} %get-tuple-element.107.refs_2_, ...), custom_call_target="tpu_custom_call" | custom-call | flops 4000000000 | bytes 8388608 | tf_op jit(solution)/shard_map/pallas_call | solution.py:534
  200.2 7.0 %shard_map.252 = (bf16[4,2,64,1152]{3,2,1,0:T(8,128)(2,1)}, bf16[4,2,64,1152]{3,2,1,0:T(8,128)(2,1)}) custom-call(s32[5]{0:T(128)} %stack.23.refs_0_, bf16[1024,1024]{1,0:T(8,128)(2,1)} %get-tuple-element.105.refs_1_, bf16[1024,512]{1,0:T(8,128)(2,1)} %get-tuple-element.112.refs_2_, f32[8,128]{1,0:T(8,128)} %get-tuple-element.113.refs_3_, ...), custom_call_target="tpu_custom_call" | custom-call | flops 4000000000 | bytes 8388608 | tf_op jit(solution)/shard_map/pallas_call | solution.py:534
  207.6 3.0 %collective-permute-done.33 = bf16[512,1152]{1,0:T(8,128)(2,1)S(1)} collective-permute-done((bf16[512,1152]{1,0:T(8,128)(2,1)}, bf16[512,1152]{1,0:T(8,128)(2,1)S(1)}, u32[]{:S(2)}, u32[]{:S(2)}) %collective-permute-start.33) | collective-permute-done | bytes 1179680 | tf_op jit(solution)/shard_map/ppermute | solution.py:49
  210.6 1.7 add_convert_fusion.11
  212.9 2.3 collective-permute-start.34
  215.3 6.2 %collective-permute-done.36 = bf16[128,1152]{1,0:T(8,128)(2,1)S(1)} collective-permute-done((bf16[128,1152]{1,0:T(8,128)(2,1)S(1)}, bf16[128,1152]{1,0:T(8,128)(2,1)S(1)}, u32[]{:S(2)}, u32[]{:S(2)}) %collective-permute-start.36) | collective-permute-done | bytes 294944 | tf_op jit(solution)/shard_map/ppermute | solution.py:49
  221.5 1.5 collective-permute-done.34
  223.8 2.5 collective-permute-start.37
  226.3 3.8 %collective-permute-done.37 = bf16[64,1152]{1,0:T(8,128)(2,1)S(1)} collective-permute-done((bf16[64,1152]{1,0:T(8,128)(2,1)S(1)}, bf16[64,1152]{1,0:T(8,128)(2,1)S(1)}, u32[]{:S(2)}, u32[]{:S(2)}) %collective-permute-start.37) | collective-permute-done | bytes 147488 | tf_op jit(solution)/shard_map/ppermute | solution.py:49
  230.9 2.2 collective-permute-start.38
  236.5 1.9 add_convert_fusion.4
  241.2 6.7 %collective-permute-done.44 = bf16[256,1024]{1,0:T(8,128)(2,1)} collective-permute-done((bf16[256,1024]{1,0:T(8,128)(2,1)}, bf16[256,1024]{1,0:T(8,128)(2,1)}, u32[]{:S(2)}, u32[]{:S(2)}) %collective-permute-start.44) | collective-permute-done | bytes 524320 | tf_op jit(solution)/shard_map/ppermute | solution.py:49
  247.9 1.2 add_convert_fusion.3
  249.1 1.8 collective-permute-start.47
  251.7 1.2 collective-permute-start.40
  253.9 2.2 collective-permute-start.27
  256.8 1.4 collective-permute-start.45
  258.8 2.0 collective-permute-start.42
  262.2 4.8 %collective-permute-done.42.refs_5_ = bf16[128,1152]{1,0:T(8,128)(2,1)S(1)} collective-permute-done((bf16[128,1152]{1,0:T(8,128)(2,1)S(1)}, bf16[128,1152]{1,0:T(8,128)(2,1)S(1)}, u32[]{:S(2)}, u32[]{:S(2)}) %collective-permute-start.42) | collective-permute-done | bytes 294944 | tf_op jit(solution)/shard_map/ppermute | solution.py:49
  267.1 2.3 collective-permute-start.41
  269.9 1.2 fusion.2
  271.1 2.0 fusion.6
  273.1 6.2 %collective-permute-done.41.refs_3_ = bf16[256,1152]{1,0:T(8,128)(2,1)S(1)} collective-permute-done((bf16[256,1152]{1,0:T(8,128)(2,1)S(1)}, bf16[256,1152]{1,0:T(8,128)(2,1)S(1)}, u32[]{:S(2)}, u32[]{:S(2)}) %collective-permute-start.41) | collective-permute-done | bytes 589856 | tf_op jit(solution)/shard_map/ppermute | solution.py:49
  280.2 4.7 %shard_map.253 = (f32[64,3072]{1,0:T(8,128)}, f32[64,3072]{1,0:T(8,128)}, f32[64,3072]{1,0:T(8,128)}, f32[64,2048]{1,0:T(8,128)}, f32[64,1024]{1,0:T(8,128)}, /*...) custom-call(s32[5]{0:T(128)} %stack.23.refs_0_, ...), custom_call_target="tpu_custom_call" | custom-call | bytes 8388608 | tf_op jit(solution)/shard_map/pallas_call | solution.py:534
  285.0 1.4 reduce
  286.4 1.4 reduce.1
  287.8 1.3 slice_bitcast_fusion
  (256 shorter events, 35.0 us)
Async XLA Ops:
  7.2 88.9 %all-gather.2.cloned.1.call-start = ((), (), s32[]{:S(2)}) async-start(), calls=%async_computation.3 | async-start | bytes 9469952 | tf_op jit(solution)/shard_map/all_gather | solution.py:606
  11.0 227.3 %reduce-scatter.2.cloned.1.call-start = ((), (), s32[]{:S(2)}) async-start(), calls=%async_computation.4 | async-start | bytes 5013504 | tf_op jit(solution)/shard_map/reduce_scatter | solution.py:674
  13.7 4.4 %collective-permute-start.9 = (bf16[80,512]{1,0:T(8,128)(2,1)S(1)}, bf16[80,512]{1,0:T(8,128)(2,1)S(1)}, u32[]{:S(2)}, u32[]{:S(2)}) collective-permute-start(bf16[80,512]{1,0:T(8,128)(2,1)S(1)} %fusion.11), channel_id=1, source_target_pairs={{0,1},{1,0},{2,3},{3,2},{4,5},{5,4},{6,7},{7,6},{8,9},{9,8},{10,11... | collective-permute-start | bytes 245768 | tf_op jit(solution)/shard_map/ppermute | solution.py:49
  13.8 4.3 %collective-permute-start.11 = (bf16[80,512]{1,0:T(8,128)(2,1)S(1)}, bf16[80,512]{1,0:T(8,128)(2,1)S(1)}, u32[]{:S(2)}, u32[]{:S(2)}) collective-permute-start(bf16[80,512]{1,0:T(8,128)(2,1)S(1)} %fusion.11), channel_id=1, source_target_pairs={{0,3},{1,2},{2,1},{3,0},{4,7},{5,6},{6,5},{7,4},{8,11},{9,10},{10,... | collective-permute-start | bytes 245768 | tf_op jit(solution)/shard_map/ppermute | solution.py:49
  14.4 6.5 %collective-permute-start.10 = (bf16[80,512]{1,0:T(8,128)(2,1)S(1)}, bf16[80,512]{1,0:T(8,128)(2,1)S(1)}, u32[]{:S(2)}, u32[]{:S(2)}) collective-permute-start(bf16[80,512]{1,0:T(8,128)(2,1)S(1)} %fusion.11), channel_id=1, source_target_pairs={{0,2},{1,3},{2,0},{3,1},{4,6},{5,7},{6,4},{7,5},{8,10},{9,11},{10,... | collective-permute-start | bytes 245768 | tf_op jit(solution)/shard_map/ppermute | solution.py:49
  16.0 24.6 %copy-start.15 = (bf16[1,128,1024]{2,1,0:T(8,128)(2,1)S(1)}, bf16[1,128,1024]{2,1,0:T(8,128)(2,1)}, u32[]{:S(2)}) copy-start(bf16[1,128,1024]{2,1,0:T(8,128)(2,1)} %param.28) | copy-start | bytes 786436
  16.0 13.1 %collective-permute-start.2 = (bf16[128,1024]{1,0:T(8,128)(2,1)S(1)}, bf16[128,1024]{1,0:T(8,128)(2,1)S(1)}, u32[]{:S(2)}, u32[]{:S(2)}) collective-permute-start(bf16[128,1024]{1,0:T(8,128)(2,1)S(1)} %bitcast.40), channel_id=1, source_target_pairs={{0,16},{16,0},{32,48},{48,32},{64,80},{80,64},{96,112},{112,96},{1... | collective-permute-start | bytes 786440 | tf_op jit(solution)/shard_map/ppermute | solution.py:49
  18.1 22.4 %copy-start.16 = (bf16[160,512]{1,0:T(8,128)(2,1)}, bf16[160,512]{1,0:T(8,128)(2,1)S(1)}, u32[]{:S(2)}) copy-start(bf16[160,512]{1,0:T(8,128)(2,1)S(1)} %pad_maximum_fusion.18.refs_7_) | copy-start | bytes 491524
  20.8 25.7 %copy-start.17 = (bf16[160,512]{1,0:T(8,128)(2,1)}, bf16[160,512]{1,0:T(8,128)(2,1)S(1)}, u32[]{:S(2)}) copy-start(bf16[160,512]{1,0:T(8,128)(2,1)S(1)} %pad_maximum_fusion.19.refs_10_) | copy-start | bytes 491524
  20.9 16.7 %collective-permute-start.12 = (bf16[160,512]{1,0:T(8,128)(2,1)S(1)}, bf16[160,512]{1,0:T(8,128)(2,1)S(1)}, u32[]{:S(2)}, u32[]{:S(2)}) collective-permute-start(bf16[160,512]{1,0:T(8,128)(2,1)S(1)} %pad_maximum_fusion.18.refs_7_), channel_id=1, source_target_pairs={{0,4},{1,5},{2,6},{3,7},{4,0},{5,1},{6,2},{7,3},{8,12},{9,13},{10,... | collective-permute-start | bytes 491528 | tf_op jit(solution)/shard_map/ppermute | solution.py:49
  22.5 15.1 %collective-permute-start = (bf16[128,1024]{1,0:T(8,128)(2,1)S(1)}, bf16[128,1024]{1,0:T(8,128)(2,1)S(1)}, u32[]{:S(2)}, u32[]{:S(2)}) collective-permute-start(bf16[128,1024]{1,0:T(8,128)(2,1)S(1)} %bitcast.41), channel_id=1, source_target_pairs={{0,32},{16,48},{32,0},{48,16},{64,96},{80,112},{96,64},{112,80},{1... | collective-permute-start | bytes 786440 | tf_op jit(solution)/shard_map/ppermute | solution.py:49
  29.1 11.4 %collective-permute-start.3 = (bf16[128,1024]{1,0:T(8,128)(2,1)S(1)}, bf16[128,1024]{1,0:T(8,128)(2,1)S(1)}, u32[]{:S(2)}, u32[]{:S(2)}) collective-permute-start(bf16[128,1024]{1,0:T(8,128)(2,1)S(1)} %collective-permute-done.2.refs_4_), channel_id=1, source_target_pairs={{0,96},{16,112},{32,64},{48,80},{64,32},{80,48},{96,0},{112,16},{1... | collective-permute-start | bytes 786440 | tf_op jit(solution)/shard_map/ppermute | solution.py:49
  34.2 10.2 %collective-permute-start.14 = (bf16[160,512]{1,0:T(8,128)(2,1)S(1)}, bf16[160,512]{1,0:T(8,128)(2,1)S(1)}, u32[]{:S(2)}, u32[]{:S(2)}) collective-permute-start(bf16[160,512]{1,0:T(8,128)(2,1)S(1)} %pad_maximum_fusion.19.refs_10_), channel_id=1, source_target_pairs={{0,12},{1,13},{2,14},{3,15},{4,8},{5,9},{6,10},{7,11},{8,4},{9,5},... | collective-permute-start | bytes 491528 | tf_op jit(solution)/shard_map/ppermute | solution.py:49
  37.6 25.0 %collective-permute-start.13 = (bf16[320,512]{1,0:T(8,128)(2,1)S(1)}, bf16[320,512]{1,0:T(8,128)(2,1)}, u32[]{:S(2)}, u32[]{:S(2)}) collective-permute-start(bf16[320,512]{1,0:T(8,128)(2,1)S(1)} %pad_maximum_fusion.6), channel_id=1, source_target_pairs={{0,12},{1,13},{2,14},{3,15},{4,8},{5,9},{6,10},{7,11},{8,4},{9,5},... | collective-permute-start | bytes 983048 | tf_op jit(solution)/shard_map/ppermute | solution.py:49
  37.7 16.0 %collective-permute-start.1 = (bf16[256,1024]{1,0:T(8,128)(2,1)S(1)}, bf16[256,1024]{1,0:T(8,128)(2,1)S(1)}, u32[]{:S(2)}, u32[]{:S(2)}) collective-permute-start(bf16[256,1024]{1,0:T(8,128)(2,1)S(1)} %pad_maximum_fusion.3), channel_id=1, source_target_pairs={{0,96},{16,112},{32,64},{48,80},{64,32},{80,48},{96,0},{112,16},{1... | collective-permute-start | bytes 1572872 | tf_op jit(solution)/shard_map/ppermute | solution.py:49
  40.6 13.0 %collective-permute-start.7 = (bf16[64,1024]{1,0:T(8,128)(2,1)S(1)}, bf16[64,1024]{1,0:T(8,128)(2,1)S(1)}, u32[]{:S(2)}, u32[]{:S(2)}) collective-permute-start(bf16[64,1024]{1,0:T(8,128)(2,1)S(1)} %get-tuple-element.159.refs_9_), channel_id=1, source_target_pairs={{0,96},{16,112},{32,64},{48,80},{64,32},{80,48},{96,0},{112,16},{1... | collective-permute-start | bytes 393224 | tf_op jit(solution)/shard_map/ppermute | solution.py:49
  44.3 9.2 %collective-permute-start.5 = (bf16[64,1024]{1,0:T(8,128)(2,1)S(1)}, bf16[64,1024]{1,0:T(8,128)(2,1)S(1)}, u32[]{:S(2)}, u32[]{:S(2)}) collective-permute-start(bf16[64,1024]{1,0:T(8,128)(2,1)S(1)} %get-tuple-element.160.refs_6_), channel_id=1, source_target_pairs={{0,32},{16,48},{32,0},{48,16},{64,96},{80,112},{96,64},{112,80},{1... | collective-permute-start | bytes 393224 | tf_op jit(solution)/shard_map/ppermute | solution.py:49
  44.4 24.2 %copy-start.33 = (bf16[160,512]{1,0:T(8,128)(2,1)}, bf16[160,512]{1,0:T(8,128)(2,1)S(1)}, u32[]{:S(2)}) copy-start(bf16[160,512]{1,0:T(8,128)(2,1)S(1)} %collective-permute-done.14.refs_11_) | copy-start | bytes 491524
  44.4 18.1 %collective-permute-start.4 = (bf16[256,1024]{1,0:T(8,128)(2,1)S(1)}, bf16[256,1024]{1,0:T(8,128)(2,1)S(1)}, u32[]{:S(2)}, u32[]{:S(2)}) collective-permute-start(bf16[256,1024]{1,0:T(8,128)(2,1)S(1)} %pad_maximum_fusion.4), channel_id=1, source_target_pairs={{0,32},{16,48},{32,0},{48,16},{64,96},{80,112},{96,64},{112,80},{1... | collective-permute-start | bytes 1572872 | tf_op jit(solution)/shard_map/ppermute | solution.py:49
  53.5 27.1 %copy-start.40 = (bf16[64,1024]{1,0:T(8,128)(2,1)}, bf16[64,1024]{1,0:T(8,128)(2,1)S(1)}, u32[]{:S(2)}) copy-start(bf16[64,1024]{1,0:T(8,128)(2,1)S(1)} %collective-permute-done.7.refs_10_) | copy-start | bytes 393220
  53.5 15.1 %collective-permute-start.15 = (bf16[320,512]{1,0:T(8,128)(2,1)S(1)}, bf16[320,512]{1,0:T(8,128)(2,1)}, u32[]{:S(2)}, u32[]{:S(2)}) collective-permute-start(bf16[320,512]{1,0:T(8,128)(2,1)S(1)} %pad_maximum_fusion.7), channel_id=1, source_target_pairs={{0,4},{1,5},{2,6},{3,7},{4,0},{5,1},{6,2},{7,3},{8,12},{9,13},{10,... | collective-permute-start | bytes 983048 | tf_op jit(solution)/shard_map/ppermute | solution.py:49
  53.6 27.0 %copy-start.41 = (bf16[64,1024]{1,0:T(8,128)(2,1)}, bf16[64,1024]{1,0:T(8,128)(2,1)S(1)}, u32[]{:S(2)}) copy-start(bf16[64,1024]{1,0:T(8,128)(2,1)S(1)} %collective-permute-done.5.refs_7_) | copy-start | bytes 393220
  53.6 8.1 %collective-permute-start.8 = (bf16[128,1024]{1,0:T(8,128)(2,1)S(1)}, bf16[128,1024]{1,0:T(8,128)(2,1)S(1)}, u32[]{:S(2)}, u32[]{:S(2)}) collective-permute-start(bf16[128,1024]{1,0:T(8,128)(2,1)S(1)} %pad_maximum_fusion.13), channel_id=1, source_target_pairs={{0,32},{16,48},{32,0},{48,16},{64,96},{80,112},{96,64},{112,80},{1... | collective-permute-start | bytes 786440 | tf_op jit(solution)/shard_map/ppermute | solution.py:49
  54.5 8.0 %collective-permute-start.6 = (bf16[128,1024]{1,0:T(8,128)(2,1)S(1)}, bf16[128,1024]{1,0:T(8,128)(2,1)S(1)}, u32[]{:S(2)}, u32[]{:S(2)}) collective-permute-start(bf16[128,1024]{1,0:T(8,128)(2,1)S(1)} %pad_maximum_fusion.12), channel_id=1, source_target_pairs={{0,96},{16,112},{32,64},{48,80},{64,32},{80,48},{96,0},{112,16},{1... | collective-permute-start | bytes 786440 | tf_op jit(solution)/shard_map/ppermute | solution.py:49
  61.7 18.9 %copy-start.55 = (bf16[128,1024]{1,0:T(8,128)(2,1)}, bf16[128,1024]{1,0:T(8,128)(2,1)S(1)}, u32[]{:S(2)}) copy-start(bf16[128,1024]{1,0:T(8,128)(2,1)S(1)} %collective-permute-done.8.refs_11_) | copy-start | bytes 786436
  62.6 18.1 %copy-start.56 = (bf16[128,1024]{1,0:T(8,128)(2,1)}, bf16[128,1024]{1,0:T(8,128)(2,1)S(1)}, u32[]{:S(2)}) copy-start(bf16[128,1024]{1,0:T(8,128)(2,1)S(1)} %collective-permute-done.6.refs_8_) | copy-start | bytes 786436
  101.3 6.5 %collective-permute-start.18 = (bf16[64,1024]{1,0:T(8,128)(2,1)}, bf16[64,1024]{1,0:T(8,128)(2,1)S(1)}, u32[]{:S(2)}, u32[]{:S(2)}) collective-permute-start(bf16[64,1024]{1,0:T(8,128)(2,1)} %get-tuple-element.88.refs_3_), channel_id=1, source_target_pairs={{0,96},{16,112},{32,64},{48,80},{64,32},{80,48},{96,0},{112,16},{1... | collective-permute-start | bytes 393224 | tf_op jit(solution)/shard_map/ppermute | solution.py:49
  102.2 6.6 %collective-permute-start.16 = (bf16[64,1024]{1,0:T(8,128)(2,1)}, bf16[64,1024]{1,0:T(8,128)(2,1)S(1)}, u32[]{:S(2)}, u32[]{:S(2)}) collective-permute-start(bf16[64,1024]{1,0:T(8,128)(2,1)} %get-tuple-element.87.refs_0_), channel_id=1, source_target_pairs={{0,32},{16,48},{32,0},{48,16},{64,96},{80,112},{96,64},{112,80},{1... | collective-permute-start | bytes 393224 | tf_op jit(solution)/shard_map/ppermute | solution.py:49
  108.7 6.5 %collective-permute-start.19 = (bf16[128,1024]{1,0:T(8,128)(2,1)S(1)}, bf16[128,1024]{1,0:T(8,128)(2,1)S(1)}, u32[]{:S(2)}, u32[]{:S(2)}) collective-permute-start(bf16[128,1024]{1,0:T(8,128)(2,1)S(1)} %pad_maximum_fusion.15), channel_id=1, source_target_pairs={{0,32},{16,48},{32,0},{48,16},{64,96},{80,112},{96,64},{112,80},{1... | collective-permute-start | bytes 786440 | tf_op jit(solution)/shard_map/ppermute | solution.py:49
  109.8 7.8 %collective-permute-start.17 = (bf16[128,1024]{1,0:T(8,128)(2,1)S(1)}, bf16[128,1024]{1,0:T(8,128)(2,1)S(1)}, u32[]{:S(2)}, u32[]{:S(2)}) collective-permute-start(bf16[128,1024]{1,0:T(8,128)(2,1)S(1)} %pad_maximum_fusion.14), channel_id=1, source_target_pairs={{0,96},{16,112},{32,64},{48,80},{64,32},{80,48},{96,0},{112,16},{1... | collective-permute-start | bytes 786440 | tf_op jit(solution)/shard_map/ppermute | solution.py:49
  139.5 7.7 %collective-permute-start.20 = (bf16[128,1024]{1,0:T(8,128)(2,1)S(1)}, bf16[128,1024]{1,0:T(8,128)(2,1)S(1)}, u32[]{:S(2)}, u32[]{:S(2)}) collective-permute-start(bf16[128,1024]{1,0:T(8,128)(2,1)S(1)} %copy-done.63), channel_id=1, source_target_pairs={{0,96},{16,112},{32,64},{48,80},{64,32},{80,48},{96,0},{112,16},{1... | collective-permute-start | bytes 786440 | tf_op jit(solution)/shard_map/ppermute | solution.py:49
  141.4 6.4 %collective-permute-start.21 = (bf16[128,1024]{1,0:T(8,128)(2,1)S(1)}, bf16[128,1024]{1,0:T(8,128)(2,1)S(1)}, u32[]{:S(2)}, u32[]{:S(2)}) collective-permute-start(bf16[128,1024]{1,0:T(8,128)(2,1)S(1)} %copy-done.62), channel_id=1, source_target_pairs={{0,32},{16,48},{32,0},{48,16},{64,96},{80,112},{96,64},{112,80},{1... | collective-permute-start | bytes 786440 | tf_op jit(solution)/shard_map/ppermute | solution.py:49
  147.8 6.3 %collective-permute-start.23 = (bf16[64,1024]{1,0:T(8,128)(2,1)S(1)}, bf16[64,1024]{1,0:T(8,128)(2,1)S(1)}, u32[]{:S(2)}, u32[]{:S(2)}) collective-permute-start(bf16[64,1024]{1,0:T(8,128)(2,1)S(1)} %get-tuple-element.149), channel_id=1, source_target_pairs={{0,96},{16,112},{32,64},{48,80},{64,32},{80,48},{96,0},{112,16},{1... | collective-permute-start | bytes 393224 | tf_op jit(solution)/shard_map/ppermute | solution.py:49
  149.3 5.0 %collective-permute-start.22 = (bf16[64,1024]{1,0:T(8,128)(2,1)S(1)}, bf16[64,1024]{1,0:T(8,128)(2,1)S(1)}, u32[]{:S(2)}, u32[]{:S(2)}) collective-permute-start(bf16[64,1024]{1,0:T(8,128)(2,1)S(1)} %get-tuple-element.150), channel_id=1, source_target_pairs={{0,32},{16,48},{32,0},{48,16},{64,96},{80,112},{96,64},{112,80},{1... | collective-permute-start | bytes 393224 | tf_op jit(solution)/shard_map/ppermute | solution.py:49
  161.9 15.5 %collective-permute-start.28 = (bf16[64,1024]{1,0:T(8,128)(2,1)}, bf16[64,1024]{1,0:T(8,128)(2,1)S(1)}, u32[]{:S(2)}, u32[]{:S(2)}) collective-permute-start(bf16[64,1024]{1,0:T(8,128)(2,1)} %get-tuple-element.102.refs_4_), channel_id=1, source_target_pairs={{0,32},{16,48},{32,0},{48,16},{64,96},{80,112},{96,64},{112,80},{1... | collective-permute-start | bytes 393224 | tf_op jit(solution)/shard_map/ppermute | solution.py:49
  162.0 23.1 %all-to-all-start.1 = ((bf16[8,128,256]{2,1,0:T(8,128)(2,1)}), bf16[8,128,256]{2,1,0:T(8,128)(2,1)S(1)}, u32[]{:S(2)}, u32[]{:S(2)}) async-start(bf16[8,128,256]{2,1,0:T(8,128)(2,1)} %get-tuple-element.109), calls=%async_computation.1 | async-start | bytes 1048576 | tf_op jit(solution)/shard_map/all_to_all | solution.py:684
  167.5 8.0 %collective-permute-start.30 = (bf16[64,1024]{1,0:T(8,128)(2,1)}, bf16[64,1024]{1,0:T(8,128)(2,1)S(1)}, u32[]{:S(2)}, u32[]{:S(2)}) collective-permute-start(bf16[64,1024]{1,0:T(8,128)(2,1)} %get-tuple-element.114.refs_7_), channel_id=1, source_target_pairs={{0,96},{16,112},{32,64},{48,80},{64,32},{80,48},{96,0},{112,16},{1... | collective-permute-start | bytes 393224 | tf_op jit(solution)/shard_map/ppermute | solution.py:49
  170.8 9.5 %collective-permute-start.24 = (bf16[128,1024]{1,0:T(8,128)(2,1)S(1)}, bf16[128,1024]{1,0:T(8,128)(2,1)S(1)}, u32[]{:S(2)}, u32[]{:S(2)}) collective-permute-start(bf16[128,1024]{1,0:T(8,128)(2,1)S(1)} %copy-done.58), channel_id=1, source_target_pairs={{0,96},{16,112},{32,64},{48,80},{64,32},{80,48},{96,0},{112,16},{1... | collective-permute-start | bytes 786440 | tf_op jit(solution)/shard_map/ppermute | solution.py:49
  171.1 9.9 %collective-permute-start.26 = (bf16[128,1024]{1,0:T(8,128)(2,1)S(1)}, bf16[128,1024]{1,0:T(8,128)(2,1)}, u32[]{:S(2)}, u32[]{:S(2)}) collective-permute-start(bf16[128,1024]{1,0:T(8,128)(2,1)S(1)} %copy-done.57), channel_id=1, source_target_pairs={{0,32},{16,48},{32,0},{48,16},{64,96},{80,112},{96,64},{112,80},{1... | collective-permute-start | bytes 786440 | tf_op jit(solution)/shard_map/ppermute | solution.py:49
  172.6 26.7 %collective-permute-start.32 = (bf16[512,256]{1,0:T(8,128)(2,1)S(1)}, bf16[512,256]{1,0:T(8,128)(2,1)S(1)}, u32[]{:S(2)}, u32[]{:S(2)}) collective-permute-start(bf16[512,256]{1,0:T(8,128)(2,1)S(1)} %bitcast.53), channel_id=1, source_target_pairs={{0,16},{16,0},{32,48},{48,32},{64,80},{80,64},{96,112},{112,96},{1... | collective-permute-start | bytes 786440 | tf_op jit(solution)/shard_map/ppermute | solution.py:49
  175.6 23.7 %copy-start.45 = (bf16[64,1024]{1,0:T(8,128)(2,1)}, bf16[64,1024]{1,0:T(8,128)(2,1)S(1)}, u32[]{:S(2)}) copy-start(bf16[64,1024]{1,0:T(8,128)(2,1)S(1)} %collective-permute-done.30.refs_8_) | copy-start | bytes 393220
  175.6 23.7 %collective-permute-start.31 = (bf16[128,1024]{1,0:T(8,128)(2,1)S(1)}, bf16[128,1024]{1,0:T(8,128)(2,1)S(1)}, u32[]{:S(2)}, u32[]{:S(2)}) collective-permute-start(bf16[128,1024]{1,0:T(8,128)(2,1)S(1)} %pad_maximum_fusion.17), channel_id=1, source_target_pairs={{0,32},{16,48},{32,0},{48,16},{64,96},{80,112},{96,64},{112,80},{1... | collective-permute-start | bytes 786440 | tf_op jit(solution)/shard_map/ppermute | solution.py:49
  177.5 21.8 %copy-start.44 = (bf16[64,1024]{1,0:T(8,128)(2,1)}, bf16[64,1024]{1,0:T(8,128)(2,1)S(1)}, u32[]{:S(2)}) copy-start(bf16[64,1024]{1,0:T(8,128)(2,1)S(1)} %collective-permute-done.28.refs_5_) | copy-start | bytes 393220
  177.5 21.9 %collective-permute-start.29 = (bf16[128,1024]{1,0:T(8,128)(2,1)S(1)}, bf16[128,1024]{1,0:T(8,128)(2,1)S(1)}, u32[]{:S(2)}, u32[]{:S(2)}) collective-permute-start(bf16[128,1024]{1,0:T(8,128)(2,1)S(1)} %pad_maximum_fusion.16), channel_id=1, source_target_pairs={{0,96},{16,112},{32,64},{48,80},{64,32},{80,48},{96,0},{112,16},{1... | collective-permute-start | bytes 786440 | tf_op jit(solution)/shard_map/ppermute | solution.py:49
  207.2 3.4 %collective-permute-start.33 = (bf16[512,1152]{1,0:T(8,128)(2,1)}, bf16[512,1152]{1,0:T(8,128)(2,1)S(1)}, u32[]{:S(2)}, u32[]{:S(2)}) collective-permute-start(bf16[512,1152]{1,0:T(8,128)(2,1)} %bitcast.59), channel_id=1, source_target_pairs={{0,1},{1,0},{2,3},{3,2},{4,5},{5,4},{6,7},{7,6},{8,9},{9,8},{10,11... | collective-permute-start | bytes 3538952 | tf_op jit(solution)/shard_map/ppermute | solution.py:49
  210.6 25.0 %copy-start.10 = (bf16[512,1152]{1,0:T(8,128)(2,1)}, bf16[512,1152]{1,0:T(8,128)(2,1)S(1)}, u32[]{:S(2)}) copy-start(bf16[512,1152]{1,0:T(8,128)(2,1)S(1)} %collective-permute-done.33) | copy-start | bytes 3538948
  212.4 9.1 %collective-permute-start.36 = (bf16[128,1152]{1,0:T(8,128)(2,1)S(1)}, bf16[128,1152]{1,0:T(8,128)(2,1)S(1)}, u32[]{:S(2)}, u32[]{:S(2)}) collective-permute-start(bf16[128,1152]{1,0:T(8,128)(2,1)S(1)} %pad_maximum_fusion.9), channel_id=1, source_target_pairs={{0,4},{1,5},{2,6},{3,7},{4,0},{5,1},{6,2},{7,3},{8,12},{9,13},{10,... | collective-permute-start | bytes 884744 | tf_op jit(solution)/shard_map/ppermute | solution.py:49
  212.9 21.6 %copy-start.3 = (bf16[1,128,1024]{2,1,0:T(8,128)(2,1)S(1)}, bf16[1,128,1024]{2,1,0:T(8,128)(2,1)}, u32[]{:S(2)}) copy-start(bf16[1,128,1024]{2,1,0:T(8,128)(2,1)} %param.15) | copy-start | bytes 786436
  212.9 10.1 %collective-permute-start.34 = (bf16[128,1152]{1,0:T(8,128)(2,1)S(1)}, bf16[128,1152]{1,0:T(8,128)(2,1)S(1)}, u32[]{:S(2)}, u32[]{:S(2)}) collective-permute-start(bf16[128,1152]{1,0:T(8,128)(2,1)S(1)} %pad_maximum_fusion.8), channel_id=1, source_target_pairs={{0,12},{1,13},{2,14},{3,15},{4,8},{5,9},{6,10},{7,11},{8,4},{9,5},... | collective-permute-start | bytes 884744 | tf_op jit(solution)/shard_map/ppermute | solution.py:49
  223.8 6.4 %collective-permute-start.37 = (bf16[64,1152]{1,0:T(8,128)(2,1)S(1)}, bf16[64,1152]{1,0:T(8,128)(2,1)S(1)}, u32[]{:S(2)}, u32[]{:S(2)}) collective-permute-start(bf16[64,1152]{1,0:T(8,128)(2,1)S(1)} %get-tuple-element.138), channel_id=1, source_target_pairs={{0,12},{1,13},{2,14},{3,15},{4,8},{5,9},{6,10},{7,11},{8,4},{9,5},... | collective-permute-start | bytes 442376 | tf_op jit(solution)/shard_map/ppermute | solution.py:49
  226.3 9.3 %collective-permute-start.35 = (bf16[64,1152]{1,0:T(8,128)(2,1)}, bf16[64,1152]{1,0:T(8,128)(2,1)}, u32[]{:S(2)}, u32[]{:S(2)}) collective-permute-start(bf16[64,1152]{1,0:T(8,128)(2,1)} %get-tuple-element.137), channel_id=1, source_target_pairs={{0,4},{1,5},{2,6},{3,7},{4,0},{5,1},{6,2},{7,3},{8,12},{9,13},{10,... | collective-permute-start | bytes 442376 | tf_op jit(solution)/shard_map/ppermute | solution.py:49
  230.9 5.6 %collective-permute-start.38 = (bf16[64,1152]{1,0:T(8,128)(2,1)}, bf16[64,1152]{1,0:T(8,128)(2,1)}, u32[]{:S(2)}, u32[]{:S(2)}) collective-permute-start(bf16[64,1152]{1,0:T(8,128)(2,1)} %add_convert_fusion.5), channel_id=1, source_target_pairs={{0,2},{1,3},{2,0},{3,1},{4,6},{5,7},{6,4},{7,5},{8,10},{9,11},{10,... | collective-permute-start | bytes 442376 | tf_op jit(solution)/shard_map/ppermute | solution.py:49
  234.6 13.3 %collective-permute-start.44 = (bf16[256,1024]{1,0:T(8,128)(2,1)}, bf16[256,1024]{1,0:T(8,128)(2,1)}, u32[]{:S(2)}, u32[]{:S(2)}) collective-permute-start(bf16[256,1024]{1,0:T(8,128)(2,1)} %get-tuple-element.125), channel_id=1, source_target_pairs={{0,96},{16,112},{32,64},{48,80},{64,32},{80,48},{96,0},{112,16},{1... | collective-permute-start | bytes 1572872 | tf_op jit(solution)/shard_map/ppermute | solution.py:49
  235.6 12.3 %collective-permute-start.46 = (bf16[256,1024]{1,0:T(8,128)(2,1)}, bf16[256,1024]{1,0:T(8,128)(2,1)}, u32[]{:S(2)}, u32[]{:S(2)}) collective-permute-start(bf16[256,1024]{1,0:T(8,128)(2,1)} %get-tuple-element.126), channel_id=1, source_target_pairs={{0,32},{16,48},{32,0},{48,16},{64,96},{80,112},{96,64},{112,80},{1... | collective-permute-start | bytes 1572872 | tf_op jit(solution)/shard_map/ppermute | solution.py:49
  240.3 11.1 %collective-permute-start.39 = (bf16[192,1152]{1,0:T(8,128)(2,1)S(1)}, bf16[192,1152]{1,0:T(8,128)(2,1)S(1)}, u32[]{:S(2)}, u32[]{:S(2)}) collective-permute-start(bf16[192,1152]{1,0:T(8,128)(2,1)S(1)} %pad_maximum_fusion.5), channel_id=1, source_target_pairs={{0,16},{16,0},{32,48},{48,32},{64,80},{80,64},{96,112},{112,96},{1... | collective-permute-start | bytes 1327112 | tf_op jit(solution)/shard_map/ppermute | solution.py:49
  249.1 9.7 %collective-permute-start.47 = (bf16[128,1024]{1,0:T(8,128)(2,1)S(1)}, bf16[128,1024]{1,0:T(8,128)(2,1)S(1)}, u32[]{:S(2)}, u32[]{:S(2)}) collective-permute-start(bf16[128,1024]{1,0:T(8,128)(2,1)S(1)} %get-tuple-element.144), channel_id=1, source_target_pairs={{0,96},{16,112},{32,64},{48,80},{64,32},{80,48},{96,0},{112,16},{1... | collective-permute-start | bytes 786440 | tf_op jit(solution)/shard_map/ppermute | solution.py:49
  251.7 10.2 %collective-permute-start.40 = (bf16[128,1152]{1,0:T(8,128)(2,1)S(1)}, bf16[128,1152]{1,0:T(8,128)(2,1)S(1)}, u32[]{:S(2)}, u32[]{:S(2)}) collective-permute-start(bf16[128,1152]{1,0:T(8,128)(2,1)S(1)} %pad_maximum_fusion.10.refs_1_), channel_id=1, source_target_pairs={{0,32},{16,48},{32,0},{48,16},{64,96},{80,112},{96,64},{112,80},{1... | collective-permute-start | bytes 884744 | tf_op jit(solution)/shard_map/ppermute | solution.py:49
  253.9 19.2 %collective-permute-start.27 = (bf16[64,1024]{1,0:T(8,128)(2,1)S(1)}, bf16[64,1024]{1,0:T(8,128)(2,1)S(1)}, u32[]{:S(2)}, u32[]{:S(2)}) collective-permute-start(bf16[64,1024]{1,0:T(8,128)(2,1)S(1)} %get-tuple-element.147), channel_id=1, source_target_pairs={{0,96},{16,112},{32,64},{48,80},{64,32},{80,48},{96,0},{112,16},{1... | collective-permute-start | bytes 393224 | tf_op jit(solution)/shard_map/ppermute | solution.py:49
  256.1 17.0 %collective-permute-start.25 = (bf16[64,1024]{1,0:T(8,128)(2,1)S(1)}, bf16[64,1024]{1,0:T(8,128)(2,1)S(1)}, u32[]{:S(2)}, u32[]{:S(2)}) collective-permute-start(bf16[64,1024]{1,0:T(8,128)(2,1)S(1)} %get-tuple-element.148), channel_id=1, source_target_pairs={{0,32},{16,48},{32,0},{48,16},{64,96},{80,112},{96,64},{112,80},{1... | collective-permute-start | bytes 393224 | tf_op jit(solution)/shard_map/ppermute | solution.py:49
  256.8 12.6 %collective-permute-start.45 = (bf16[128,1024]{1,0:T(8,128)(2,1)S(1)}, bf16[128,1024]{1,0:T(8,128)(2,1)S(1)}, u32[]{:S(2)}, u32[]{:S(2)}) collective-permute-start(bf16[128,1024]{1,0:T(8,128)(2,1)S(1)} %get-tuple-element.143), channel_id=1, source_target_pairs={{0,32},{16,48},{32,0},{48,16},{64,96},{80,112},{96,64},{112,80},{1... | collective-permute-start | bytes 786440 | tf_op jit(solution)/shard_map/ppermute | solution.py:49
  258.8 8.3 %collective-permute-start.42 = (bf16[128,1152]{1,0:T(8,128)(2,1)S(1)}, bf16[128,1152]{1,0:T(8,128)(2,1)S(1)}, u32[]{:S(2)}, u32[]{:S(2)}) collective-permute-start(bf16[128,1152]{1,0:T(8,128)(2,1)S(1)} %pad_maximum_fusion.11.refs_4_), channel_id=1, source_target_pairs={{0,96},{16,112},{32,64},{48,80},{64,32},{80,48},{96,0},{112,16},{1... | collective-permute-start | bytes 884744 | tf_op jit(solution)/shard_map/ppermute | solution.py:49
  261.9 8.0 %collective-permute-start.48 = (bf16[128,1024]{1,0:T(8,128)(2,1)S(1)}, bf16[128,1024]{1,0:T(8,128)(2,1)S(1)}, u32[]{:S(2)}, u32[]{:S(2)}) collective-permute-start(bf16[128,1024]{1,0:T(8,128)(2,1)S(1)} %add_convert_fusion.1), channel_id=1, source_target_pairs={{0,16},{16,0},{32,48},{48,32},{64,80},{80,64},{96,112},{112,96},{1... | collective-permute-start | bytes 786440 | tf_op jit(solution)/shard_map/ppermute | solution.py:49
  267.1 12.3 %collective-permute-start.41 = (bf16[256,1152]{1,0:T(8,128)(2,1)S(1)}, bf16[256,1152]{1,0:T(8,128)(2,1)S(1)}, u32[]{:S(2)}, u32[]{:S(2)}) collective-permute-start(bf16[256,1152]{1,0:T(8,128)(2,1)S(1)} %pad_maximum_fusion), channel_id=1, source_target_pairs={{0,96},{16,112},{32,64},{48,80},{64,32},{80,48},{96,0},{112,16},{1... | collective-permute-start | bytes 1769480 | tf_op jit(solution)/shard_map/ppermute | solution.py:49
  269.4 10.8 %collective-permute-start.43 = (bf16[256,1152]{1,0:T(8,128)(2,1)S(1)}, bf16[256,1152]{1,0:T(8,128)(2,1)}, u32[]{:S(2)}, u32[]{:S(2)}) collective-permute-start(bf16[256,1152]{1,0:T(8,128)(2,1)S(1)} %pad_maximum_fusion.1), channel_id=1, source_target_pairs={{0,32},{16,48},{32,0},{48,16},{64,96},{80,112},{96,64},{112,80},{1... | collective-permute-start | bytes 1769480 | tf_op jit(solution)/shard_map/ppermute | solution.py:49
  (54 other events, 383.3 us)
Sparse Core Ops, SparseCore 0:
  11.2 70.1 all-gather.1
  138.8 73.7 reduce-scatter.1

commit v2 on v1

--- a/solution.py
+++ b/solution.py
@@ -26,6 +26,17 @@
 MEGA = 1 << 20
 GRANT = 60
 
+TOKEN_PIECES = (
+    (0, 0, 0, 0),
+    (3, 0, 0, 1),
+    (1, 0, 1, 0),
+    (2, 0, 3, 0),
+    (2, 1, 2, 0),
+    (4, 0, 1, 1),
+    (5, 0, 3, 1),
+    (6, 0, 2, 1),
+)
+
 EPSILON = 1e-06
 THETA = 1000000.0
 NEGATIVE = -1e30
@@ -41,7 +52,6 @@
     (5, 0, 1, 1),
     (5, 1, 2, 1),
 )
-KEPT = ((0, 0), (1, 0), (0, 1), (3, 1))
 
 
 def exchange(values, axis, bits):
@@ -52,9 +62,18 @@
 swap_x_hi = functools.partial(exchange, axis="seq", bits=1)
 swap_z_a = functools.partial(exchange, axis="seq", bits=2)
 swap_z_b = functools.partial(exchange, axis="seq", bits=6)
+swap_z_both = functools.partial(exchange, axis="seq", bits=4)
 swap_core = functools.partial(exchange, axis="fsdp", bits=1)
 swap_x_lo = functools.partial(exchange, axis="fsdp", bits=2)
 swap_chip = functools.partial(exchange, axis="fsdp", bits=3)
+
+
+def swap_x_both(values):
+    places = [(i, j) for i in range(N_SEQ) for j in range(N_FSDP)]
+    pairs = [(i * N_FSDP + j, (i ^ 1) * N_FSDP + (j ^ 2)) for i, j in places]
+    return lax.ppermute(values, ("seq", "fsdp"), pairs)
+
+
 swap_y_a = functools.partial(exchange, axis="fsdp", bits=4)
 swap_y_b = functools.partial(exchange, axis="fsdp", bits=12)
 
@@ -76,20 +95,19 @@
     return rows[:middle], rows[middle:]
 
 
-def scatter4(first_0, first_1, block, swap_a, swap_b, between=None):
+def scatter4(first_0, first_1, passed_0, passed_1, swap_a, swap_b, tie=None):
     got_0, got_1 = swap_b(first_0), swap_a(first_1)
-    if between is not None:
-        got_0, got_1 = after((got_0, got_1), between)
+    if tie is not None:
+        got_0, got_1 = tie(got_0, got_1)
     n = got_0.shape[0] // 2
-    last_0 = swap_a((block(1, 0) + got_0[n:].astype(jnp.float32)).astype(jnp.bfloat16))
-    last_1 = swap_b((block(3, 1) + got_1[n:].astype(jnp.float32)).astype(jnp.bfloat16))
-    return got_0, got_1, last_0, last_1
-
-
-def total4(block, got_0, got_1, last_0, last_1):
-    n = got_0.shape[0] // 2
-    mine_0 = block(0, 0) + got_0[:n].astype(jnp.float32) + last_0.astype(jnp.float32)
-    mine_1 = block(0, 1) + got_1[:n].astype(jnp.float32) + last_1.astype(jnp.float32)
+    last_0 = swap_a((passed_0 + got_0[n:].astype(jnp.float32)).astype(jnp.bfloat16))
+    last_1 = swap_b((passed_1 + got_1[n:].astype(jnp.float32)).astype(jnp.bfloat16))
+    return got_0[:n], got_1[:n], last_0, last_1
+
+
+def total4(own_0, own_1, got_0, got_1, last_0, last_1):
+    mine_0 = own_0 + got_0.astype(jnp.float32) + last_0.astype(jnp.float32)
+    mine_1 = own_1 + got_1.astype(jnp.float32) + last_1.astype(jnp.float32)
     return mine_0, mine_1
 
 
@@ -137,11 +155,11 @@
 
 
 def front_kernel(
-    at, x0, x1, x2, x3, x4, x5, w0, w1, w2, w3, w4, w5, first_key, table,
-    normed, raw, heads, mixed, turned, log_total, gains, weight, value_t,
+    at, w0, w1, w2, w3, w4, w5, x0, x1, x2, x3, x4, x5, x6, table, first_key,
+    turned, normed, raw, heads, mixed, log_total, gains, weight, value_t, arrived,
 ):
     z, x_hi, y, x_lo, core = at[0], at[1], at[2], at[3], at[4]
-    weights, tokens = (w0, w1, w2, w3, w4, w5), (x0, x1, x2, x3, x4, x5)
+    weights, tokens = (w0, w1, w2, w3, w4, w5), (x0, x1, x2, x3, x4, x5, x6)
     extra = jnp.zeros((EXTRA, UNIT), jnp.float32)
     for array, step, relative, color in PIECES:
         for other in range(2):
@@ -156,7 +174,7 @@
     gains[0:1, :] = gain
     gains[1:2, :] = jnp.concatenate([extra[2:3], extra[3:4]], axis=1)
     gains[2:3, 0:UNIT] = extra[4:5]
-    for array, step, relative, color in PIECES:
+    for array, step, relative, color in TOKEN_PIECES:
         values = tokens[array][step * ROWS : (step + 1) * ROWS, :].astype(jnp.float32)
         place = (2 * (z ^ relative) + (x_hi ^ color)) * ROWS
         normed[pl.ds(pl.multiple_of(place, ROWS), ROWS), :] = (
@@ -198,17 +216,23 @@
                     value_t[:, first : first + s.shape[0]], weights_now.astype(jnp.bfloat16)
                 )
             log_total[head : head + 1, rows] = highest + jnp.log(total)
-            result = (result / total).T.astype(jnp.bfloat16)
-            mixed[rows, columns] = result
-            for part in range(2):
-                turned[part ^ x_hi, (begin // BLOCK) ^ z, :, columns] = result[
-                    part * ROWS : (part + 1) * ROWS
-                ]
+            mixed[rows, columns] = (result / total).T.astype(jnp.bfloat16)
+        mixed.send(rows)
+        for part in range(2):
+            i = begin // ROWS + part
+            goal = turned.at[part ^ x_hi, (begin // BLOCK) ^ z]
+            copy = pltpu.make_async_copy(
+                mixed.place.at[i * ROWS : (i + 1) * ROWS], goal, arrived.at[i]
+            )
+            copy.start()
+            mixed.copies.append(copy)
 
 
 def back_kernel(
-    at, raw, heads, log_total, grad, first_key, table, gains, weight,
-    back, gain_grads, first_0, first_1, keep, key_t, key_sum, value_sum, query_sum, turned,
+    at, heads, grad, first_key, log_total, raw, table, gains, weight,
+    normed, mixed_mine, mixed_other, p0, p1, p2, p3, p4, p5,
+    mine, theirs, first_0, first_1, passed, own, back, key_t, key_sum, value_sum, query_sum,
+    gain_grads, proj, mixed, share, turned, done,
 ):
     key, value = slice(2 * HEAD, 3 * HEAD), slice(3 * HEAD, 4 * HEAD)
     key_t[...] = heads[:, key].astype(jnp.float32).T.astype(jnp.bfloat16)
@@ -256,20 +280,15 @@
             mean = jnp.mean(unit * pulled, axis=-1, keepdims=True)
             back[rows, columns] = (inverse * (pulled - unit * mean)).astype(jnp.bfloat16)
 
-    back.send()
     z, x_hi = at[0], at[1]
     for relative in range(Z):
         for color in range(2):
             place = (2 * (z ^ relative) + (x_hi ^ color)) * ROWS
             begin = (2 * relative + color) * ROWS
             turned[begin : begin + ROWS, :] = back[pl.ds(pl.multiple_of(place, ROWS), ROWS), :]
-    send_order(contract(turned[...], weight[...]), first_0, first_1, keep)
-
-
-def grad_kernel(
-    at, normed, back, gain_grads, p0, p1, p2, p3, p4, p5, mixed_mine, mixed_other,
-    mine, theirs, share, proj, mixed, done,
-):
+    send_order(contract(turned[...], weight[...]), first_0, first_1, passed, own)
+    for values in (first_0, first_1, passed, own):
+        values.send()
     y, x_lo, core = at[2], at[3], at[4]
     ordered((p0, p1, p2, p3, p4, p5), proj)
     mixed[:, : 2 * HEAD] = mixed_mine[...]
@@ -313,14 +332,13 @@
 
 
 def mid_kernel(
-    keep, got_0, got_1, last_0, last_1, hidden, incoming, gains, later,
+    own, got_0, got_1, last_0, last_1, hidden, incoming, gains, later,
     hidden_grad, upper, lower, mixed_grad, weights, arrived,
 ):
     parts = fetch(later, weights, arrived, [(i * 2 * HEAD, 2 * HEAD) for i in range(N_SEQ)])
     half = ROWS // 2
-    total_0 = keep[:half, :] + got_0[:half, :].astype(jnp.float32) + last_0[...].astype(jnp.float32)
-    total_1 = keep[2 * half : 3 * half, :] + got_1[:half, :].astype(jnp.float32)
-    total_1 = total_1 + last_1[...].astype(jnp.float32)
+    total_0 = own[:half, :] + got_0[...].astype(jnp.float32) + last_0[...].astype(jnp.float32)
+    total_1 = own[half:, :] + got_1[...].astype(jnp.float32) + last_1[...].astype(jnp.float32)
     pulled = jnp.concatenate([total_0, total_1], axis=0) * gains[1:2, :]
     inverse = inverse_norm(hidden[...])
     unit = hidden[...] * inverse
@@ -341,7 +359,7 @@
         place[begin : begin + half, :] = pieces[array][step * half : (step + 1) * half, :]
 
 
-def send_order(values, first_0, first_1, keep):
+def send_order(values, first_0, first_1, passed, own):
     half = values.shape[0] // 8
 
     def block(relative, color):
@@ -352,23 +370,16 @@
     first_0[half:, :] = block(2, 0).astype(jnp.bfloat16)
     first_1[:half, :] = block(1, 1).astype(jnp.bfloat16)
     first_1[half:, :] = block(2, 1).astype(jnp.bfloat16)
-    for i, (relative, color) in enumerate(KEPT):
-        keep[i * half : (i + 1) * half, :] = block(relative, color)
-
-
-def kept(values):
-    half = values.shape[0] // 4
-
-    def block(relative, color):
-        i = KEPT.index((relative, color))
-        return values[i * half : (i + 1) * half]
-
-    return block
+    passed[:half, :] = block(1, 0)
+    passed[half:, :] = block(3, 1)
+    own[:half, :] = block(0, 0)
+    own[half:, :] = block(0, 1)
 
 
 def mlp_kernel(
     n0, n1, n2, n3, n4, n5, c0, c1, c2, c3, c4, c5, later,
-    rows, incoming, both_grad, inner, first_0, first_1, keep, weights, arrived,
+    first_0, first_1, passed, own, share, down_0, down_1, down_passed, down_own,
+    weights, arrived, rows, incoming, both_grad, inner,
 ):
     steps = range(0, FF_Z, BLOCK)
     parts = fetch(
@@ -377,8 +388,6 @@
     )
     ordered((n0, n1, n2, n3, n4, n5), rows)
     ordered((c0, c1, c2, c3, c4, c5), incoming)
-    rows.send()
-    incoming.send()
     for i, begin in enumerate(steps):
         columns, second = slice(begin, begin + BLOCK), slice(FF_Z + begin, FF_Z + begin + BLOCK)
         gate = product(rows[...], parts[3 * i]()[...])
@@ -391,32 +400,55 @@
             inner_grad * up * sigmoid * (1.0 + gate * (1.0 - sigmoid))
         ).astype(jnp.bfloat16)
         both_grad[:, second] = (inner_grad * swish).astype(jnp.bfloat16)
-    send_order(contract(both_grad[...], weights[:, : 2 * FF_Z]), first_0, first_1, keep)
-
-
-def mlp_grad_kernel(
-    rows, incoming, both_grad, inner, later,
-    share, first_0, first_1, keep, weights, arrived,
-):
-    whole = fetch(later, weights, arrived, [(0, FF_Z)], 2 * D + 2 * FF_Z)
+    send_order(contract(both_grad[...], weights[:, : 2 * FF_Z]), first_0, first_1, passed, own)
+    for values in (first_0, first_1, passed, own):
+        values.send()
     for begin in range(0, D, BLOCK):
         goal = slice(begin, begin + BLOCK)
         share[goal, : 2 * FF_Z] = outer_rows(rows[:, goal], both_grad[...]).astype(jnp.bfloat16)
         share[goal, 2 * FF_Z :] = outer_rows(incoming[:, goal], inner[...]).astype(jnp.bfloat16)
         share.send(goal)
-    send_order(contract(inner[...], whole[0]()[...]), first_0, first_1, keep)
-
-
-def last_kernel(
-    at, p0, p1, p2, p3, p4, p5, w_gate, w_up, w_query, w_key, w_value, norm_post, norm_input,
-    gate, up, down_t, query, key, value, output_t, post_grad, input_grad, gain_grads,
+    send_order(
+        contract(inner[...], weights[:, 2 * FF_Z :]), down_0, down_1, down_passed, down_own
+    )
+
+
+def weighed(*pairs):
+    return functools.reduce(
+        jnp.add,
+        [
+            jnp.sum(grad[...] * weight[...].astype(jnp.float32), axis=1, keepdims=True)
+            for grad, weight in pairs
+        ],
+    )
+
+
+def as_row(column):
+    return jnp.broadcast_to(column, (OWN, HEAD)).T[0:1, :]
+
+
+def last_mlp_kernel(mlp, w_gate, w_up, norm, gate, up, down_t, norm_grad):
+    for place in range(Z):
+        part = mlp[2 * place].astype(jnp.float32) + mlp[2 * place + 1].astype(jnp.float32)
+        columns = slice(place * FF_Z, (place + 1) * FF_Z)
+        gate[:, columns] = part[:, :FF_Z]
+        up[:, columns] = part[:, FF_Z : 2 * FF_Z]
+        down_t[:, columns] = part[:, 2 * FF_Z :]
+    for result in (gate, up, down_t):
+        result.send()
+    norm_grad[...] = as_row(weighed((gate, w_gate), (up, w_up)) / norm[...])
+
+
+def last_attn_kernel(
+    at, p0, p1, p2, p3, p4, p5, w_query, w_key, w_value, norm,
+    query, key, value, output_t, norm_grad, query_gain, key_gain,
 ):
     z, x_hi = at[0], at[1]
     pieces = (p0, p1, p2, p3, p4, p5)
-    half, middle = OWN // 2, SHARE - FF_Z
+    each = HEAD // N_FSDP
     gain_total = jnp.zeros((8, HEAD), jnp.float32)
     for array, step, relative, color in PIECES:
-        begin = 2 * step * OWN
+        begin = step * OWN
         part = pieces[array][begin : begin + OWN, :].astype(jnp.float32)
         place, theirs = z ^ relative, x_hi ^ color
         head = 2 * place + theirs
@@ -432,30 +464,11 @@
             share = part[:, first : first + 2 * HEAD]
             output_t[:, goal] = share if color == 0 else output_t[:, goal] + share
         gain_total += part[0:8, 2 * UNIT :]
-        left = pieces[array][begin + OWN : begin + OWN + half, :].astype(jnp.float32)
-        right = pieces[array][begin + OWN + half : begin + 2 * OWN, :].astype(jnp.float32)
-        rows = slice(color * half, (color + 1) * half)
-        start = place * FF_Z
-        columns = pl.ds(pl.multiple_of(start, FF_Z), FF_Z)
-        gate[rows, columns] = left[:, :FF_Z]
-        up[rows, pl.ds(pl.multiple_of(start, FF_Z), middle)] = left[:, FF_Z:]
-        up[rows, pl.ds(pl.multiple_of(start + middle, middle), middle)] = right[:, :middle]
-        down_t[rows, columns] = right[:, middle:]
-    for result in (gate, up, down_t, query, key, value, output_t):
+    for result in (query, key, value, output_t):
         result.send()
-    gain_grads[...] = gain_total
-
-    def paired(*pairs):
-        return functools.reduce(
-            jnp.add,
-            [
-                jnp.sum(grad[...] * weight[...].astype(jnp.float32), axis=1, keepdims=True)
-                for grad, weight in pairs
-            ],
-        )
-
-    post_grad[...] = paired((gate, w_gate), (up, w_up)) / norm_post[...]
-    input_grad[...] = paired((query, w_query), (key, w_key), (value, w_value)) / norm_input[...]
+    query_gain[...] = gain_total[0:1, :each]
+    key_gain[...] = gain_total[0:1, each : 2 * each]
+    norm_grad[...] = as_row(weighed((query, w_query), (key, w_key), (value, w_value)) / norm[...])
 
 
 class Reading:
@@ -499,7 +512,7 @@
     return result
 
 
-def kernel_call(kernel, inputs, outs, limit, scratch=(), flops=0, raw=(), raw_outs=0):
+def kernel_call(kernel, inputs, outs, scratch=(), flops=0, raw=(), raw_outs=0):
     modes = ["scalar" if x.ndim == 1 else "raw" if i in raw else "copy" for i, x in enumerate(inputs)]
     n_in, n_out = len(inputs), len(outs)
     buffers = [pltpu.VMEM(x.shape, x.dtype) for x, m in zip(inputs, modes) if m == "copy"]
@@ -573,7 +586,7 @@
     ids = segments[0]
     first_key = jnp.sum((ids[None, :] < ids[:, None]).astype(jnp.int32), axis=1).reshape(1, LENGTH)
 
-    token_pieces = gather4(sequence, swap_x_hi(sequence), swap_z_a, swap_z_b)
+    other_rows = swap_x_hi(sequence)
 
     def spread(values):
         wide = jnp.tile(values, N_FSDP)
@@ -595,7 +608,22 @@
     pair = jnp.concatenate([piece, swap_core(piece)], axis=0)
     other_pair = jnp.concatenate([swap_x_lo(piece), swap_chip(piece)], axis=0)
     pair, other_pair = lax.optimization_barrier((pair, other_pair))
-    unit_pieces = gather4(pair, other_pair, swap_y_a, swap_y_b)
+    pair_1, other_pair_1 = swap_y_a(pair), swap_y_b(other_pair)
+
+    pair_2 = swap_y_b(jnp.concatenate([pair, pair_1], axis=0))
+    other_pair_2 = swap_y_a(jnp.concatenate([other_pair, other_pair_1], axis=0))
+    unit_pieces = (pair, pair_1, pair_2, other_pair, other_pair_1, other_pair_2)
+    rows_1 = swap_z_a(sequence)
+    rows_2 = swap_z_b(jnp.concatenate([sequence, rows_1], axis=0))
+    token_pieces = (
+        sequence,
+        rows_1,
+        rows_2,
+        other_rows,
+        swap_z_a(other_rows),
+        swap_z_b(other_rows),
+        swap_z_both(other_rows),
+    )
 
     def slice_z(values):
         return lax.dynamic_slice_in_dim(values, z * FF_Z, FF_Z, 1)
@@ -605,122 +633,112 @@
     )
     later = lax.all_gather(later, "fsdp", axis=0, tiled=True)
 
-    incoming = after(cotangent[0], (token_pieces[1], token_pieces[4]))
-    cotangent_z = gather4(*halves(incoming), swap_z_a, swap_z_b)
-    token_pieces = after(token_pieces, cotangent_z)
-
-    normed, raw, heads, mixed, turned, log_total, gains, weight = kernel_call(
+    turned, normed, raw, heads, mixed, log_total, gains, weight = kernel_call(
         front_kernel,
-        (at, *token_pieces, *unit_pieces, first_key, table),
+        (at, *unit_pieces, *token_pieces, table, first_key),
         (
+            ((2, Z, ROWS, 2 * HEAD), bf16),
             ((LENGTH, D), bf16),
             ((LENGTH, 3 * HEAD), f32),
             ((LENGTH, UNIT), bf16),
             ((LENGTH, 2 * HEAD), bf16),
-            ((2, Z, ROWS, 2 * HEAD), bf16),
             ((8, LENGTH), f32),
             ((8, D), f32),
             ((D, UNIT), bf16),
         ),
-        28,
-        scratch=(((HEAD, LENGTH), bf16),),
+        scratch=(((HEAD, LENGTH), bf16), pltpu.SemaphoreType.DMA((8,))),
         flops=4 * 10**9,
+        raw_outs=1,
     )
 
     mixed_tokens = lax.all_to_all(
         mixed.reshape(N_SEQ, ROWS, 2 * HEAD), "seq", split_axis=0, concat_axis=0, tiled=True
     )
+    turned = turned.reshape(2, Z * ROWS, 2 * HEAD)
+    mixed_mine, mixed_other = turned[0], swap_x_hi(turned[1])
+    mixed_tokens, mixed_other = lax.optimization_barrier((mixed_tokens, mixed_other))
+    incoming = after(cotangent[0], mixed)
+    cotangent_z = gather4(*halves(incoming), swap_z_a, swap_z_b)
     half_rows = ((ROWS // 2, D), bf16)
     hidden, upper, lower = kernel_call(
         out_kernel,
         (mixed_tokens, sequence, gains, later),
         (((ROWS, D), f32), half_rows, half_rows),
-        16,
         scratch=(((ROWS, 2 * D), bf16), ((D, 2 * D), bf16), pltpu.SemaphoreType.DMA((1,))),
         flops=10**9,
         raw=(3,),
     )
-    turned = after(turned, upper).reshape(2, Z * ROWS, 2 * HEAD)
-    mixed_mine, mixed_other = turned[0], swap_x_hi(turned[1])
+    upper, lower = after((upper, lower), cotangent_z)
     normed_post_z = gather4(upper, lower, swap_z_a, swap_z_b)
-    sent = (((ROWS, D), bf16), ((ROWS, D), bf16), ((2 * ROWS, D), f32))
-    rows_z, incoming_z, both_grad, inner, first_0, first_1, keep = kernel_call(
+    sent = (((ROWS, D), bf16), ((ROWS, D), bf16), ((ROWS, D), f32), ((ROWS, D), f32))
+    first_0, first_1, passed, own, mlp_share, down_0, down_1, down_passed, down_own = kernel_call(
         mlp_kernel,
         (*normed_post_z, *cotangent_z, later),
-        (
+        (*sent, ((D, 3 * FF_Z), bf16), *sent),
+        scratch=(
+            ((D, 3 * FF_Z), bf16),
+            pltpu.SemaphoreType.DMA((9,)),
             ((Z * ROWS, D), bf16),
             ((Z * ROWS, D), bf16),
             ((Z * ROWS, 2 * FF_Z), bf16),
             ((Z * ROWS, FF_Z), bf16),
-            *sent,
         ),
-        28,
-        scratch=(((D, 3 * FF_Z), bf16), pltpu.SemaphoreType.DMA((9,))),
-        flops=4 * 10**9,
+        flops=8 * 10**9,
         raw=(12,),
     )
-    mlp_share, down_0, down_1, down_keep = kernel_call(
-        mlp_grad_kernel,
-        (rows_z, incoming_z, both_grad, inner, later),
-        (((D, 3 * FF_Z), bf16), *sent),
-        24,
-        scratch=(((D, FF_Z), bf16), pltpu.SemaphoreType.DMA((1,))),
-        flops=4 * 10**9,
-        raw=(4,),
-    )
     got_0, got_1, last_0, last_1 = scatter4(
-        first_0, first_1, kept(keep), swap_z_a, swap_z_b, mlp_share
+        first_0, first_1, *halves(passed), swap_z_a, swap_z_b
     )
     mlp_share = lax.psum_scatter(mlp_share, "fsdp", scatter_dimension=0, tiled=True)
     hidden_grad, upper, lower, mixed_grad = kernel_call(
         mid_kernel,
-        (keep, got_0, got_1, last_0, last_1, hidden, cotangent[0], gains, later),
+        (own, got_0, got_1, last_0, last_1, hidden, cotangent[0], gains, later),
         (((ROWS, D), f32), half_rows, half_rows, ((N_SEQ, ROWS, 2 * HEAD), bf16)),
-        16,
         scratch=(((D, 2 * D), bf16), pltpu.SemaphoreType.DMA((8,))),
         flops=10**9,
         raw=(8,),
     )
     mixed_grad = lax.all_to_all(mixed_grad, "seq", split_axis=0, concat_axis=0, tiled=True)
+    down_got = []
+
+    def tie_down(*got):
+        down_got.extend(after(got, upper))
+        return down_got
+
+    down_parts = scatter4(down_0, down_1, *halves(down_passed), swap_z_a, swap_z_b, tie_down)
+    upper, lower = after((upper, lower), tuple(down_got))
     proj_grad_z = gather4(upper, lower, swap_z_a, swap_z_b)
-    down_0, down_1 = after((down_0, down_1), upper)
-    down_got_0, down_got_1, down_last_0, down_last_1 = scatter4(
-        down_0, down_1, kept(down_keep), swap_z_a, swap_z_b
-    )
-    mixed_grad = after(mixed_grad, (down_got_0, down_got_1))
-
-    back, gain_grads, dx_0, dx_1, dx_keep = kernel_call(
+    result = hidden + jnp.concatenate(total4(*halves(down_own), *down_parts), axis=0)
+    result = result.astype(bf16)
+
+    share, share_sent, dx_0, dx_1, dx_passed, dx_own = kernel_call(
         back_kernel,
-        (at, raw, heads, log_total, mixed_grad.reshape(LENGTH, 2 * HEAD), first_key, table, gains, weight),
         (
-            ((LENGTH, UNIT), bf16),
-            ((8, HEAD), f32),
+            at, heads, mixed_grad.reshape(LENGTH, 2 * HEAD), first_key, log_total, raw, table, gains,
+            weight, normed, mixed_mine, mixed_other, *proj_grad_z,
+        ),
+        (
+            ((Z, 2, OWN, SHARE), bf16),
+            ((Z, 2, OWN, SHARE), bf16),
             ((2 * ROWS, D), bf16),
             ((2 * ROWS, D), bf16),
-            ((4 * ROWS, D), f32),
+            ((2 * ROWS, D), f32),
+            ((2 * ROWS, D), f32),
         ),
-        30,
         scratch=(
+            ((LENGTH, UNIT), bf16),
             ((HEAD, LENGTH), bf16),
             ((LENGTH, HEAD), f32),
             ((LENGTH, HEAD), f32),
             ((LENGTH, 2 * HEAD), f32),
-            ((LENGTH, UNIT), bf16),
-        ),
-        flops=4 * 10**9,
-    )
-    share, share_sent = kernel_call(
-        grad_kernel,
-        (at, normed, back, gain_grads, *proj_grad_z, mixed_mine, mixed_other),
-        (((Z, 2, OWN, SHARE), bf16), ((Z, 2, OWN, SHARE), bf16)),
-        20,
-        scratch=(
-            ((2, Z, 2, OWN, SHARE), bf16),
+            ((8, HEAD), f32),
             ((Z * ROWS, D), bf16),
             ((Z * ROWS, UNIT), bf16),
+            ((2, Z, 2, OWN, SHARE), bf16),
+            ((LENGTH, UNIT), bf16),
             pltpu.SemaphoreType.DMA((2,)),
         ),
-        flops=4 * 10**9,
+        flops=8 * 10**9,
         raw_outs=2,
     )
     share = share.reshape(D // 2, SHARE)
@@ -734,29 +752,35 @@
     def share_pair(one, two):
         return jnp.concatenate([share_block(*one), share_block(*two)], axis=0).astype(bf16)
 
-    share_0, share_1 = total4(
-        share_block,
-        *scatter4(
-            share_pair((3, 0), (2, 0)), share_pair((1, 1), (2, 1)), share_block, swap_y_a, swap_y_b
-        ),
-    )
-    attn_share = (share_0 + swap_x_lo(share_1.astype(bf16)).astype(f32)).astype(bf16)
-
-    mine = jnp.concatenate([attn_share, mlp_share[:, :SHARE], mlp_share[:, SHARE:]], axis=0)
-    mine = lax.optimization_barrier(mine)
-    other = swap_x_hi(mine)
-    mlp_sum = (mine[OWN:].astype(f32) + other[OWN:].astype(f32)).astype(bf16)
-    half = OWN // 2
-    zero = jnp.concatenate([mine[:OWN], mlp_sum[:half], mlp_sum[OWN : OWN + half]], axis=0)
-    one = jnp.concatenate([other[:OWN], mlp_sum[half:OWN], mlp_sum[OWN + half :]], axis=0)
-    zero, one = lax.optimization_barrier((zero, one))
-    last_pieces = gather4(zero, one, swap_z_a, swap_z_b)
-
-    normed_grad, other_grad = total4(
-        kept(dx_keep), *scatter4(dx_0, dx_1, kept(dx_keep), swap_z_a, swap_z_b)
-    )
-    normed_grad = normed_grad + swap_x_hi(other_grad.astype(bf16)).astype(f32)
-    normed_grad = normed_grad * gains[0:1]
+    dx_got = swap_z_b(dx_0), swap_z_a(dx_1)
+    share_got = (
+        swap_y_b(share_pair((3, 0), (2, 0))),
+        swap_y_a(share_pair((1, 1), (2, 1))),
+    )
+    dx_got, share_got = lax.optimization_barrier((dx_got, share_got))
+
+    def second(got, passed_0, passed_1, swap_a, swap_b):
+        n = got[0].shape[0] // 2
+        last_0 = swap_a((passed_0 + got[0][n:].astype(f32)).astype(bf16))
+        last_1 = swap_b((passed_1 + got[1][n:].astype(f32)).astype(bf16))
+        return got[0][:n], got[1][:n], last_0, last_1
+
+    share_parts = second(share_got, share_block(1, 0), share_block(3, 1), swap_y_a, swap_y_b)
+    dx_parts = second(dx_got, *halves(dx_passed), swap_z_a, swap_z_b)
+    share_parts, dx_parts = lax.optimization_barrier((share_parts, dx_parts))
+    share_0, share_1 = total4(share_block(0, 0), share_block(0, 1), *share_parts)
+    share_0, share_1 = share_0.astype(bf16), share_1.astype(bf16)
+    normed_grad, other_grad = total4(*halves(dx_own), *dx_parts)
+    other_grad = other_grad.astype(bf16)
+    share_0, share_1, other_grad = lax.optimization_barrier((share_0, share_1, other_grad))
+    attn_share = (share_0.astype(f32) + swap_x_lo(share_1).astype(f32)).astype(bf16)
+    other_attn = swap_x_hi(share_0).astype(f32) + swap_x_both(share_1).astype(f32)
+    other_attn = other_attn.astype(bf16)
+    other_grad = swap_x_hi(other_grad)
+    attn_share, other_attn, other_grad = lax.optimization_barrier(
+        (attn_share, other_attn, other_grad)
+    )
+    normed_grad = (normed_grad + other_grad.astype(f32)) * gains[0:1]
     widened = sequence.astype(f32)
     inverse = inverse_norm(widened)
     unit_input = widened * inverse
@@ -764,52 +788,40 @@
         normed_grad - unit_input * jnp.mean(unit_input * normed_grad, axis=-1, keepdims=True)
     )
 
-    down_last = after((down_last_0, down_last_1), last_pieces)
-    down = total4(kept(down_keep), down_got_0, down_got_1, *down_last)
-    result = (hidden + jnp.concatenate(down, axis=0)).astype(bf16)
-
-    (
-        gate_total,
-        up_total,
-        down_total,
-        query_total,
-        key_total,
-        value_total,
-        output_total,
-        post_gain_total,
-        input_gain_total,
-        head_gain_total,
-    ) = kernel_call(
-        last_kernel,
+    last_pieces = gather4(attn_share, other_attn, swap_z_a, swap_z_b)
+    mlp_pieces = lax.all_gather(mlp_share, "seq", axis=0, tiled=False)
+
+    query_total, key_total, value_total, output_total, input_gain, query_gain, key_gain = kernel_call(
+        last_attn_kernel,
         (
-            at, *last_pieces, w_gate, w_up, w_query, w_key, w_value,
-            norm_post.astype(f32).reshape(OWN, 1), norm_input.astype(f32).reshape(OWN, 1),
+            at, *last_pieces, w_query, w_key, w_value, norm_input.astype(f32).reshape(OWN, 1),
         ),
         (
-            ((OWN, FF), f32),
-            ((OWN, FF), f32),
-            ((OWN, FF), f32),
             ((OWN, 2 * D), f32),
             ((OWN, D), f32),
             ((OWN, D), f32),
             ((OWN, 2 * D), f32),
-            ((OWN, 1), f32),
-            ((OWN, 1), f32),
-            ((8, HEAD), f32),
+            ((1, OWN), f32),
+            ((1, HEAD // N_FSDP), f32),
+            ((1, HEAD // N_FSDP), f32),
         ),
-        16,
+    )
+    gate_total, up_total, down_total, post_gain = kernel_call(
+        last_mlp_kernel,
+        (mlp_pieces, w_gate, w_up, norm_post.astype(f32).reshape(OWN, 1)),
+        (((OWN, FF), f32), ((OWN, FF), f32), ((OWN, FF), f32), ((1, OWN), f32)),
     )
     return (
         result[None],
         tokens_grad[None],
-        input_gain_total.reshape(OWN),
+        input_gain[0],
         query_total,
         key_total,
         value_total,
-        head_gain_total[0, :8],
-        head_gain_total[0, 8:16],
+        query_gain[0],
+        key_gain[0],
         output_total.T,
-        post_gain_total.reshape(OWN),
+        post_gain[0],
         gate_total,
         up_total,
         down_total.T,

time: 304 us -> 280 us (0.921)
  the two profiles are of different devices: /device:TPU:2 before, /device:TPU:1 now
where the time goes in v2:
time: 280 us; the launch traced here: 275 us
  starting transfers between devices  88.9 us (32%)
  waiting for transfers between devices  75.5 us (27%)
  Pallas kernels  61.1 us (22%)
  local copies, waits for them, and re-layouts  18.4 us (7%)
  other arithmetic  15.5 us (6%)
  between operations  15.3 us (5%)
    ppermute x50, starting transfers between devices, exchange(): return lax.ppermute(values, axis, [(i, i ^ bits) for i in range(size)])  79.2 us
    pallas_call x7, Pallas kernels, kernel_call(): pl.pallas_call(body, out_shape=[jax.ShapeDtypeStruct(shape, dtype) for sh...  61.1 us
    ppermute x50, waiting for transfers between devices, exchange(): return lax.ppermute(values, axis, [(i, i ^ bits) for i in range(size)])  55.4 us
    ppermute x1, waiting for transfers between devices, swap_x_both(): return lax.ppermute(values, ('seq', 'fsdp'), pairs)  10.8 us
    unnamed x122, local copies, waits for them, and re-layouts  8.35 us
    all_to_all x1, starting transfers between devices, per_device(): lax.all_to_all(mixed.reshape(N_SEQ, ROWS, 2 * HEAD), 'seq', split_axis=0,...  6.08 us
  transfers between devices with their start and end apart: 56, of which 17 were waited for; matrix products, arithmetic and copies ran while one was open for 8% of the time, Pallas kernels for 15%

profile of v2, /device:TPU:1, one launch (start us, length us, event | category | flops | bytes accessed | tf_op | source)
XLA Modules:
  0.0 274.8 jit_solution(1314133433736417413)
XLA Ops:
  8.2 1.0 constant_dynamic-slice_fusion
  9.2 1.8 pad_maximum_fusion
  13.7 1.5 collective-permute-start
  15.2 1.3 collective-permute-start.2
  16.6 1.7 collective-permute-start.7
  18.3 2.7 collective-permute-start.9
  21.2 1.4 collective-permute-start.3
  22.6 1.9 collective-permute-start.5
  24.5 3.6 %collective-permute-start.8 = (bf16[256,1024]{1,0:T(8,128)(2,1)S(1)}, bf16[256,1024]{1,0:T(8,128)(2,1)S(1)}, u32[]{:S(2)}, u32[]{:S(2)}) collective-permute-start(bf16[256,1024]{1,0:T(8,128)(2,1)S(1)} %pad_maximum_fusion.1), channel_id=1, source_target_pairs={{0,96},{16,112},{32,64},{48,80},{64,32},{80,48},{96,0},{112,16},{1... | collective-permute-start | bytes 1572872 | tf_op jit(solution)/shard_map/ppermute | solution.py:59
  28.1 2.0 collective-permute-done.9.refs_10_
  30.1 2.0 collective-permute-start.10
  32.1 3.1 %collective-permute-start.4 = (bf16[320,512]{1,0:T(8,128)(2,1)S(1)}, bf16[320,512]{1,0:T(8,128)(2,1)}, u32[]{:S(2)}, u32[]{:S(2)}) collective-permute-start(bf16[320,512]{1,0:T(8,128)(2,1)S(1)} %pad_maximum_fusion.2), channel_id=1, source_target_pairs={{0,12},{1,13},{2,14},{3,15},{4,8},{5,9},{6,10},{7,11},{8,4},{9,5},... | collective-permute-start | bytes 983048 | tf_op jit(solution)/shard_map/ppermute | solution.py:59
  35.3 3.0 %collective-permute-start.11 = (bf16[128,1024]{1,0:T(8,128)(2,1)S(1)}, bf16[128,1024]{1,0:T(8,128)(2,1)S(1)}, u32[]{:S(2)}, u32[]{:S(2)}) collective-permute-start(bf16[128,1024]{1,0:T(8,128)(2,1)S(1)} %collective-permute-done.9.refs_10_), channel_id=1, source_target_pairs={{0,96},{16,112},{32,64},{48,80},{64,32},{80,48},{96,0},{112,16},{1... | collective-permute-start | bytes 786440 | tf_op jit(solution)/shard_map/ppermute | solution.py:59
  38.3 2.9 %collective-permute-start.12 = (bf16[128,1024]{1,0:T(8,128)(2,1)S(1)}, bf16[128,1024]{1,0:T(8,128)(2,1)S(1)}, u32[]{:S(2)}, u32[]{:S(2)}) collective-permute-start(bf16[128,1024]{1,0:T(8,128)(2,1)S(1)} %collective-permute-done.9.refs_10_), channel_id=1, source_target_pairs={{0,64},{16,80},{32,96},{48,112},{64,0},{80,16},{96,32},{112,48},{1... | collective-permute-start | bytes 786440 | tf_op jit(solution)/shard_map/ppermute | solution.py:59
  41.9 1.2 convert_reduce_fusion
  43.1 6.8 %collective-permute-done.11.refs_12_ = bf16[128,1024]{1,0:T(8,128)(2,1)S(1)} collective-permute-done((bf16[128,1024]{1,0:T(8,128)(2,1)S(1)}, bf16[128,1024]{1,0:T(8,128)(2,1)S(1)}, u32[]{:S(2)}, u32[]{:S(2)}) %collective-permute-start.11) | collective-permute-done | bytes 262176 | tf_op jit(solution)/shard_map/ppermute | solution.py:59
  50.9 11.5 %shard_map.246 = (bf16[2,4,128,256]{3,2,1,0:T(8,128)(2,1)}, bf16[1024,1024]{1,0:T(8,128)(2,1)}, f32[1024,384]{1,0:T(8,128)}, bf16[1024,512]{1,0:T(8,128)(2,1)}, ...) custom-call(s32[5]{0:T(128)} %stack.23.refs_0_, ...), custom_call_target="tpu_custom_call" | custom-call | flops 4000000000 | bytes 8388608 | tf_op jit(solution)/shard_map/pallas_call | solution.py:547
  62.4 6.1 %all-to-all-start = ((bf16[8,128,256]{2,1,0:T(8,128)(2,1)}), bf16[8,128,256]{2,1,0:T(8,128)(2,1)S(1)}, u32[]{:S(2)}, u32[]{:S(2)}) async-start(bf16[8,128,256]{2,1,0:T(8,128)(2,1)} %bitcast.50), calls=%async_computation | async-start | bytes 1048576 | tf_op jit(solution)/shard_map/all_to_all | solution.py:654
  68.6 1.5 collective-permute-start.14
  70.1 1.8 collective-permute-start.16
  72.6 2.7 collective-permute-start.13
  76.6 7.8 %collective-permute-done.13.refs_11_ = bf16[512,256]{1,0:T(8,128)(2,1)S(1)} collective-permute-done((bf16[512,256]{1,0:T(8,128)(2,1)S(1)}, bf16[512,256]{1,0:T(8,128)(2,1)S(1)}, u32[]{:S(2)}, u32[]{:S(2)}) %collective-permute-start.13) | collective-permute-done | bytes 262176 | tf_op jit(solution)/shard_map/ppermute | solution.py:59
  85.2 5.2 %shard_map.247 = (f32[128,1024]{1,0:T(8,128)}, bf16[64,1024]{1,0:T(8,128)(2,1)}, bf16[64,1024]{1,0:T(8,128)(2,1)}) custom-call(bf16[8,128,256]{2,1,0:T(8,128)(2,1)} %copy-done.4, bf16[128,1024]{1,0:T(8,128)(2,1)} %bitcast.40, f32[8,1024]{1,0:T(8,128)} %get-tuple-element.88.refs_2_.refs_7_, ...), custom_call_target="tpu_custom_call" | custom-call | flops 1000000000 | bytes 8388608 | tf_op jit(solution)/shard_map/pallas_call | solution.py:547
  90.5 2.0 collective-permute-start.18
  92.5 2.6 collective-permute-start.20
  96.1 4.0 %collective-permute-start.19 = (bf16[128,1024]{1,0:T(8,128)(2,1)S(1)}, bf16[128,1024]{1,0:T(8,128)(2,1)S(1)}, u32[]{:S(2)}, u32[]{:S(2)}) collective-permute-start(bf16[128,1024]{1,0:T(8,128)(2,1)S(1)} %pad_maximum_fusion.10), channel_id=1, source_target_pairs={{0,96},{16,112},{32,64},{48,80},{64,32},{80,48},{96,0},{112,16},{1... | collective-permute-start | bytes 786440 | tf_op jit(solution)/shard_map/ppermute | solution.py:59
  101.4 2.7 collective-permute-done.19.refs_2_
  104.1 2.8 %collective-permute-done.21.refs_5_ = bf16[128,1024]{1,0:T(8,128)(2,1)S(1)} collective-permute-done((bf16[128,1024]{1,0:T(8,128)(2,1)S(1)}, bf16[128,1024]{1,0:T(8,128)(2,1)S(1)}, u32[]{:S(2)}, u32[]{:S(2)}) %collective-permute-start.21) | collective-permute-done | bytes 262176 | tf_op jit(solution)/shard_map/ppermute | solution.py:59
  107.6 15.7 %shard_map.248 = (bf16[128,1024]{1,0:T(8,128)(2,1)}, bf16[128,1024]{1,0:T(8,128)(2,1)}, f32[128,1024]{1,0:T(8,128)}, f32[128,1024]{1,0:T(8,128)}, bf16[1024,2304...) custom-call(bf16[64,1024]{1,0:T(8,128)(2,1)} %get-tuple-element.93.r, ...), custom_call_target="tpu_custom_call" | custom-call | flops 8000000000 | bytes 8388608 | tf_op jit(solution)/shard_map/pallas_call | solution.py:547
  124.6 2.4 collective-permute-start.22
  127.8 2.9 %collective-permute-done.24 = bf16[128,1024]{1,0:T(8,128)(2,1)S(1)} collective-permute-done((bf16[128,1024]{1,0:T(8,128)(2,1)S(1)}, bf16[128,1024]{1,0:T(8,128)(2,1)S(1)}, u32[]{:S(2)}, u32[]{:S(2)}) %collective-permute-start.24) | collective-permute-done | bytes 262176 | tf_op jit(solution)/shard_map/ppermute | solution.py:59
  130.9 1.5 collective-permute-start.27
  133.8 2.6 collective-permute-done.26.refs_3_
  136.4 1.5 collective-permute-done.27.refs_4_
  138.5 6.4 %shard_map.249 = (f32[128,1024]{1,0:T(8,128)}, bf16[64,1024]{1,0:T(8,128)(2,1)}, bf16[64,1024]{1,0:T(8,128)(2,1)}, bf16[8,128,256]{2,1,0:T(8,128)(2,1)}) custom-call(f32[128,1024]{1,0:T(8,128)} %get-tuple-element.98.refs_0_, bf16[64,1024]{1,0:T(8,128)(2,1)} %slice.190.refs_1_, bf16[64,1024]{1,0:T(8,128)(2,1)} %slice.191.refs_2_, ...), custom_call_target="tpu_custom_call" | custom-call | flops 1000000000 | bytes 8388608 | tf_op jit(solution)/shard_map/pallas_call | solution.py:547
  145.2 1.7 collective-permute-start.32
  146.8 3.5 %all-to-all-start.1 = ((bf16[8,128,256]{2,1,0:T(8,128)(2,1)}), bf16[8,128,256]{2,1,0:T(8,128)(2,1)S(1)}, u32[]{:S(2)}, u32[]{:S(2)}) async-start(bf16[8,128,256]{2,1,0:T(8,128)(2,1)} %get-tuple-element.108), calls=%async_computation.1 | async-start | bytes 1048576 | tf_op jit(solution)/shard_map/all_to_all | solution.py:701
  151.4 2.6 collective-permute-start.31
  154.1 6.7 %collective-permute-done.31.refs_14_ = bf16[128,1024]{1,0:T(8,128)(2,1)S(1)} collective-permute-done((bf16[128,1024]{1,0:T(8,128)(2,1)S(1)}, bf16[128,1024]{1,0:T(8,128)(2,1)S(1)}, u32[]{:S(2)}, u32[]{:S(2)}) %collective-permute-start.31) | collective-permute-done | bytes 262176 | tf_op jit(solution)/shard_map/ppermute | solution.py:59
  160.9 3.9 %all-to-all-done.1 = bf16[8,128,256]{2,1,0:T(8,128)(2,1)S(1)} async-done(((bf16[8,128,256]{2,1,0:T(8,128)(2,1)}), bf16[8,128,256]{2,1,0:T(8,128)(2,1)S(1)}, u32[]{:S(2)}, u32[]{:S(2)}) %all-to-all-start.1) | async-done | bytes 524320 | tf_op jit(solution)/shard_map/all_to_all | solution.py:701
  165.6 15.1 %shard_map.250 = (bf16[4,2,64,1152]{3,2,1,0:T(8,128)(2,1)}, bf16[4,2,64,1152]{3,2,1,0:T(8,128)(2,1)}, bf16[256,1024]{1,0:T(8,128)(2,1)}, bf16[256,1024]{1,0:T(8,...) custom-call(s32[5]{0:T(128)} %stack.23.refs_0_, bf16[1024,512]{1,0:T(8,128)(2,1)} %get-tuple-element.107.refs_1_, ...), custom_call_target="tpu_custom_call" | custom-call | flops 8000000000 | bytes 8388608 | tf_op jit(solution)/shard_map/pallas_call | solution.py:547
  180.7 9.3 %collective-permute-start.36 = (bf16[512,1152]{1,0:T(8,128)(2,1)}, bf16[512,1152]{1,0:T(8,128)(2,1)S(1)}, u32[]{:S(2)}, u32[]{:S(2)}) collective-permute-start(bf16[512,1152]{1,0:T(8,128)(2,1)} %bitcast.60), channel_id=1, source_target_pairs={{0,1},{1,0},{2,3},{3,2},{4,5},{5,4},{6,7},{7,6},{8,9},{9,8},{10,11... | collective-permute-start | bytes 3538952 | tf_op jit(solution)/shard_map/ppermute | solution.py:59
  191.1 1.6 collective-permute-done.36
  192.7 1.3 add_convert_fusion.10
  194.1 2.5 collective-permute-start.37
  199.5 1.7 add_convert_fusion.14
  201.3 4.0 %collective-permute-done.34 = bf16[256,1024]{1,0:T(8,128)(2,1)} collective-permute-done((bf16[256,1024]{1,0:T(8,128)(2,1)}, bf16[256,1024]{1,0:T(8,128)(2,1)}, u32[]{:S(2)}, u32[]{:S(2)}) %collective-permute-start.34) | collective-permute-done | bytes 524320 | tf_op jit(solution)/shard_map/ppermute | solution.py:59
  206.7 1.6 add_convert_fusion.1
  208.4 2.2 collective-permute-start.42
  210.8 2.6 collective-permute-start.40
  213.4 1.1 convert_add_fusion.1
  214.6 1.1 slice.178
  215.7 1.0 slice.179
  218.7 2.5 collective-permute-start.44
  221.7 2.4 collective-permute-done.43
  224.1 10.8 %collective-permute-done.45 = bf16[64,1152]{1,0:T(8,128)(2,1)S(1)} collective-permute-done((bf16[64,1152]{1,0:T(8,128)(2,1)S(1)}, bf16[64,1152]{1,0:T(8,128)(2,1)S(1)}, u32[]{:S(2)}, u32[]{:S(2)}) %collective-permute-start.45) | collective-permute-done | bytes 147488 | tf_op jit(solution)/shard_map/ppermute | solution.py:74
  235.0 1.3 collective-permute-start.47
  236.3 1.9 collective-permute-start.49
  239.1 2.6 collective-permute-start.48
  241.9 1.1 fusion.6
  243.0 10.8 %collective-permute-done.48.refs_3_ = bf16[128,1152]{1,0:T(8,128)(2,1)S(1)} collective-permute-done((bf16[128,1152]{1,0:T(8,128)(2,1)S(1)}, bf16[128,1152]{1,0:T(8,128)(2,1)S(1)}, u32[]{:S(2)}, u32[]{:S(2)}) %collective-permute-start.48) | collective-permute-done | bytes 294944 | tf_op jit(solution)/shard_map/ppermute | solution.py:59
  255.2 3.4 %shard_map.251 = (f32[64,2048]{1,0:T(8,128)}, f32[64,1024]{1,0:T(8,128)}, f32[64,1024]{1,0:T(8,128)}, f32[64,2048]{1,0:T(8,128)}, f32[1,64]{1,0:T(1,128)}, /*index=5*/f32[1,8]{1,0:T(1,128)}, f32[1,8]{1,0:T(1,128)}) custom-call(s32[5]{0:T(128)} %stack.23.refs_0_, bf16[64,1152]{1,0:T(8,128)(2,1)} %copy-done.6, bf16[64,1152]{1,0:T(8,128)(2,1)} %copy-done.15, ...), custom_call_target="tpu_custom_call" | custom-call | bytes 8388608 | tf_op jit(solution)/shard_map/pallas_call | solution.py:547
  258.6 5.3 %all-gather.6.cloned.1.call-done = bf16[512,2304]{1,0:T(8,128)(2,1)} async-done(((bf16[64,2304]{1,0:T(8,128)(2,1)}), bf16[512,2304]{1,0:T(8,128)(2,1)}) %all-gather.6.cloned.1.call-update) | async-done | bytes 2359312 | tf_op jit(solution)/shard_map/all_gather | solution.py:792
  264.0 3.8 %shard_map.252 = (f32[64,3072]{1,0:T(8,128)}, f32[64,3072]{1,0:T(8,128)}, f32[64,3072]{1,0:T(8,128)}, f32[1,64]{1,0:T(1,128)}) custom-call(bf16[8,64,2304]{2,1,0:T(8,128)(2,1)} %bitcast.44, bf16[64,3072]{1,0:T(8,128)(2,1)} %refs_1_.1, bf16[64,3072]{1,0:T(8,128)(2,1)} %refs_2_.1, f32[64,1]{1,0:T(8,128)} %copy.33.refs_3_), custom_call_target="tpu_custom_call" | custom-call | bytes 8388608 | tf_op jit(solution)/shard_map/pallas_call | solution.py:547
  (248 shorter events, 28.4 us)
Async XLA Ops:
  7.2 77.2 %all-gather.4.cloned.1.call-start = ((), (), s32[]{:S(2)}) async-start(), calls=%async_computation.3 | async-start | bytes 9469952 | tf_op jit(solution)/shard_map/all_gather | solution.py:634
  13.7 7.4 %collective-permute-start = (bf16[80,512]{1,0:T(8,128)(2,1)S(1)}, bf16[80,512]{1,0:T(8,128)(2,1)S(1)}, u32[]{:S(2)}, u32[]{:S(2)}) collective-permute-start(bf16[80,512]{1,0:T(8,128)(2,1)S(1)} %fusion.11), channel_id=1, source_target_pairs={{0,1},{1,0},{2,3},{3,2},{4,5},{5,4},{6,7},{7,6},{8,9},{9,8},{10,11... | collective-permute-start | bytes 245768 | tf_op jit(solution)/shard_map/ppermute | solution.py:59
  15.2 5.9 %collective-permute-start.2 = (bf16[80,512]{1,0:T(8,128)(2,1)S(1)}, bf16[80,512]{1,0:T(8,128)(2,1)S(1)}, u32[]{:S(2)}, u32[]{:S(2)}) collective-permute-start(bf16[80,512]{1,0:T(8,128)(2,1)S(1)} %fusion.11), channel_id=1, source_target_pairs={{0,3},{1,2},{2,1},{3,0},{4,7},{5,6},{6,5},{7,4},{8,11},{9,10},{10,... | collective-permute-start | bytes 245768 | tf_op jit(solution)/shard_map/ppermute | solution.py:59
  16.4 4.7 %collective-permute-start.1 = (bf16[80,512]{1,0:T(8,128)(2,1)S(1)}, bf16[80,512]{1,0:T(8,128)(2,1)S(1)}, u32[]{:S(2)}, u32[]{:S(2)}) collective-permute-start(bf16[80,512]{1,0:T(8,128)(2,1)S(1)} %fusion.11), channel_id=1, source_target_pairs={{0,2},{1,3},{2,0},{3,1},{4,6},{5,7},{6,4},{7,5},{8,10},{9,11},{10,... | collective-permute-start | bytes 245768 | tf_op jit(solution)/shard_map/ppermute | solution.py:59
  16.6 7.8 %collective-permute-start.7 = (bf16[128,1024]{1,0:T(8,128)(2,1)S(1)}, bf16[128,1024]{1,0:T(8,128)(2,1)S(1)}, u32[]{:S(2)}, u32[]{:S(2)}) collective-permute-start(bf16[128,1024]{1,0:T(8,128)(2,1)S(1)} %bitcast.41), channel_id=1, source_target_pairs={{0,32},{16,48},{32,0},{48,16},{64,96},{80,112},{96,64},{112,80},{1... | collective-permute-start | bytes 786440 | tf_op jit(solution)/shard_map/ppermute | solution.py:59
  18.3 11.7 %collective-permute-start.9 = (bf16[128,1024]{1,0:T(8,128)(2,1)S(1)}, bf16[128,1024]{1,0:T(8,128)(2,1)S(1)}, u32[]{:S(2)}, u32[]{:S(2)}) collective-permute-start(bf16[128,1024]{1,0:T(8,128)(2,1)S(1)} %bitcast.42), channel_id=1, source_target_pairs={{0,16},{16,0},{32,48},{48,32},{64,80},{80,64},{96,112},{112,96},{1... | collective-permute-start | bytes 786440 | tf_op jit(solution)/shard_map/ppermute | solution.py:59
  21.2 20.7 %copy-start.39 = (s32[1,1024]{1,0:T(1,128)S(1)}, s32[1,1024]{1,0:T(1,128)}, u32[]{:S(2)}) copy-start(s32[1,1024]{1,0:T(1,128)} %param.16) | copy-start | bytes 12292
  21.2 10.9 %collective-permute-start.3 = (bf16[160,512]{1,0:T(8,128)(2,1)S(1)}, bf16[160,512]{1,0:T(8,128)(2,1)S(1)}, u32[]{:S(2)}, u32[]{:S(2)}) collective-permute-start(bf16[160,512]{1,0:T(8,128)(2,1)S(1)} %pad_maximum_fusion.14.refs_1_), channel_id=1, source_target_pairs={{0,4},{1,5},{2,6},{3,7},{4,0},{5,1},{6,2},{7,3},{8,12},{9,13},{10,... | collective-permute-start | bytes 491528 | tf_op jit(solution)/shard_map/ppermute | solution.py:59
  22.6 12.6 %collective-permute-start.5 = (bf16[160,512]{1,0:T(8,128)(2,1)S(1)}, bf16[160,512]{1,0:T(8,128)(2,1)S(1)}, u32[]{:S(2)}, u32[]{:S(2)}) collective-permute-start(bf16[160,512]{1,0:T(8,128)(2,1)S(1)} %pad_maximum_fusion.15.refs_4_), channel_id=1, source_target_pairs={{0,12},{1,13},{2,14},{3,15},{4,8},{5,9},{6,10},{7,11},{8,4},{9,5},... | collective-permute-start | bytes 491528 | tf_op jit(solution)/shard_map/ppermute | solution.py:59
  24.5 25.4 %collective-permute-start.8 = (bf16[256,1024]{1,0:T(8,128)(2,1)S(1)}, bf16[256,1024]{1,0:T(8,128)(2,1)S(1)}, u32[]{:S(2)}, u32[]{:S(2)}) collective-permute-start(bf16[256,1024]{1,0:T(8,128)(2,1)S(1)} %pad_maximum_fusion.1), channel_id=1, source_target_pairs={{0,96},{16,112},{32,64},{48,80},{64,32},{80,48},{96,0},{112,16},{1... | collective-permute-start | bytes 1572872 | tf_op jit(solution)/shard_map/ppermute | solution.py:59
  30.1 19.9 %copy-start.46 = (bf16[128,1024]{1,0:T(8,128)(2,1)}, bf16[128,1024]{1,0:T(8,128)(2,1)S(1)}, u32[]{:S(2)}) copy-start(bf16[128,1024]{1,0:T(8,128)(2,1)S(1)} %collective-permute-done.9.refs_10_) | copy-start | bytes 786436
  30.1 8.2 %collective-permute-start.10 = (bf16[128,1024]{1,0:T(8,128)(2,1)S(1)}, bf16[128,1024]{1,0:T(8,128)(2,1)S(1)}, u32[]{:S(2)}, u32[]{:S(2)}) collective-permute-start(bf16[128,1024]{1,0:T(8,128)(2,1)S(1)} %collective-permute-done.9.refs_10_), channel_id=1, source_target_pairs={{0,32},{16,48},{32,0},{48,16},{64,96},{80,112},{96,64},{112,80},{1... | collective-permute-start | bytes 786440 | tf_op jit(solution)/shard_map/ppermute | solution.py:59
  32.1 17.9 %copy-start.28 = (bf16[160,512]{1,0:T(8,128)(2,1)}, bf16[160,512]{1,0:T(8,128)(2,1)S(1)}, u32[]{:S(2)}) copy-start(bf16[160,512]{1,0:T(8,128)(2,1)S(1)} %collective-permute-done.3.refs_2_) | copy-start | bytes 491524
  32.1 17.8 %collective-permute-start.4 = (bf16[320,512]{1,0:T(8,128)(2,1)S(1)}, bf16[320,512]{1,0:T(8,128)(2,1)}, u32[]{:S(2)}, u32[]{:S(2)}) collective-permute-start(bf16[320,512]{1,0:T(8,128)(2,1)S(1)} %pad_maximum_fusion.2), channel_id=1, source_target_pairs={{0,12},{1,13},{2,14},{3,15},{4,8},{5,9},{6,10},{7,11},{8,4},{9,5},... | collective-permute-start | bytes 983048 | tf_op jit(solution)/shard_map/ppermute | solution.py:59
  35.2 14.7 %collective-permute-start.6 = (bf16[320,512]{1,0:T(8,128)(2,1)S(1)}, bf16[320,512]{1,0:T(8,128)(2,1)}, u32[]{:S(2)}, u32[]{:S(2)}) collective-permute-start(bf16[320,512]{1,0:T(8,128)(2,1)S(1)} %pad_maximum_fusion.3), channel_id=1, source_target_pairs={{0,4},{1,5},{2,6},{3,7},{4,0},{5,1},{6,2},{7,3},{8,12},{9,13},{10,... | collective-permute-start | bytes 983048 | tf_op jit(solution)/shard_map/ppermute | solution.py:59
  35.3 14.6 %collective-permute-start.11 = (bf16[128,1024]{1,0:T(8,128)(2,1)S(1)}, bf16[128,1024]{1,0:T(8,128)(2,1)S(1)}, u32[]{:S(2)}, u32[]{:S(2)}) collective-permute-start(bf16[128,1024]{1,0:T(8,128)(2,1)S(1)} %collective-permute-done.9.refs_10_), channel_id=1, source_target_pairs={{0,96},{16,112},{32,64},{48,80},{64,32},{80,48},{96,0},{112,16},{1... | collective-permute-start | bytes 786440 | tf_op jit(solution)/shard_map/ppermute | solution.py:59
  38.3 11.6 %collective-permute-start.12 = (bf16[128,1024]{1,0:T(8,128)(2,1)S(1)}, bf16[128,1024]{1,0:T(8,128)(2,1)S(1)}, u32[]{:S(2)}, u32[]{:S(2)}) collective-permute-start(bf16[128,1024]{1,0:T(8,128)(2,1)S(1)} %collective-permute-done.9.refs_10_), channel_id=1, source_target_pairs={{0,64},{16,80},{32,96},{48,112},{64,0},{80,16},{96,32},{112,48},{1... | collective-permute-start | bytes 786440 | tf_op jit(solution)/shard_map/ppermute | solution.py:59
  62.4 22.0 %all-to-all-start = ((bf16[8,128,256]{2,1,0:T(8,128)(2,1)}), bf16[8,128,256]{2,1,0:T(8,128)(2,1)S(1)}, u32[]{:S(2)}, u32[]{:S(2)}) async-start(bf16[8,128,256]{2,1,0:T(8,128)(2,1)} %bitcast.50), calls=%async_computation | async-start | bytes 1048576 | tf_op jit(solution)/shard_map/all_to_all | solution.py:654
  68.5 137.4 %reduce-scatter.2.cloned.1.call-start = ((), (), s32[]{:S(2)}) async-start(), calls=%async_computation.4 | async-start | bytes 5013504 | tf_op jit(solution)/shard_map/reduce_scatter | solution.py:692
  68.6 21.8 %copy-start.23 = (bf16[64,1024]{1,0:T(8,128)(2,1)}, bf16[64,1024]{1,0:T(8,128)(2,1)S(1)}, u32[]{:S(2)}) copy-start(bf16[64,1024]{1,0:T(8,128)(2,1)S(1)} %get-tuple-element.171.refs_9_) | copy-start | bytes 393220
  68.6 21.8 %copy-start.24 = (bf16[64,1024]{1,0:T(8,128)(2,1)}, bf16[64,1024]{1,0:T(8,128)(2,1)S(1)}, u32[]{:S(2)}) copy-start(bf16[64,1024]{1,0:T(8,128)(2,1)S(1)} %get-tuple-element.172.refs_6_) | copy-start | bytes 393220
  68.6 6.7 %collective-permute-start.14 = (bf16[64,1024]{1,0:T(8,128)(2,1)S(1)}, bf16[64,1024]{1,0:T(8,128)(2,1)S(1)}, u32[]{:S(2)}, u32[]{:S(2)}) collective-permute-start(bf16[64,1024]{1,0:T(8,128)(2,1)S(1)} %get-tuple-element.172.refs_6_), channel_id=1, source_target_pairs={{0,32},{16,48},{32,0},{48,16},{64,96},{80,112},{96,64},{112,80},{1... | collective-permute-start | bytes 393224 | tf_op jit(solution)/shard_map/ppermute | solution.py:59
  70.1 6.2 %collective-permute-start.16 = (bf16[64,1024]{1,0:T(8,128)(2,1)S(1)}, bf16[64,1024]{1,0:T(8,128)(2,1)S(1)}, u32[]{:S(2)}, u32[]{:S(2)}) collective-permute-start(bf16[64,1024]{1,0:T(8,128)(2,1)S(1)} %get-tuple-element.171.refs_9_), channel_id=1, source_target_pairs={{0,96},{16,112},{32,64},{48,80},{64,32},{80,48},{96,0},{112,16},{1... | collective-permute-start | bytes 393224 | tf_op jit(solution)/shard_map/ppermute | solution.py:59
  72.6 11.8 %collective-permute-start.13 = (bf16[512,256]{1,0:T(8,128)(2,1)S(1)}, bf16[512,256]{1,0:T(8,128)(2,1)S(1)}, u32[]{:S(2)}, u32[]{:S(2)}) collective-permute-start(bf16[512,256]{1,0:T(8,128)(2,1)S(1)} %bitcast.54), channel_id=1, source_target_pairs={{0,16},{16,0},{32,48},{48,32},{64,80},{80,64},{96,112},{112,96},{1... | collective-permute-start | bytes 786440 | tf_op jit(solution)/shard_map/ppermute | solution.py:59
  75.3 15.1 %collective-permute-start.15 = (bf16[128,1024]{1,0:T(8,128)(2,1)S(1)}, bf16[128,1024]{1,0:T(8,128)(2,1)S(1)}, u32[]{:S(2)}, u32[]{:S(2)}) collective-permute-start(bf16[128,1024]{1,0:T(8,128)(2,1)S(1)} %pad_maximum_fusion.8), channel_id=1, source_target_pairs={{0,96},{16,112},{32,64},{48,80},{64,32},{80,48},{96,0},{112,16},{1... | collective-permute-start | bytes 786440 | tf_op jit(solution)/shard_map/ppermute | solution.py:59
  76.3 14.2 %collective-permute-start.17 = (bf16[128,1024]{1,0:T(8,128)(2,1)S(1)}, bf16[128,1024]{1,0:T(8,128)(2,1)S(1)}, u32[]{:S(2)}, u32[]{:S(2)}) collective-permute-start(bf16[128,1024]{1,0:T(8,128)(2,1)S(1)} %pad_maximum_fusion.9), channel_id=1, source_target_pairs={{0,32},{16,48},{32,0},{48,16},{64,96},{80,112},{96,64},{112,80},{1... | collective-permute-start | bytes 786440 | tf_op jit(solution)/shard_map/ppermute | solution.py:59
  90.5 16.4 %copy-start.52 = (bf16[128,1024]{1,0:T(8,128)(2,1)}, bf16[128,1024]{1,0:T(8,128)(2,1)S(1)}, u32[]{:S(2)}) copy-start(bf16[128,1024]{1,0:T(8,128)(2,1)S(1)} %collective-permute-done.15.refs_8_) | copy-start | bytes 786436
  90.5 16.4 %copy-start.53 = (bf16[128,1024]{1,0:T(8,128)(2,1)}, bf16[128,1024]{1,0:T(8,128)(2,1)S(1)}, u32[]{:S(2)}) copy-start(bf16[128,1024]{1,0:T(8,128)(2,1)S(1)} %collective-permute-done.17.refs_11_) | copy-start | bytes 786436
  90.5 4.6 %collective-permute-start.18 = (bf16[64,1024]{1,0:T(8,128)(2,1)}, bf16[64,1024]{1,0:T(8,128)(2,1)S(1)}, u32[]{:S(2)}, u32[]{:S(2)}) collective-permute-start(bf16[64,1024]{1,0:T(8,128)(2,1)} %get-tuple-element.93.refs_0_), channel_id=1, source_target_pairs={{0,32},{16,48},{32,0},{48,16},{64,96},{80,112},{96,64},{112,80},{1... | collective-permute-start | bytes 393224 | tf_op jit(solution)/shard_map/ppermute | solution.py:59
  92.5 7.6 %collective-permute-start.20 = (bf16[64,1024]{1,0:T(8,128)(2,1)}, bf16[64,1024]{1,0:T(8,128)(2,1)S(1)}, u32[]{:S(2)}, u32[]{:S(2)}) collective-permute-start(bf16[64,1024]{1,0:T(8,128)(2,1)} %get-tuple-element.94.refs_3_), channel_id=1, source_target_pairs={{0,96},{16,112},{32,64},{48,80},{64,32},{80,48},{96,0},{112,16},{1... | collective-permute-start | bytes 393224 | tf_op jit(solution)/shard_map/ppermute | solution.py:59
  96.1 8.0 %collective-permute-start.19 = (bf16[128,1024]{1,0:T(8,128)(2,1)S(1)}, bf16[128,1024]{1,0:T(8,128)(2,1)S(1)}, u32[]{:S(2)}, u32[]{:S(2)}) collective-permute-start(bf16[128,1024]{1,0:T(8,128)(2,1)S(1)} %pad_maximum_fusion.10), channel_id=1, source_target_pairs={{0,96},{16,112},{32,64},{48,80},{64,32},{80,48},{96,0},{112,16},{1... | collective-permute-start | bytes 786440 | tf_op jit(solution)/shard_map/ppermute | solution.py:59
  101.1 5.8 %collective-permute-start.21 = (bf16[128,1024]{1,0:T(8,128)(2,1)S(1)}, bf16[128,1024]{1,0:T(8,128)(2,1)S(1)}, u32[]{:S(2)}, u32[]{:S(2)}) collective-permute-start(bf16[128,1024]{1,0:T(8,128)(2,1)S(1)} %pad_maximum_fusion.11), channel_id=1, source_target_pairs={{0,32},{16,48},{32,0},{48,16},{64,96},{80,112},{96,64},{112,80},{1... | collective-permute-start | bytes 786440 | tf_op jit(solution)/shard_map/ppermute | solution.py:59
  124.3 6.4 %collective-permute-start.24 = (bf16[128,1024]{1,0:T(8,128)(2,1)S(1)}, bf16[128,1024]{1,0:T(8,128)(2,1)S(1)}, u32[]{:S(2)}, u32[]{:S(2)}) collective-permute-start(bf16[128,1024]{1,0:T(8,128)(2,1)S(1)} %copy-done.55), channel_id=1, source_target_pairs={{0,96},{16,112},{32,64},{48,80},{64,32},{80,48},{96,0},{112,16},{1... | collective-permute-start | bytes 786440 | tf_op jit(solution)/shard_map/ppermute | solution.py:59
  124.6 6.1 %collective-permute-start.25 = (bf16[128,1024]{1,0:T(8,128)(2,1)S(1)}, bf16[128,1024]{1,0:T(8,128)(2,1)S(1)}, u32[]{:S(2)}, u32[]{:S(2)}) collective-permute-start(bf16[128,1024]{1,0:T(8,128)(2,1)S(1)} %copy-done.54), channel_id=1, source_target_pairs={{0,32},{16,48},{32,0},{48,16},{64,96},{80,112},{96,64},{112,80},{1... | collective-permute-start | bytes 786440 | tf_op jit(solution)/shard_map/ppermute | solution.py:59
  124.6 20.3 %collective-permute-start.22 = (bf16[128,1024]{1,0:T(8,128)(2,1)S(1)}, bf16[128,1024]{1,0:T(8,128)(2,1)}, u32[]{:S(2)}, u32[]{:S(2)}) collective-permute-start(bf16[128,1024]{1,0:T(8,128)(2,1)S(1)} %copy-done.51), channel_id=1, source_target_pairs={{0,96},{16,112},{32,64},{48,80},{64,32},{80,48},{96,0},{112,16},{1... | collective-permute-start | bytes 786440 | tf_op jit(solution)/shard_map/ppermute | solution.py:59
  127.0 17.9 %collective-permute-start.23 = (bf16[128,1024]{1,0:T(8,128)(2,1)S(1)}, bf16[128,1024]{1,0:T(8,128)(2,1)}, u32[]{:S(2)}, u32[]{:S(2)}) collective-permute-start(bf16[128,1024]{1,0:T(8,128)(2,1)S(1)} %copy-done.50), channel_id=1, source_target_pairs={{0,32},{16,48},{32,0},{48,16},{64,96},{80,112},{96,64},{112,80},{1... | collective-permute-start | bytes 786440 | tf_op jit(solution)/shard_map/ppermute | solution.py:59
  130.8 5.6 %collective-permute-start.26 = (bf16[64,1024]{1,0:T(8,128)(2,1)S(1)}, bf16[64,1024]{1,0:T(8,128)(2,1)S(1)}, u32[]{:S(2)}, u32[]{:S(2)}) collective-permute-start(bf16[64,1024]{1,0:T(8,128)(2,1)S(1)} %get-tuple-element.170), channel_id=1, source_target_pairs={{0,32},{16,48},{32,0},{48,16},{64,96},{80,112},{96,64},{112,80},{1... | collective-permute-start | bytes 393224 | tf_op jit(solution)/shard_map/ppermute | solution.py:59
  130.9 7.0 %collective-permute-start.27 = (bf16[64,1024]{1,0:T(8,128)(2,1)S(1)}, bf16[64,1024]{1,0:T(8,128)(2,1)S(1)}, u32[]{:S(2)}, u32[]{:S(2)}) collective-permute-start(bf16[64,1024]{1,0:T(8,128)(2,1)S(1)} %get-tuple-element.169), channel_id=1, source_target_pairs={{0,96},{16,112},{32,64},{48,80},{64,32},{80,48},{96,0},{112,16},{1... | collective-permute-start | bytes 393224 | tf_op jit(solution)/shard_map/ppermute | solution.py:59
  145.0 5.4 %collective-permute-start.30 = (bf16[64,1024]{1,0:T(8,128)(2,1)}, bf16[64,1024]{1,0:T(8,128)(2,1)S(1)}, u32[]{:S(2)}, u32[]{:S(2)}) collective-permute-start(bf16[64,1024]{1,0:T(8,128)(2,1)} %get-tuple-element.115.refs_12_), channel_id=1, source_target_pairs={{0,32},{16,48},{32,0},{48,16},{64,96},{80,112},{96,64},{112,80},{1... | collective-permute-start | bytes 393224 | tf_op jit(solution)/shard_map/ppermute | solution.py:59
  145.2 8.8 %collective-permute-start.32 = (bf16[64,1024]{1,0:T(8,128)(2,1)}, bf16[64,1024]{1,0:T(8,128)(2,1)S(1)}, u32[]{:S(2)}, u32[]{:S(2)}) collective-permute-start(bf16[64,1024]{1,0:T(8,128)(2,1)} %get-tuple-element.116.refs_15_), channel_id=1, source_target_pairs={{0,96},{16,112},{32,64},{48,80},{64,32},{80,48},{96,0},{112,16},{1... | collective-permute-start | bytes 393224 | tf_op jit(solution)/shard_map/ppermute | solution.py:59
  146.8 18.0 %all-to-all-start.1 = ((bf16[8,128,256]{2,1,0:T(8,128)(2,1)}), bf16[8,128,256]{2,1,0:T(8,128)(2,1)S(1)}, u32[]{:S(2)}, u32[]{:S(2)}) async-start(bf16[8,128,256]{2,1,0:T(8,128)(2,1)} %get-tuple-element.108), calls=%async_computation.1 | async-start | bytes 1048576 | tf_op jit(solution)/shard_map/all_to_all | solution.py:701
  150.3 113.6 %all-gather.6.cloned.1.call-start = ((), (), s32[]{:S(2)}) async-start(), calls=%async_computation.5 | async-start | bytes 2654208 | tf_op jit(solution)/shard_map/all_gather | solution.py:792
  151.4 9.5 %collective-permute-start.31 = (bf16[128,1024]{1,0:T(8,128)(2,1)S(1)}, bf16[128,1024]{1,0:T(8,128)(2,1)S(1)}, u32[]{:S(2)}, u32[]{:S(2)}) collective-permute-start(bf16[128,1024]{1,0:T(8,128)(2,1)S(1)} %pad_maximum_fusion.12), channel_id=1, source_target_pairs={{0,96},{16,112},{32,64},{48,80},{64,32},{80,48},{96,0},{112,16},{1... | collective-permute-start | bytes 786440 | tf_op jit(solution)/shard_map/ppermute | solution.py:59
  154.0 6.8 %collective-permute-start.33 = (bf16[128,1024]{1,0:T(8,128)(2,1)S(1)}, bf16[128,1024]{1,0:T(8,128)(2,1)S(1)}, u32[]{:S(2)}, u32[]{:S(2)}) collective-permute-start(bf16[128,1024]{1,0:T(8,128)(2,1)S(1)} %pad_maximum_fusion.13), channel_id=1, source_target_pairs={{0,32},{16,48},{32,0},{48,16},{64,96},{80,112},{96,64},{112,80},{1... | collective-permute-start | bytes 786440 | tf_op jit(solution)/shard_map/ppermute | solution.py:59
  165.6 24.4 %copy-start.2 = (bf16[1,128,1024]{2,1,0:T(8,128)(2,1)S(1)}, bf16[1,128,1024]{2,1,0:T(8,128)(2,1)}, u32[]{:S(2)}) copy-start(bf16[1,128,1024]{2,1,0:T(8,128)(2,1)} %param.15) | copy-start | bytes 786436
  180.7 12.0 %collective-permute-start.36 = (bf16[512,1152]{1,0:T(8,128)(2,1)}, bf16[512,1152]{1,0:T(8,128)(2,1)S(1)}, u32[]{:S(2)}, u32[]{:S(2)}) collective-permute-start(bf16[512,1152]{1,0:T(8,128)(2,1)} %bitcast.60), channel_id=1, source_target_pairs={{0,1},{1,0},{2,3},{3,2},{4,5},{5,4},{6,7},{7,6},{8,9},{9,8},{10,11... | collective-permute-start | bytes 3538952 | tf_op jit(solution)/shard_map/ppermute | solution.py:59
  190.2 15.1 %collective-permute-start.34 = (bf16[256,1024]{1,0:T(8,128)(2,1)}, bf16[256,1024]{1,0:T(8,128)(2,1)}, u32[]{:S(2)}, u32[]{:S(2)}) collective-permute-start(bf16[256,1024]{1,0:T(8,128)(2,1)} %get-tuple-element.118), channel_id=1, source_target_pairs={{0,96},{16,112},{32,64},{48,80},{64,32},{80,48},{96,0},{112,16},{1... | collective-permute-start | bytes 1572872 | tf_op jit(solution)/shard_map/ppermute | solution.py:59
  190.8 15.1 %collective-permute-start.35 = (bf16[256,1024]{1,0:T(8,128)(2,1)}, bf16[256,1024]{1,0:T(8,128)(2,1)}, u32[]{:S(2)}, u32[]{:S(2)}) collective-permute-start(bf16[256,1024]{1,0:T(8,128)(2,1)} %get-tuple-element.119), channel_id=1, source_target_pairs={{0,32},{16,48},{32,0},{48,16},{64,96},{80,112},{96,64},{112,80},{1... | collective-permute-start | bytes 1572872 | tf_op jit(solution)/shard_map/ppermute | solution.py:59
  194.1 11.8 %collective-permute-start.37 = (bf16[128,1152]{1,0:T(8,128)(2,1)S(1)}, bf16[128,1152]{1,0:T(8,128)(2,1)S(1)}, u32[]{:S(2)}, u32[]{:S(2)}) collective-permute-start(bf16[128,1152]{1,0:T(8,128)(2,1)S(1)} %pad_maximum_fusion.4), channel_id=1, source_target_pairs={{0,12},{1,13},{2,14},{3,15},{4,8},{5,9},{6,10},{7,11},{8,4},{9,5},... | collective-permute-start | bytes 884744 | tf_op jit(solution)/shard_map/ppermute | solution.py:59
  197.4 8.5 %collective-permute-start.38 = (bf16[128,1152]{1,0:T(8,128)(2,1)}, bf16[128,1152]{1,0:T(8,128)(2,1)S(1)}, u32[]{:S(2)}, u32[]{:S(2)}) collective-permute-start(bf16[128,1152]{1,0:T(8,128)(2,1)} %pad_maximum_fusion.5), channel_id=1, source_target_pairs={{0,4},{1,5},{2,6},{3,7},{4,0},{5,1},{6,2},{7,3},{8,12},{9,13},{10,... | collective-permute-start | bytes 884744 | tf_op jit(solution)/shard_map/ppermute | solution.py:59
  201.3 9.6 %collective-permute-start.28 = (bf16[64,1024]{1,0:T(8,128)(2,1)}, bf16[64,1024]{1,0:T(8,128)(2,1)S(1)}, u32[]{:S(2)}, u32[]{:S(2)}) collective-permute-start(bf16[64,1024]{1,0:T(8,128)(2,1)} %get-tuple-element.167), channel_id=1, source_target_pairs={{0,32},{16,48},{32,0},{48,16},{64,96},{80,112},{96,64},{112,80},{1... | collective-permute-start | bytes 393224 | tf_op jit(solution)/shard_map/ppermute | solution.py:59
  205.3 8.1 %collective-permute-start.29 = (bf16[64,1024]{1,0:T(8,128)(2,1)}, bf16[64,1024]{1,0:T(8,128)(2,1)}, u32[]{:S(2)}, u32[]{:S(2)}) collective-permute-start(bf16[64,1024]{1,0:T(8,128)(2,1)} %get-tuple-element.168), channel_id=1, source_target_pairs={{0,96},{16,112},{32,64},{48,80},{64,32},{80,48},{96,0},{112,16},{1... | collective-permute-start | bytes 393224 | tf_op jit(solution)/shard_map/ppermute | solution.py:59
  208.3 8.3 %collective-permute-start.41 = (bf16[128,1024]{1,0:T(8,128)(2,1)S(1)}, bf16[128,1024]{1,0:T(8,128)(2,1)S(1)}, u32[]{:S(2)}, u32[]{:S(2)}) collective-permute-start(bf16[128,1024]{1,0:T(8,128)(2,1)S(1)} %get-tuple-element.162), channel_id=1, source_target_pairs={{0,32},{16,48},{32,0},{48,16},{64,96},{80,112},{96,64},{112,80},{1... | collective-permute-start | bytes 786440 | tf_op jit(solution)/shard_map/ppermute | solution.py:59
  208.4 8.2 %collective-permute-start.42 = (bf16[128,1024]{1,0:T(8,128)(2,1)S(1)}, bf16[128,1024]{1,0:T(8,128)(2,1)S(1)}, u32[]{:S(2)}, u32[]{:S(2)}) collective-permute-start(bf16[128,1024]{1,0:T(8,128)(2,1)S(1)} %get-tuple-element.161), channel_id=1, source_target_pairs={{0,96},{16,112},{32,64},{48,80},{64,32},{80,48},{96,0},{112,16},{1... | collective-permute-start | bytes 786440 | tf_op jit(solution)/shard_map/ppermute | solution.py:59
  210.7 5.9 %collective-permute-start.39 = (bf16[64,1152]{1,0:T(8,128)(2,1)S(1)}, bf16[64,1152]{1,0:T(8,128)(2,1)S(1)}, u32[]{:S(2)}, u32[]{:S(2)}) collective-permute-start(bf16[64,1152]{1,0:T(8,128)(2,1)S(1)} %get-tuple-element.156), channel_id=1, source_target_pairs={{0,4},{1,5},{2,6},{3,7},{4,0},{5,1},{6,2},{7,3},{8,12},{9,13},{10,... | collective-permute-start | bytes 442376 | tf_op jit(solution)/shard_map/ppermute | solution.py:59
  210.8 5.8 %collective-permute-start.40 = (bf16[64,1152]{1,0:T(8,128)(2,1)S(1)}, bf16[64,1152]{1,0:T(8,128)(2,1)S(1)}, u32[]{:S(2)}, u32[]{:S(2)}) collective-permute-start(bf16[64,1152]{1,0:T(8,128)(2,1)S(1)} %get-tuple-element.155), channel_id=1, source_target_pairs={{0,12},{1,13},{2,14},{3,15},{4,8},{5,9},{6,10},{7,11},{8,4},{9,5},... | collective-permute-start | bytes 442376 | tf_op jit(solution)/shard_map/ppermute | solution.py:59
  217.0 7.1 %collective-permute-start.43 = (bf16[64,1152]{1,0:T(8,128)(2,1)S(1)}, bf16[64,1152]{1,0:T(8,128)(2,1)S(1)}, u32[]{:S(2)}, u32[]{:S(2)}) collective-permute-start(bf16[64,1152]{1,0:T(8,128)(2,1)S(1)} %get-tuple-element.136), channel_id=1, source_target_pairs={{0,2},{1,3},{2,0},{3,1},{4,6},{5,7},{6,4},{7,5},{8,10},{9,11},{10,... | collective-permute-start | bytes 442376 | tf_op jit(solution)/shard_map/ppermute | solution.py:59
  218.7 16.2 %collective-permute-start.45 = (bf16[64,1152]{1,0:T(8,128)(2,1)S(1)}, bf16[64,1152]{1,0:T(8,128)(2,1)S(1)}, u32[]{:S(2)}, u32[]{:S(2)}) collective-permute-start(bf16[64,1152]{1,0:T(8,128)(2,1)S(1)} %get-tuple-element.136), channel_id=1, source_target_pairs={{0,18},{1,19},{2,16},{3,17},{4,22},{5,23},{6,20},{7,21},{8,26},{9,... | collective-permute-start | bytes 442376 | tf_op jit(solution)/shard_map/ppermute | solution.py:74
  218.7 16.2 %collective-permute-start.44 = (bf16[64,1152]{1,0:T(8,128)(2,1)S(1)}, bf16[64,1152]{1,0:T(8,128)(2,1)S(1)}, u32[]{:S(2)}, u32[]{:S(2)}) collective-permute-start(bf16[64,1152]{1,0:T(8,128)(2,1)S(1)} %get-tuple-element.135), channel_id=1, source_target_pairs={{0,16},{16,0},{32,48},{48,32},{64,80},{80,64},{96,112},{112,96},{1... | collective-permute-start | bytes 442376 | tf_op jit(solution)/shard_map/ppermute | solution.py:59
  221.2 13.8 %collective-permute-start.46 = (bf16[128,1024]{1,0:T(8,128)(2,1)S(1)}, bf16[128,1024]{1,0:T(8,128)(2,1)S(1)}, u32[]{:S(2)}, u32[]{:S(2)}) collective-permute-start(bf16[128,1024]{1,0:T(8,128)(2,1)S(1)} %add_convert_fusion), channel_id=1, source_target_pairs={{0,16},{16,0},{32,48},{48,32},{64,80},{80,64},{96,112},{112,96},{1... | collective-permute-start | bytes 786440 | tf_op jit(solution)/shard_map/ppermute | solution.py:59
  235.0 4.1 %collective-permute-start.47 = (bf16[64,1152]{1,0:T(8,128)(2,1)S(1)}, bf16[64,1152]{1,0:T(8,128)(2,1)S(1)}, u32[]{:S(2)}, u32[]{:S(2)}) collective-permute-start(bf16[64,1152]{1,0:T(8,128)(2,1)S(1)} %add_convert_fusion.4.refs_1_), channel_id=1, source_target_pairs={{0,32},{16,48},{32,0},{48,16},{64,96},{80,112},{96,64},{112,80},{1... | collective-permute-start | bytes 442376 | tf_op jit(solution)/shard_map/ppermute | solution.py:59
  236.3 5.5 %collective-permute-start.49 = (bf16[64,1152]{1,0:T(8,128)(2,1)S(1)}, bf16[64,1152]{1,0:T(8,128)(2,1)S(1)}, u32[]{:S(2)}, u32[]{:S(2)}) collective-permute-start(bf16[64,1152]{1,0:T(8,128)(2,1)S(1)} %add_convert_fusion.3.refs_4_), channel_id=1, source_target_pairs={{0,96},{16,112},{32,64},{48,80},{64,32},{80,48},{96,0},{112,16},{1... | collective-permute-start | bytes 442376 | tf_op jit(solution)/shard_map/ppermute | solution.py:59
  239.1 14.6 %collective-permute-start.48 = (bf16[128,1152]{1,0:T(8,128)(2,1)S(1)}, bf16[128,1152]{1,0:T(8,128)(2,1)S(1)}, u32[]{:S(2)}, u32[]{:S(2)}) collective-permute-start(bf16[128,1152]{1,0:T(8,128)(2,1)S(1)} %pad_maximum_fusion.6), channel_id=1, source_target_pairs={{0,96},{16,112},{32,64},{48,80},{64,32},{80,48},{96,0},{112,16},{1... | collective-permute-start | bytes 884744 | tf_op jit(solution)/shard_map/ppermute | solution.py:59
  241.8 12.0 %collective-permute-start.50 = (bf16[128,1152]{1,0:T(8,128)(2,1)S(1)}, bf16[128,1152]{1,0:T(8,128)(2,1)S(1)}, u32[]{:S(2)}, u32[]{:S(2)}) collective-permute-start(bf16[128,1152]{1,0:T(8,128)(2,1)S(1)} %pad_maximum_fusion.7), channel_id=1, source_target_pairs={{0,32},{16,48},{32,0},{48,16},{64,96},{80,112},{96,64},{112,80},{1... | collective-permute-start | bytes 884744 | tf_op jit(solution)/shard_map/ppermute | solution.py:59
  (54 other events, 297.6 us)
Sparse Core Ops, SparseCore 0:
  11.2 67.7 all-gather.3
  123.5 73.6 reduce-scatter.1
  206.8 57.1 all-gather.5

commit v3 on v2

--- a/solution.py
+++ b/solution.py
@@ -90,6 +90,11 @@
     return zero, zero_1, zero_2, one, one_1, one_2
 
 
+def gather_z(values):
+    groups = [[2 * z + x_hi for z in range(Z)] for x_hi in range(2)]
+    return lax.all_gather(values, "seq", axis=0, tiled=False, axis_index_groups=groups)
+
+
 def halves(rows):
     middle = rows.shape[0] // 2
     return rows[:middle], rows[middle:]
@@ -106,9 +111,14 @@
 
 
 def total4(own_0, own_1, got_0, got_1, last_0, last_1):
-    mine_0 = own_0 + got_0.astype(jnp.float32) + last_0.astype(jnp.float32)
-    mine_1 = own_1 + got_1.astype(jnp.float32) + last_1.astype(jnp.float32)
+    n = own_0.shape[0]
+    mine_0 = own_0 + wide(got_0[:n]) + wide(last_0)
+    mine_1 = own_1 + wide(got_1[:n]) + wide(last_1)
     return mine_0, mine_1
+
+
+def wide(values):
+    return values.astype(jnp.float32)
 
 
 def rotation():
@@ -238,8 +248,8 @@
     key_t[...] = heads[:, key].astype(jnp.float32).T.astype(jnp.bfloat16)
     key_sum[...] = jnp.zeros_like(key_sum)
     value_sum[...] = jnp.zeros_like(value_sum)
-    for begin in range(0, LENGTH, BLOCK):
-        rows, end = slice(begin, begin + BLOCK), begin + BLOCK
+    for start in range(0, LENGTH, BLOCK):
+        rows, end = slice(start, start + BLOCK), start + BLOCK
         for head in range(2):
             columns = slice(head * HEAD, (head + 1) * HEAD)
             query, rows_grad = heads[rows, columns], grad[rows, columns]
@@ -247,7 +257,7 @@
             prob_grad = contract(heads[:end, value], rows_grad)
             log_now = log_total[head : head + 1, rows]
             parts, mean = [], 0.0
-            for first, s in allowed_scores(scores, first_key, begin):
+            for first, s in allowed_scores(scores, first_key, start):
                 prob = jnp.exp(s - log_now)
                 pulled = prob_grad[first : first + s.shape[0]]
                 mean += jnp.sum(prob * pulled, axis=0, keepdims=True)
@@ -266,8 +276,8 @@
         columns = slice(head * HEAD, (head + 1) * HEAD)
         which = 0 if head < 2 else 1
         gain = gains[2:3, which * HEAD : (which + 1) * HEAD]
-        for begin in range(0, LENGTH, BLOCK):
-            rows = slice(begin, begin + BLOCK)
+        for start in range(0, LENGTH, BLOCK):
+            rows = slice(start, start + BLOCK)
             cosine, sine = turns(table[rows, :])
             pulled = (query_sum[rows, columns] if head < 2 else key_sum[rows, :]) * SCALE
             pulled = pulled.astype(jnp.bfloat16).astype(jnp.float32)
@@ -284,8 +294,8 @@
     for relative in range(Z):
         for color in range(2):
             place = (2 * (z ^ relative) + (x_hi ^ color)) * ROWS
-            begin = (2 * relative + color) * ROWS
-            turned[begin : begin + ROWS, :] = back[pl.ds(pl.multiple_of(place, ROWS), ROWS), :]
+            goal = (2 * relative + color) * ROWS
+            turned[goal : goal + ROWS, :] = back[pl.ds(pl.multiple_of(place, ROWS), ROWS), :]
     send_order(contract(turned[...], weight[...]), first_0, first_1, passed, own)
     for values in (first_0, first_1, passed, own):
         values.send()
@@ -296,12 +306,12 @@
     lane = lax.broadcasted_iota(jnp.int32, (OWN, HEAD), 1)
     line = lax.broadcasted_iota(jnp.int32, (OWN, HEAD), 0)
     each = HEAD // N_FSDP
-    for begin in range(0, D, BLOCK):
-        goal = slice(begin, begin + BLOCK)
+    for start in range(0, D, BLOCK):
+        goal = slice(start, start + BLOCK)
         attn = outer_rows(normed[:, goal], back[...]).astype(jnp.bfloat16)
         output = outer_rows(proj[:, goal], mixed[...]).astype(jnp.bfloat16)
         for part in range(BLOCK // OWN):
-            owner = begin // OWN + part
+            owner = start // OWN + part
             query_gain = pltpu.roll(gain_grads[0:1, :], (HEAD - each * owner) % HEAD, 1)
             key_gain = pltpu.roll(gain_grads[1:2, :], (HEAD + each - each * owner) % HEAD, 1)
             head_gains = jnp.where(lane < each, query_gain, key_gain)
@@ -320,11 +330,10 @@
         copy.wait()
 
 
-def out_kernel(mixed, tokens, gains, later, hidden, upper, lower, rows, weights, arrived):
-    whole = fetch(later, weights, arrived, [(0, 2 * D)])
+def out_kernel(mixed, tokens, gains, weights, hidden, upper, lower, rows):
     for head in range(N_SEQ):
         rows[:, head * 2 * HEAD : (head + 1) * 2 * HEAD] = mixed[head]
-    values = tokens[...].astype(jnp.float32) + contract(rows[...], whole[0]()[...])
+    values = tokens[...].astype(jnp.float32) + contract(rows[...], weights[...])
     hidden[...] = values
     values = (values * inverse_norm(values) * gains[1:2, :]).astype(jnp.bfloat16)
     upper[...] = values[: ROWS // 2]
@@ -332,10 +341,9 @@
 
 
 def mid_kernel(
-    own, got_0, got_1, last_0, last_1, hidden, incoming, gains, later,
-    hidden_grad, upper, lower, mixed_grad, weights, arrived,
+    own, got_0, got_1, last_0, last_1, hidden, incoming, gains, weights,
+    hidden_grad, upper, lower, mixed_grad,
 ):
-    parts = fetch(later, weights, arrived, [(i * 2 * HEAD, 2 * HEAD) for i in range(N_SEQ)])
     half = ROWS // 2
     total_0 = own[:half, :] + got_0[...].astype(jnp.float32) + last_0[...].astype(jnp.float32)
     total_1 = own[half:, :] + got_1[...].astype(jnp.float32) + last_1[...].astype(jnp.float32)
@@ -349,7 +357,7 @@
     upper[...] = grad[:half]
     lower[...] = grad[half:]
     for head in range(N_SEQ):
-        mixed_grad[head] = product(grad, parts[head]()[...]).astype(jnp.bfloat16)
+        mixed_grad[head] = product(grad, weights[:, head * 2 * HEAD : (head + 1) * 2 * HEAD]).astype(jnp.bfloat16)
 
 
 def ordered(pieces, place):
@@ -377,22 +385,18 @@
 
 
 def mlp_kernel(
-    n0, n1, n2, n3, n4, n5, c0, c1, c2, c3, c4, c5, later,
+    n0, n1, n2, n3, n4, n5, c0, c1, c2, c3, c4, c5, weights,
     first_0, first_1, passed, own, share, down_0, down_1, down_passed, down_own,
-    weights, arrived, rows, incoming, both_grad, inner,
+    rows, incoming, both_grad, inner,
 ):
-    steps = range(0, FF_Z, BLOCK)
-    parts = fetch(
-        later, weights, arrived,
-        [(i * FF_Z + begin, BLOCK) for begin in steps for i in range(3)], 2 * D,
-    )
     ordered((n0, n1, n2, n3, n4, n5), rows)
     ordered((c0, c1, c2, c3, c4, c5), incoming)
-    for i, begin in enumerate(steps):
-        columns, second = slice(begin, begin + BLOCK), slice(FF_Z + begin, FF_Z + begin + BLOCK)
-        gate = product(rows[...], parts[3 * i]()[...])
-        up = product(rows[...], parts[3 * i + 1]()[...])
-        inner_grad = product(incoming[...], parts[3 * i + 2]()[...])
+    for first in range(0, FF_Z, BLOCK):
+        columns, second = slice(first, first + BLOCK), slice(FF_Z + first, FF_Z + first + BLOCK)
+        third = slice(2 * FF_Z + first, 2 * FF_Z + first + BLOCK)
+        gate = product(rows[...], weights[:, columns])
+        up = product(rows[...], weights[:, second])
+        inner_grad = product(incoming[...], weights[:, third])
         sigmoid = jax.nn.sigmoid(gate)
         swish = gate * sigmoid
         inner[:, columns] = (swish * up).astype(jnp.bfloat16)
@@ -403,14 +407,16 @@
     send_order(contract(both_grad[...], weights[:, : 2 * FF_Z]), first_0, first_1, passed, own)
     for values in (first_0, first_1, passed, own):
         values.send()
-    for begin in range(0, D, BLOCK):
-        goal = slice(begin, begin + BLOCK)
+    send_order(
+        contract(inner[...], weights[:, 2 * FF_Z :]), down_0, down_1, down_passed, down_own
+    )
+    for values in (down_0, down_1, down_passed, down_own):
+        values.send()
+    for first in range(0, D, BLOCK):
+        goal = slice(first, first + BLOCK)
         share[goal, : 2 * FF_Z] = outer_rows(rows[:, goal], both_grad[...]).astype(jnp.bfloat16)
         share[goal, 2 * FF_Z :] = outer_rows(incoming[:, goal], inner[...]).astype(jnp.bfloat16)
         share.send(goal)
-    send_order(
-        contract(inner[...], weights[:, 2 * FF_Z :]), down_0, down_1, down_passed, down_own
-    )
 
 
 def weighed(*pairs):
@@ -427,21 +433,9 @@
     return jnp.broadcast_to(column, (OWN, HEAD)).T[0:1, :]
 
 
-def last_mlp_kernel(mlp, w_gate, w_up, norm, gate, up, down_t, norm_grad):
-    for place in range(Z):
-        part = mlp[2 * place].astype(jnp.float32) + mlp[2 * place + 1].astype(jnp.float32)
-        columns = slice(place * FF_Z, (place + 1) * FF_Z)
-        gate[:, columns] = part[:, :FF_Z]
-        up[:, columns] = part[:, FF_Z : 2 * FF_Z]
-        down_t[:, columns] = part[:, 2 * FF_Z :]
-    for result in (gate, up, down_t):
-        result.send()
-    norm_grad[...] = as_row(weighed((gate, w_gate), (up, w_up)) / norm[...])
-
-
-def last_attn_kernel(
-    at, p0, p1, p2, p3, p4, p5, w_query, w_key, w_value, norm,
-    query, key, value, output_t, norm_grad, query_gain, key_gain,
+def last_kernel(
+    at, p0, p1, p2, p3, p4, p5, mlp, w_query, w_key, w_value, norm, w_gate, w_up, norm_post,
+    query, key, value, output_t, norm_grad, query_gain, key_gain, gate, up, down_t, post_grad,
 ):
     z, x_hi = at[0], at[1]
     pieces = (p0, p1, p2, p3, p4, p5)
@@ -468,22 +462,16 @@
         result.send()
     query_gain[...] = gain_total[0:1, :each]
     key_gain[...] = gain_total[0:1, each : 2 * each]
+    for place in range(Z):
+        part = mlp[place].astype(jnp.float32)
+        columns = slice(place * FF_Z, (place + 1) * FF_Z)
+        gate[:, columns] = part[:, :FF_Z]
+        up[:, columns] = part[:, FF_Z : 2 * FF_Z]
+        down_t[:, columns] = part[:, 2 * FF_Z :]
+    for result in (gate, up, down_t):
+        result.send()
     norm_grad[...] = as_row(weighed((query, w_query), (key, w_key), (value, w_value)) / norm[...])
-
-
-class Reading:
-    def __init__(self, copy, place):
-        self.copy, self.place, self.shape = copy, place, place.shape
-        copy.start()
-
-    def __getitem__(self, index):
-        return self()[index]
-
-    def __call__(self):
-        if self.copy is not None:
-            self.copy.wait()
-            self.copy = None
-        return self.place
+    post_grad[...] = as_row(weighed((gate, w_gate), (up, w_up)) / norm_post[...])
 
 
 class Writing:
@@ -503,39 +491,34 @@
         self.copies.append(copy)
 
 
-def fetch(source, place, arrived, parts, begin=0):
-    result = []
-    for i, (first, size) in enumerate(parts):
-        part = place.at[:, pl.ds(first, size)]
-        copy = pltpu.make_async_copy(source.at[:, pl.ds(begin + first, size)], part, arrived.at[i])
-        result.append(Reading(copy, part))
-    return result
-
-
-def kernel_call(kernel, inputs, outs, scratch=(), flops=0, raw=(), raw_outs=0):
-    modes = ["scalar" if x.ndim == 1 else "raw" if i in raw else "copy" for i, x in enumerate(inputs)]
-    n_in, n_out = len(inputs), len(outs)
-    buffers = [pltpu.VMEM(x.shape, x.dtype) for x, m in zip(inputs, modes) if m == "copy"]
-    out_buffers = [pltpu.VMEM(shape, dtype) for shape, dtype in outs[raw_outs:]]
-    n_sent = 24
+def kernel_call(kernel, inputs, outs, scratch=(), flops=0, cuts=None, raw_outs=0):
+    cuts = cuts or {}
+    n_in, n_out, n_sent = len(inputs), len(outs), 24
+
+    def shape(i):
+        return (inputs[i].shape[0], cuts[i][1]) if i in cuts else inputs[i].shape
+
+    copied = [i for i, x in enumerate(inputs) if x.ndim > 1]
+    buffers = [pltpu.VMEM(shape(i), inputs[i].dtype) for i in copied]
+    out_buffers = [pltpu.VMEM(size, dtype) for size, dtype in outs[raw_outs:]]
 
     def body(*refs):
         ins, results, rest = refs[:n_in], refs[n_in : n_in + n_out], refs[n_in + n_out :]
-        places, rest = iter(rest[: len(buffers)]), rest[len(buffers) :]
+        places, rest = rest[: len(buffers)], rest[len(buffers) :]
         out_places, rest = rest[: len(out_buffers)], rest[len(out_buffers) :]
         (arrived, sent), rest = rest[:2], rest[2:]
+        args, copies = list(ins), []
+        for i, place in zip(copied, places):
+            source = ins[i].at[:, pl.ds(*cuts[i])] if i in cuts else ins[i]
+            copies.append(pltpu.make_async_copy(source, place, arrived.at[i]))
+            args[i] = place
+        for copy in copies:
+            copy.start()
+        for copy in copies:
+            copy.wait()
         semaphores = iter([sent.at[i] for i in range(n_sent)])
-        args = []
-        for i, (ref, mode) in enumerate(zip(ins, modes)):
-            if mode == "copy":
-                place = next(places)
-                ref = Reading(pltpu.make_async_copy(ref, place, arrived.at[i]), place)
-            args.append(ref)
         writes = [Writing(p, g, semaphores) for p, g in zip(out_places, results[raw_outs:])]
         kernel(*args, *results[:raw_outs], *writes, *rest)
-        for read in args:
-            if isinstance(read, Reading):
-                read()
         for write in writes:
             if not write.copies:
                 write.send()
@@ -547,7 +530,7 @@
     return pl.pallas_call(
         body,
         out_shape=[jax.ShapeDtypeStruct(shape, dtype) for shape, dtype in outs],
-        in_specs=[scalars if m == "scalar" else anywhere for m in modes],
+        in_specs=[anywhere if x.ndim > 1 else scalars for x in inputs],
         out_specs=[anywhere] * n_out,
         scratch_shapes=[
             *buffers,
@@ -654,9 +637,6 @@
     mixed_tokens = lax.all_to_all(
         mixed.reshape(N_SEQ, ROWS, 2 * HEAD), "seq", split_axis=0, concat_axis=0, tiled=True
     )
-    turned = turned.reshape(2, Z * ROWS, 2 * HEAD)
-    mixed_mine, mixed_other = turned[0], swap_x_hi(turned[1])
-    mixed_tokens, mixed_other = lax.optimization_barrier((mixed_tokens, mixed_other))
     incoming = after(cotangent[0], mixed)
     cotangent_z = gather4(*halves(incoming), swap_z_a, swap_z_b)
     half_rows = ((ROWS // 2, D), bf16)
@@ -664,9 +644,9 @@
         out_kernel,
         (mixed_tokens, sequence, gains, later),
         (((ROWS, D), f32), half_rows, half_rows),
-        scratch=(((ROWS, 2 * D), bf16), ((D, 2 * D), bf16), pltpu.SemaphoreType.DMA((1,))),
+        scratch=(((ROWS, 2 * D), bf16),),
         flops=10**9,
-        raw=(3,),
+        cuts={3: (0, 2 * D)},
     )
     upper, lower = after((upper, lower), cotangent_z)
     normed_post_z = gather4(upper, lower, swap_z_a, swap_z_b)
@@ -676,40 +656,30 @@
         (*normed_post_z, *cotangent_z, later),
         (*sent, ((D, 3 * FF_Z), bf16), *sent),
         scratch=(
-            ((D, 3 * FF_Z), bf16),
-            pltpu.SemaphoreType.DMA((9,)),
             ((Z * ROWS, D), bf16),
             ((Z * ROWS, D), bf16),
             ((Z * ROWS, 2 * FF_Z), bf16),
             ((Z * ROWS, FF_Z), bf16),
         ),
         flops=8 * 10**9,
-        raw=(12,),
-    )
-    got_0, got_1, last_0, last_1 = scatter4(
-        first_0, first_1, *halves(passed), swap_z_a, swap_z_b
-    )
+        cuts={12: (2 * D, 3 * FF_Z)},
+    )
+    turned = after(turned, first_0).reshape(2, Z * ROWS, 2 * HEAD)
+    mixed_mine, mixed_other = turned[0], swap_x_hi(turned[1])
+    sums = scatter4(first_0, first_1, *halves(passed), swap_z_a, swap_z_b)
+    (got_0, got_1, last_0, last_1), mixed_other = lax.optimization_barrier((sums, mixed_other))
     mlp_share = lax.psum_scatter(mlp_share, "fsdp", scatter_dimension=0, tiled=True)
     hidden_grad, upper, lower, mixed_grad = kernel_call(
         mid_kernel,
         (own, got_0, got_1, last_0, last_1, hidden, cotangent[0], gains, later),
         (((ROWS, D), f32), half_rows, half_rows, ((N_SEQ, ROWS, 2 * HEAD), bf16)),
-        scratch=(((D, 2 * D), bf16), pltpu.SemaphoreType.DMA((8,))),
         flops=10**9,
-        raw=(8,),
+        cuts={8: (0, 2 * D)},
     )
     mixed_grad = lax.all_to_all(mixed_grad, "seq", split_axis=0, concat_axis=0, tiled=True)
-    down_got = []
-
-    def tie_down(*got):
-        down_got.extend(after(got, upper))
-        return down_got
-
-    down_parts = scatter4(down_0, down_1, *halves(down_passed), swap_z_a, swap_z_b, tie_down)
-    upper, lower = after((upper, lower), tuple(down_got))
     proj_grad_z = gather4(upper, lower, swap_z_a, swap_z_b)
-    result = hidden + jnp.concatenate(total4(*halves(down_own), *down_parts), axis=0)
-    result = result.astype(bf16)
+    down_0, down_1 = after((down_0, down_1), proj_grad_z)
+    down_got = swap_z_b(down_0), swap_z_a(down_1)
 
     share, share_sent, dx_0, dx_1, dx_passed, dx_own = kernel_call(
         back_kernel,
@@ -741,6 +711,7 @@
         flops=8 * 10**9,
         raw_outs=2,
     )
+    share, share_sent, dx_0, dx_1 = after((share, share_sent, dx_0, dx_1), down_got)
     share = share.reshape(D // 2, SHARE)
     other_share = swap_core(share_sent.reshape(D // 2, SHARE))
 
@@ -761,25 +732,25 @@
 
     def second(got, passed_0, passed_1, swap_a, swap_b):
         n = got[0].shape[0] // 2
-        last_0 = swap_a((passed_0 + got[0][n:].astype(f32)).astype(bf16))
-        last_1 = swap_b((passed_1 + got[1][n:].astype(f32)).astype(bf16))
-        return got[0][:n], got[1][:n], last_0, last_1
+        last_0 = swap_a((passed_0 + wide(got[0][n:])).astype(bf16))
+        last_1 = swap_b((passed_1 + wide(got[1][n:])).astype(bf16))
+        return *got, last_0, last_1
 
     share_parts = second(share_got, share_block(1, 0), share_block(3, 1), swap_y_a, swap_y_b)
     dx_parts = second(dx_got, *halves(dx_passed), swap_z_a, swap_z_b)
-    share_parts, dx_parts = lax.optimization_barrier((share_parts, dx_parts))
+    mlp_other = swap_x_hi(mlp_share)
+    share_parts, dx_parts, mlp_other = lax.optimization_barrier((share_parts, dx_parts, mlp_other))
+    mlp_pieces = gather_z((wide(mlp_share) + wide(mlp_other)).astype(bf16))
     share_0, share_1 = total4(share_block(0, 0), share_block(0, 1), *share_parts)
     share_0, share_1 = share_0.astype(bf16), share_1.astype(bf16)
     normed_grad, other_grad = total4(*halves(dx_own), *dx_parts)
     other_grad = other_grad.astype(bf16)
-    share_0, share_1, other_grad = lax.optimization_barrier((share_0, share_1, other_grad))
+    share_0, share_1 = lax.optimization_barrier((share_0, share_1))
     attn_share = (share_0.astype(f32) + swap_x_lo(share_1).astype(f32)).astype(bf16)
     other_attn = swap_x_hi(share_0).astype(f32) + swap_x_both(share_1).astype(f32)
     other_attn = other_attn.astype(bf16)
-    other_grad = swap_x_hi(other_grad)
-    attn_share, other_attn, other_grad = lax.optimization_barrier(
-        (attn_share, other_attn, other_grad)
-    )
+    attn_share, other_attn = lax.optimization_barrier((attn_share, other_attn))
+    other_grad = swap_x_hi(after(other_grad, attn_share))
     normed_grad = (normed_grad + other_grad.astype(f32)) * gains[0:1]
     widened = sequence.astype(f32)
     inverse = inverse_norm(widened)
@@ -789,12 +760,21 @@
     )
 
     last_pieces = gather4(attn_share, other_attn, swap_z_a, swap_z_b)
-    mlp_pieces = lax.all_gather(mlp_share, "seq", axis=0, tiled=False)
-
-    query_total, key_total, value_total, output_total, input_gain, query_gain, key_gain = kernel_call(
-        last_attn_kernel,
+    down_got = after(down_got, last_pieces[1])
+    down_parts = second(down_got, *halves(down_passed), swap_z_a, swap_z_b)
+    result = hidden + jnp.concatenate(total4(*halves(down_own), *down_parts), axis=0)
+    result = result.astype(bf16)
+
+    last_pieces = after(last_pieces, mlp_pieces)
+    (
+        query_total, key_total, value_total, output_total, input_gain, query_gain, key_gain,
+        gate_total, up_total, down_total, post_gain,
+    ) = kernel_call(
+        last_kernel,
         (
-            at, *last_pieces, w_query, w_key, w_value, norm_input.astype(f32).reshape(OWN, 1),
+            at, *last_pieces, mlp_pieces,
+            w_query, w_key, w_value, norm_input.astype(f32).reshape(OWN, 1),
+            w_gate, w_up, norm_post.astype(f32).reshape(OWN, 1),
         ),
         (
             ((OWN, 2 * D), f32),
@@ -804,12 +784,11 @@
             ((1, OWN), f32),
             ((1, HEAD // N_FSDP), f32),
             ((1, HEAD // N_FSDP), f32),
+            ((OWN, FF), f32),
+            ((OWN, FF), f32),
+            ((OWN, FF), f32),
+            ((1, OWN), f32),
         ),
-    )
-    gate_total, up_total, down_total, post_gain = kernel_call(
-        last_mlp_kernel,
-        (mlp_pieces, w_gate, w_up, norm_post.astype(f32).reshape(OWN, 1)),
-        (((OWN, FF), f32), ((OWN, FF), f32), ((OWN, FF), f32), ((1, OWN), f32)),
     )
     return (
         result[None],

time: 280 us -> 271 us (0.968)
  the two profiles are of different devices: /device:TPU:1 before, /device:TPU:0 now
where the time goes in v3:
time: 271 us; the launch traced here: 266 us
  starting transfers between devices  91 us (34%)
  waiting for transfers between devices  68.8 us (25%)
  Pallas kernels  53.1 us (20%)
  other arithmetic  22.4 us (8%)
  local copies, waits for them, and re-layouts  15.7 us (6%)
  between operations  14.8 us (5%)
    ppermute x51, starting transfers between devices, exchange(): return lax.ppermute(values, axis, [(i, i ^ bits) for i in range(size)])  75.6 us
    ppermute x51, waiting for transfers between devices, exchange(): return lax.ppermute(values, axis, [(i, i ^ bits) for i in range(size)])  64.9 us
    pallas_call x6, Pallas kernels, kernel_call(): pl.pallas_call(body, out_shape=[jax.ShapeDtypeStruct(shape, dtype) for sh...  53.1 us
    all_to_all x1, starting transfers between devices, per_device(): lax.all_to_all(mixed.reshape(N_SEQ, ROWS, 2 * HEAD), 'seq', split_axis=0,...  8.42 us
    unnamed x124, local copies, waits for them, and re-layouts  7.73 us
    all_to_all x1, starting transfers between devices, per_device(): lax.all_to_all(mixed_grad, 'seq', split_axis=0, concat_axis=0, tiled=True)  6.32 us
  transfers between devices with their start and end apart: 57, of which 27 were waited for; matrix products, arithmetic and copies ran while one was open for 10% of the time, Pallas kernels for 13%

profile of v3, /device:TPU:0, one launch (start us, length us, event | category | flops | bytes accessed | tf_op | source)
XLA Modules:
  0.0 265.9 jit_solution(7335464786348943347)
XLA Ops:
  9.2 1.8 pad_maximum_fusion
  13.8 1.7 collective-permute-start.2
  15.9 2.0 collective-permute-start.7
  17.9 3.0 %collective-permute-start.9 = (bf16[128,1024]{1,0:T(8,128)(2,1)S(1)}, bf16[128,1024]{1,0:T(8,128)(2,1)}, u32[]{:S(2)}, u32[]{:S(2)}) collective-permute-start(bf16[128,1024]{1,0:T(8,128)(2,1)S(1)} %bitcast.42), channel_id=1, source_target_pairs={{0,16},{16,0},{32,48},{48,32},{64,80},{80,64},{96,112},{112,96},{1... | collective-permute-start | bytes 786440 | tf_op jit(solution)/shard_map/ppermute | solution.py:59
  21.0 1.7 collective-permute-start.3
  22.7 2.2 collective-permute-start.5
  24.9 3.8 %collective-permute-start.8 = (bf16[256,1024]{1,0:T(8,128)(2,1)S(1)}, bf16[256,1024]{1,0:T(8,128)(2,1)S(1)}, u32[]{:S(2)}, u32[]{:S(2)}) collective-permute-start(bf16[256,1024]{1,0:T(8,128)(2,1)S(1)} %pad_maximum_fusion.1), channel_id=1, source_target_pairs={{0,96},{16,112},{32,64},{48,80},{64,32},{80,48},{96,0},{112,16},{1... | collective-permute-start | bytes 1572872 | tf_op jit(solution)/shard_map/ppermute | solution.py:59
  28.7 2.6 collective-permute-done.9.refs_10_
  31.3 1.8 collective-permute-start.10
  33.1 3.4 %collective-permute-start.4 = (bf16[320,512]{1,0:T(8,128)(2,1)S(1)}, bf16[320,512]{1,0:T(8,128)(2,1)S(1)}, u32[]{:S(2)}, u32[]{:S(2)}) collective-permute-start(bf16[320,512]{1,0:T(8,128)(2,1)S(1)} %pad_maximum_fusion.2), channel_id=1, source_target_pairs={{0,12},{1,13},{2,14},{3,15},{4,8},{5,9},{6,10},{7,11},{8,4},{9,5},... | collective-permute-start | bytes 983048 | tf_op jit(solution)/shard_map/ppermute | solution.py:59
  36.6 3.0 %collective-permute-start.11 = (bf16[128,1024]{1,0:T(8,128)(2,1)}, bf16[128,1024]{1,0:T(8,128)(2,1)S(1)}, u32[]{:S(2)}, u32[]{:S(2)}) collective-permute-start(bf16[128,1024]{1,0:T(8,128)(2,1)} %collective-permute-done.9.refs_10_), channel_id=1, source_target_pairs={{0,96},{16,112},{32,64},{48,80},{64,32},{80,48},{96,0},{112,16},{1... | collective-permute-start | bytes 786440 | tf_op jit(solution)/shard_map/ppermute | solution.py:59
  39.6 3.2 %collective-permute-start.12 = (bf16[128,1024]{1,0:T(8,128)(2,1)}, bf16[128,1024]{1,0:T(8,128)(2,1)}, u32[]{:S(2)}, u32[]{:S(2)}) collective-permute-start(bf16[128,1024]{1,0:T(8,128)(2,1)} %collective-permute-done.9.refs_10_), channel_id=1, source_target_pairs={{0,64},{16,80},{32,96},{48,112},{64,0},{80,16},{96,32},{112,48},{1... | collective-permute-start | bytes 786440 | tf_op jit(solution)/shard_map/ppermute | solution.py:59
  43.4 1.2 convert_reduce_fusion
  44.6 6.2 %collective-permute-done.11.refs_12_ = bf16[128,1024]{1,0:T(8,128)(2,1)S(1)} collective-permute-done((bf16[128,1024]{1,0:T(8,128)(2,1)}, bf16[128,1024]{1,0:T(8,128)(2,1)S(1)}, u32[]{:S(2)}, u32[]{:S(2)}) %collective-permute-start.11) | collective-permute-done | bytes 262176 | tf_op jit(solution)/shard_map/ppermute | solution.py:59
  50.8 1.5 collective-permute-done.6.refs_6_
  53.3 10.7 %shard_map.246 = (bf16[2,4,128,256]{3,2,1,0:T(8,128)(2,1)}, bf16[1024,1024]{1,0:T(8,128)(2,1)}, f32[1024,384]{1,0:T(8,128)}, bf16[1024,512]{1,0:T(8,128)(2,1)}, ...) custom-call(s32[5]{0:T(128)} %stack.23.refs_0_, ...), custom_call_target="tpu_custom_call" | custom-call | flops 4000000000 | bytes 8388608 | tf_op jit(solution)/shard_map/pallas_call | solution.py:530
  64.6 8.4 %all-to-all-start = ((bf16[8,128,256]{2,1,0:T(8,128)(2,1)}), bf16[8,128,256]{2,1,0:T(8,128)(2,1)S(1)}, u32[]{:S(2)}, u32[]{:S(2)}) async-start(bf16[8,128,256]{2,1,0:T(8,128)(2,1)} %bitcast.51), calls=%async_computation | async-start | bytes 1048576 | tf_op jit(solution)/shard_map/all_to_all | solution.py:637
  73.1 3.2 %collective-permute-start.15 = (bf16[64,1024]{1,0:T(8,128)(2,1)S(1)}, bf16[64,1024]{1,0:T(8,128)(2,1)S(1)}, u32[]{:S(2)}, u32[]{:S(2)}) collective-permute-start(bf16[64,1024]{1,0:T(8,128)(2,1)S(1)} %get-tuple-element.199.refs_9_), channel_id=1, source_target_pairs={{0,96},{16,112},{32,64},{48,80},{64,32},{80,48},{96,0},{112,16},{1... | collective-permute-start | bytes 393224 | tf_op jit(solution)/shard_map/ppermute | solution.py:59
  76.5 6.3 %collective-permute-done.15.refs_10_ = bf16[64,1024]{1,0:T(8,128)(2,1)S(1)} collective-permute-done((bf16[64,1024]{1,0:T(8,128)(2,1)S(1)}, bf16[64,1024]{1,0:T(8,128)(2,1)S(1)}, u32[]{:S(2)}, u32[]{:S(2)}) %collective-permute-start.15) | collective-permute-done | bytes 131104 | tf_op jit(solution)/shard_map/ppermute | solution.py:59
  84.8 5.0 %shard_map.247 = (f32[128,1024]{1,0:T(8,128)}, bf16[64,1024]{1,0:T(8,128)(2,1)}, bf16[64,1024]{1,0:T(8,128)(2,1)}) custom-call(bf16[8,128,256]{2,1,0:T(8,128)(2,1)} %copy-done.4, bf16[128,1024]{1,0:T(8,128)(2,1)} %bitcast.40, f32[8,1024]{1,0:T(8,128)} %get-tuple-element.100.refs_2_.refs_7_, ...), custom_call_target="tpu_custom_call" | custom-call | flops 1000000000 | bytes 8388608 | tf_op jit(solution)/shard_map/pallas_call | solution.py:530
  90.9 2.2 collective-permute-start.19
  93.1 2.1 collective-permute-done.17.refs_1_
  96.1 2.4 collective-permute-start.18
  100.0 3.8 %collective-permute-done.18.refs_2_ = bf16[128,1024]{1,0:T(8,128)(2,1)S(1)} collective-permute-done((bf16[128,1024]{1,0:T(8,128)(2,1)S(1)}, bf16[128,1024]{1,0:T(8,128)(2,1)S(1)}, u32[]{:S(2)}, u32[]{:S(2)}) %collective-permute-start.18) | collective-permute-done | bytes 262176 | tf_op jit(solution)/shard_map/ppermute | solution.py:59
  103.8 2.4 collective-permute-done.20.refs_5_
  106.9 12.3 %shard_map.248 = (bf16[128,1024]{1,0:T(8,128)(2,1)}, bf16[128,1024]{1,0:T(8,128)(2,1)}, f32[128,1024]{1,0:T(8,128)}, f32[128,1024]{1,0:T(8,128)}, bf16[1024,2304...) custom-call(bf16[64,1024]{1,0:T(8,128)(2,1)} %get-tuple-element.105., ...), custom_call_target="tpu_custom_call" | custom-call | flops 8000000000 | bytes 8388608 | tf_op jit(solution)/shard_map/pallas_call | solution.py:530
  120.2 2.2 collective-permute-start.21
  123.2 2.8 %collective-permute-start.25 = (bf16[512,256]{1,0:T(8,128)(2,1)S(1)}, bf16[512,256]{1,0:T(8,128)(2,1)S(1)}, u32[]{:S(2)}, u32[]{:S(2)}) collective-permute-start(bf16[512,256]{1,0:T(8,128)(2,1)S(1)} %bitcast.54), channel_id=1, source_target_pairs={{0,16},{16,0},{32,48},{48,32},{64,80},{80,64},{96,112},{112,96},{1... | collective-permute-start | bytes 786440 | tf_op jit(solution)/shard_map/ppermute | solution.py:59
  126.0 3.2 %collective-permute-done.21 = bf16[128,1024]{1,0:T(8,128)(2,1)S(1)} collective-permute-done((bf16[128,1024]{1,0:T(8,128)(2,1)S(1)}, bf16[128,1024]{1,0:T(8,128)(2,1)S(1)}, u32[]{:S(2)}, u32[]{:S(2)}) %collective-permute-start.21) | collective-permute-done | bytes 262176 | tf_op jit(solution)/shard_map/ppermute | solution.py:59
  129.4 2.0 collective-permute-start.24
  134.3 1.3 collective-permute-done.24.refs_4_
  136.3 4.8 %shard_map.249 = (f32[128,1024]{1,0:T(8,128)}, bf16[64,1024]{1,0:T(8,128)(2,1)}, bf16[64,1024]{1,0:T(8,128)(2,1)}, bf16[8,128,256]{2,1,0:T(8,128)(2,1)}) custom-call(f32[128,1024]{1,0:T(8,128)} %get-tuple-element.110.refs_0_, bf16[64,1024]{1,0:T(8,128)(2,1)} %slice.190.refs_1_, bf16[64,1024]{1,0:T(8,128)(2,1)} %slice.191.refs_2_, ...), custom_call_target="tpu_custom_call" | custom-call | flops 1000000000 | bytes 8388608 | tf_op jit(solution)/shard_map/pallas_call | solution.py:530
  142.2 1.6 collective-permute-start.28
  143.9 6.3 %all-to-all-start.1 = ((bf16[8,128,256]{2,1,0:T(8,128)(2,1)}), bf16[8,128,256]{2,1,0:T(8,128)(2,1)S(1)}, u32[]{:S(2)}, u32[]{:S(2)}) async-start(bf16[8,128,256]{2,1,0:T(8,128)(2,1)} %get-tuple-element.125), calls=%async_computation.1 | async-start | bytes 1048576 | tf_op jit(solution)/shard_map/all_to_all | solution.py:679
  151.2 3.3 %collective-permute-start.27 = (bf16[128,1024]{1,0:T(8,128)(2,1)S(1)}, bf16[128,1024]{1,0:T(8,128)(2,1)S(1)}, u32[]{:S(2)}, u32[]{:S(2)}) collective-permute-start(bf16[128,1024]{1,0:T(8,128)(2,1)S(1)} %pad_maximum_fusion.12), channel_id=1, source_target_pairs={{0,96},{16,112},{32,64},{48,80},{64,32},{80,48},{96,0},{112,16},{1... | collective-permute-start | bytes 786440 | tf_op jit(solution)/shard_map/ppermute | solution.py:59
  154.8 7.8 %collective-permute-done.27.refs_14_ = bf16[128,1024]{1,0:T(8,128)(2,1)S(1)} collective-permute-done((bf16[128,1024]{1,0:T(8,128)(2,1)S(1)}, bf16[128,1024]{1,0:T(8,128)(2,1)S(1)}, u32[]{:S(2)}, u32[]{:S(2)}) %collective-permute-start.27) | collective-permute-done | bytes 262176 | tf_op jit(solution)/shard_map/ppermute | solution.py:59
  163.8 1.4 collective-permute-start.30
  166.7 15.0 %shard_map.250 = (bf16[4,2,64,1152]{3,2,1,0:T(8,128)(2,1)}, bf16[4,2,64,1152]{3,2,1,0:T(8,128)(2,1)}, bf16[256,1024]{1,0:T(8,128)(2,1)}, bf16[256,1024]{1,0:T(8,...) custom-call(s32[5]{0:T(128)} %stack.23.refs_0_, bf16[1024,512]{1,0:T(8,128)(2,1)} %get-tuple-element.124.refs_1_, ...), custom_call_target="tpu_custom_call" | custom-call | flops 8000000000 | bytes 8388608 | tf_op jit(solution)/shard_map/pallas_call | solution.py:530
  183.1 1.6 collective-permute-start.33
  184.7 1.4 collective-permute-start.34
  186.1 1.3 add_convert_fusion.11
  189.3 1.3 collective-permute-start.36
  191.4 7.5 %collective-permute-done.33 = bf16[256,1024]{1,0:T(8,128)(2,1)S(1)} collective-permute-done((bf16[256,1024]{1,0:T(8,128)(2,1)}, bf16[256,1024]{1,0:T(8,128)(2,1)S(1)}, u32[]{:S(2)}, u32[]{:S(2)}) %collective-permute-start.33) | collective-permute-done | bytes 524320 | tf_op jit(solution)/shard_map/ppermute | solution.py:59
  199.3 2.2 add_convert_fusion.2
  201.6 1.4 collective-permute-start.39
  202.9 1.9 collective-permute-start.40
  204.8 2.1 collective-permute-start.41
  208.1 1.3 collective-permute-start.37
  209.3 1.3 collective-permute-start.38
  211.4 1.9 collective-permute-done.37
  213.3 2.6 collective-permute-done.38
  215.9 1.8 add_convert_fusion.6
  219.1 2.7 %collective-permute-start.43 = (bf16[64,1152]{1,0:T(8,128)(2,1)}, bf16[64,1152]{1,0:T(8,128)(2,1)}, u32[]{:S(2)}, u32[]{:S(2)}) collective-permute-start(bf16[64,1152]{1,0:T(8,128)(2,1)} %get-tuple-element.149), channel_id=1, source_target_pairs={{0,16},{16,0},{32,48},{48,32},{64,80},{80,64},{96,112},{112,96},{1... | collective-permute-start | bytes 442376 | tf_op jit(solution)/shard_map/ppermute | solution.py:59
  224.3 2.4 collective-permute-done.44
  228.9 2.1 collective-permute-start.48
  231.1 1.4 collective-permute-start.50
  232.4 4.7 %collective-permute-done.45.refs_2_ = bf16[64,1152]{1,0:T(8,128)(2,1)S(1)} collective-permute-done((bf16[64,1152]{1,0:T(8,128)(2,1)S(1)}, bf16[64,1152]{1,0:T(8,128)(2,1)S(1)}, u32[]{:S(2)}, u32[]{:S(2)}) %collective-permute-start.45) | collective-permute-done | bytes 147488 | tf_op jit(solution)/shard_map/ppermute | solution.py:59
  237.5 3.3 %collective-permute-start.49 = (bf16[128,1152]{1,0:T(8,128)(2,1)S(1)}, bf16[128,1152]{1,0:T(8,128)(2,1)S(1)}, u32[]{:S(2)}, u32[]{:S(2)}) collective-permute-start(bf16[128,1152]{1,0:T(8,128)(2,1)S(1)} %pad_maximum_fusion.6), channel_id=1, source_target_pairs={{0,96},{16,112},{32,64},{48,80},{64,32},{80,48},{96,0},{112,16},{1... | collective-permute-start | bytes 884744 | tf_op jit(solution)/shard_map/ppermute | solution.py:59
  240.8 1.3 collective-permute-done.50.refs_5_
  243.0 1.2 fusion.2
  244.3 2.1 fusion.6
  246.5 1.3 collective-permute-done.47
  248.6 4.4 %collective-permute-done.49.refs_3_ = bf16[128,1152]{1,0:T(8,128)(2,1)S(1)} collective-permute-done((bf16[128,1152]{1,0:T(8,128)(2,1)S(1)}, bf16[128,1152]{1,0:T(8,128)(2,1)S(1)}, u32[]{:S(2)}, u32[]{:S(2)}) %collective-permute-start.49) | collective-permute-done | bytes 294944 | tf_op jit(solution)/shard_map/ppermute | solution.py:59
  253.8 5.3 %shard_map.251 = (f32[64,2048]{1,0:T(8,128)}, f32[64,1024]{1,0:T(8,128)}, f32[64,1024]{1,0:T(8,128)}, f32[64,2048]{1,0:T(8,128)}, f32[1,64]{1,0:T(1,128)}, /*ind...) custom-call(s32[5]{0:T(128)} %stack.23.refs_0_, ...), custom_call_target="tpu_custom_call" | custom-call | bytes 8388608 | tf_op jit(solution)/shard_map/pallas_call | solution.py:530
  (246 shorter events, 39.8 us)
Async XLA Ops:
  7.2 76.7 %all-gather.4.cloned.1.call-start = ((), (), s32[]{:S(2)}) async-start(), calls=%async_computation.3 | async-start | bytes 9469952 | tf_op jit(solution)/shard_map/all_gather | solution.py:617
  13.7 7.3 %collective-permute-start = (bf16[80,512]{1,0:T(8,128)(2,1)S(1)}, bf16[80,512]{1,0:T(8,128)(2,1)S(1)}, u32[]{:S(2)}, u32[]{:S(2)}) collective-permute-start(bf16[80,512]{1,0:T(8,128)(2,1)S(1)} %fusion.11), channel_id=1, source_target_pairs={{0,1},{1,0},{2,3},{3,2},{4,5},{5,4},{6,7},{7,6},{8,9},{9,8},{10,11... | collective-permute-start | bytes 245768 | tf_op jit(solution)/shard_map/ppermute | solution.py:59
  13.8 7.2 %collective-permute-start.2 = (bf16[80,512]{1,0:T(8,128)(2,1)S(1)}, bf16[80,512]{1,0:T(8,128)(2,1)S(1)}, u32[]{:S(2)}, u32[]{:S(2)}) collective-permute-start(bf16[80,512]{1,0:T(8,128)(2,1)S(1)} %fusion.11), channel_id=1, source_target_pairs={{0,3},{1,2},{2,1},{3,0},{4,7},{5,6},{6,5},{7,4},{8,11},{9,10},{10,... | collective-permute-start | bytes 245768 | tf_op jit(solution)/shard_map/ppermute | solution.py:59
  15.5 5.5 %collective-permute-start.1 = (bf16[80,512]{1,0:T(8,128)(2,1)S(1)}, bf16[80,512]{1,0:T(8,128)(2,1)S(1)}, u32[]{:S(2)}, u32[]{:S(2)}) collective-permute-start(bf16[80,512]{1,0:T(8,128)(2,1)S(1)} %fusion.11), channel_id=1, source_target_pairs={{0,2},{1,3},{2,0},{3,1},{4,6},{5,7},{6,4},{7,5},{8,10},{9,11},{10,... | collective-permute-start | bytes 245768 | tf_op jit(solution)/shard_map/ppermute | solution.py:59
  15.9 9.0 %collective-permute-start.7 = (bf16[128,1024]{1,0:T(8,128)(2,1)S(1)}, bf16[128,1024]{1,0:T(8,128)(2,1)S(1)}, u32[]{:S(2)}, u32[]{:S(2)}) collective-permute-start(bf16[128,1024]{1,0:T(8,128)(2,1)S(1)} %bitcast.41), channel_id=1, source_target_pairs={{0,32},{16,48},{32,0},{48,16},{64,96},{80,112},{96,64},{112,80},{1... | collective-permute-start | bytes 786440 | tf_op jit(solution)/shard_map/ppermute | solution.py:59
  17.9 13.4 %collective-permute-start.9 = (bf16[128,1024]{1,0:T(8,128)(2,1)S(1)}, bf16[128,1024]{1,0:T(8,128)(2,1)}, u32[]{:S(2)}, u32[]{:S(2)}) collective-permute-start(bf16[128,1024]{1,0:T(8,128)(2,1)S(1)} %bitcast.42), channel_id=1, source_target_pairs={{0,16},{16,0},{32,48},{48,32},{64,80},{80,64},{96,112},{112,96},{1... | collective-permute-start | bytes 786440 | tf_op jit(solution)/shard_map/ppermute | solution.py:59
  21.0 22.4 %copy-start.41 = (s32[1,1024]{1,0:T(1,128)S(1)}, s32[1,1024]{1,0:T(1,128)}, u32[]{:S(2)}) copy-start(s32[1,1024]{1,0:T(1,128)} %param.16) | copy-start | bytes 12292
  21.0 12.1 %collective-permute-start.3 = (bf16[160,512]{1,0:T(8,128)(2,1)S(1)}, bf16[160,512]{1,0:T(8,128)(2,1)S(1)}, u32[]{:S(2)}, u32[]{:S(2)}) collective-permute-start(bf16[160,512]{1,0:T(8,128)(2,1)S(1)} %pad_maximum_fusion.14.refs_1_), channel_id=1, source_target_pairs={{0,4},{1,5},{2,6},{3,7},{4,0},{5,1},{6,2},{7,3},{8,12},{9,13},{10,... | collective-permute-start | bytes 491528 | tf_op jit(solution)/shard_map/ppermute | solution.py:59
  22.7 13.8 %collective-permute-start.5 = (bf16[160,512]{1,0:T(8,128)(2,1)S(1)}, bf16[160,512]{1,0:T(8,128)(2,1)S(1)}, u32[]{:S(2)}, u32[]{:S(2)}) collective-permute-start(bf16[160,512]{1,0:T(8,128)(2,1)S(1)} %pad_maximum_fusion.15.refs_4_), channel_id=1, source_target_pairs={{0,12},{1,13},{2,14},{3,15},{4,8},{5,9},{6,10},{7,11},{8,4},{9,5},... | collective-permute-start | bytes 491528 | tf_op jit(solution)/shard_map/ppermute | solution.py:59
  24.9 27.5 %collective-permute-start.8 = (bf16[256,1024]{1,0:T(8,128)(2,1)S(1)}, bf16[256,1024]{1,0:T(8,128)(2,1)S(1)}, u32[]{:S(2)}, u32[]{:S(2)}) collective-permute-start(bf16[256,1024]{1,0:T(8,128)(2,1)S(1)} %pad_maximum_fusion.1), channel_id=1, source_target_pairs={{0,96},{16,112},{32,64},{48,80},{64,32},{80,48},{96,0},{112,16},{1... | collective-permute-start | bytes 1572872 | tf_op jit(solution)/shard_map/ppermute | solution.py:59
  31.3 8.3 %collective-permute-start.10 = (bf16[128,1024]{1,0:T(8,128)(2,1)}, bf16[128,1024]{1,0:T(8,128)(2,1)}, u32[]{:S(2)}, u32[]{:S(2)}) collective-permute-start(bf16[128,1024]{1,0:T(8,128)(2,1)} %collective-permute-done.9.refs_10_), channel_id=1, source_target_pairs={{0,32},{16,48},{32,0},{48,16},{64,96},{80,112},{96,64},{112,80},{1... | collective-permute-start | bytes 786440 | tf_op jit(solution)/shard_map/ppermute | solution.py:59
  33.1 19.3 %copy-start.30 = (bf16[160,512]{1,0:T(8,128)(2,1)}, bf16[160,512]{1,0:T(8,128)(2,1)S(1)}, u32[]{:S(2)}) copy-start(bf16[160,512]{1,0:T(8,128)(2,1)S(1)} %collective-permute-done.3.refs_2_) | copy-start | bytes 491524
  33.1 17.7 %collective-permute-start.4 = (bf16[320,512]{1,0:T(8,128)(2,1)S(1)}, bf16[320,512]{1,0:T(8,128)(2,1)S(1)}, u32[]{:S(2)}, u32[]{:S(2)}) collective-permute-start(bf16[320,512]{1,0:T(8,128)(2,1)S(1)} %pad_maximum_fusion.2), channel_id=1, source_target_pairs={{0,12},{1,13},{2,14},{3,15},{4,8},{5,9},{6,10},{7,11},{8,4},{9,5},... | collective-permute-start | bytes 983048 | tf_op jit(solution)/shard_map/ppermute | solution.py:59
  36.5 15.8 %collective-permute-start.6 = (bf16[320,512]{1,0:T(8,128)(2,1)S(1)}, bf16[320,512]{1,0:T(8,128)(2,1)S(1)}, u32[]{:S(2)}, u32[]{:S(2)}) collective-permute-start(bf16[320,512]{1,0:T(8,128)(2,1)S(1)} %pad_maximum_fusion.3), channel_id=1, source_target_pairs={{0,4},{1,5},{2,6},{3,7},{4,0},{5,1},{6,2},{7,3},{8,12},{9,13},{10,... | collective-permute-start | bytes 983048 | tf_op jit(solution)/shard_map/ppermute | solution.py:59
  36.6 14.2 %collective-permute-start.11 = (bf16[128,1024]{1,0:T(8,128)(2,1)}, bf16[128,1024]{1,0:T(8,128)(2,1)S(1)}, u32[]{:S(2)}, u32[]{:S(2)}) collective-permute-start(bf16[128,1024]{1,0:T(8,128)(2,1)} %collective-permute-done.9.refs_10_), channel_id=1, source_target_pairs={{0,96},{16,112},{32,64},{48,80},{64,32},{80,48},{96,0},{112,16},{1... | collective-permute-start | bytes 786440 | tf_op jit(solution)/shard_map/ppermute | solution.py:59
  39.6 11.2 %collective-permute-start.12 = (bf16[128,1024]{1,0:T(8,128)(2,1)}, bf16[128,1024]{1,0:T(8,128)(2,1)}, u32[]{:S(2)}, u32[]{:S(2)}) collective-permute-start(bf16[128,1024]{1,0:T(8,128)(2,1)} %collective-permute-done.9.refs_10_), channel_id=1, source_target_pairs={{0,64},{16,80},{32,96},{48,112},{64,0},{80,16},{96,32},{112,48},{1... | collective-permute-start | bytes 786440 | tf_op jit(solution)/shard_map/ppermute | solution.py:59
  64.0 25.8 %copy-start.20 = (bf16[64,1024]{1,0:T(8,128)(2,1)}, bf16[64,1024]{1,0:T(8,128)(2,1)S(1)}, u32[]{:S(2)}) copy-start(bf16[64,1024]{1,0:T(8,128)(2,1)S(1)} %get-tuple-element.199.refs_9_) | copy-start | bytes 393220
  64.0 25.8 %copy-start.21 = (bf16[64,1024]{1,0:T(8,128)(2,1)}, bf16[64,1024]{1,0:T(8,128)(2,1)S(1)}, u32[]{:S(2)}) copy-start(bf16[64,1024]{1,0:T(8,128)(2,1)S(1)} %get-tuple-element.200.refs_6_) | copy-start | bytes 393220
  64.0 12.3 %collective-permute-start.13 = (bf16[64,1024]{1,0:T(8,128)(2,1)S(1)}, bf16[64,1024]{1,0:T(8,128)(2,1)S(1)}, u32[]{:S(2)}, u32[]{:S(2)}) collective-permute-start(bf16[64,1024]{1,0:T(8,128)(2,1)S(1)} %get-tuple-element.200.refs_6_), channel_id=1, source_target_pairs={{0,32},{16,48},{32,0},{48,16},{64,96},{80,112},{96,64},{112,80},{1... | collective-permute-start | bytes 393224 | tf_op jit(solution)/shard_map/ppermute | solution.py:59
  64.6 19.4 %all-to-all-start = ((bf16[8,128,256]{2,1,0:T(8,128)(2,1)}), bf16[8,128,256]{2,1,0:T(8,128)(2,1)S(1)}, u32[]{:S(2)}, u32[]{:S(2)}) async-start(bf16[8,128,256]{2,1,0:T(8,128)(2,1)} %bitcast.51), calls=%async_computation | async-start | bytes 1048576 | tf_op jit(solution)/shard_map/all_to_all | solution.py:637
  73.0 131.8 %reduce-scatter.2.cloned.1.call-start = ((), (), s32[]{:S(2)}) async-start(), calls=%async_computation.4 | async-start | bytes 5013504 | tf_op jit(solution)/shard_map/reduce_scatter | solution.py:671
  73.1 9.7 %collective-permute-start.15 = (bf16[64,1024]{1,0:T(8,128)(2,1)S(1)}, bf16[64,1024]{1,0:T(8,128)(2,1)S(1)}, u32[]{:S(2)}, u32[]{:S(2)}) collective-permute-start(bf16[64,1024]{1,0:T(8,128)(2,1)S(1)} %get-tuple-element.199.refs_9_), channel_id=1, source_target_pairs={{0,96},{16,112},{32,64},{48,80},{64,32},{80,48},{96,0},{112,16},{1... | collective-permute-start | bytes 393224 | tf_op jit(solution)/shard_map/ppermute | solution.py:59
  76.3 13.6 %collective-permute-start.14 = (bf16[128,1024]{1,0:T(8,128)(2,1)S(1)}, bf16[128,1024]{1,0:T(8,128)(2,1)S(1)}, u32[]{:S(2)}, u32[]{:S(2)}) collective-permute-start(bf16[128,1024]{1,0:T(8,128)(2,1)S(1)} %pad_maximum_fusion.8), channel_id=1, source_target_pairs={{0,96},{16,112},{32,64},{48,80},{64,32},{80,48},{96,0},{112,16},{1... | collective-permute-start | bytes 786440 | tf_op jit(solution)/shard_map/ppermute | solution.py:59
  82.8 7.1 %collective-permute-start.16 = (bf16[128,1024]{1,0:T(8,128)(2,1)S(1)}, bf16[128,1024]{1,0:T(8,128)(2,1)S(1)}, u32[]{:S(2)}, u32[]{:S(2)}) collective-permute-start(bf16[128,1024]{1,0:T(8,128)(2,1)S(1)} %pad_maximum_fusion.9), channel_id=1, source_target_pairs={{0,32},{16,48},{32,0},{48,16},{64,96},{80,112},{96,64},{112,80},{1... | collective-permute-start | bytes 786440 | tf_op jit(solution)/shard_map/ppermute | solution.py:59
  89.9 5.3 %collective-permute-start.17 = (bf16[64,1024]{1,0:T(8,128)(2,1)}, bf16[64,1024]{1,0:T(8,128)(2,1)S(1)}, u32[]{:S(2)}, u32[]{:S(2)}) collective-permute-start(bf16[64,1024]{1,0:T(8,128)(2,1)} %get-tuple-element.105.refs_0_), channel_id=1, source_target_pairs={{0,32},{16,48},{32,0},{48,16},{64,96},{80,112},{96,64},{112,80},{1... | collective-permute-start | bytes 393224 | tf_op jit(solution)/shard_map/ppermute | solution.py:59
  90.9 7.7 %collective-permute-start.19 = (bf16[64,1024]{1,0:T(8,128)(2,1)}, bf16[64,1024]{1,0:T(8,128)(2,1)S(1)}, u32[]{:S(2)}, u32[]{:S(2)}) collective-permute-start(bf16[64,1024]{1,0:T(8,128)(2,1)} %get-tuple-element.106.refs_3_), channel_id=1, source_target_pairs={{0,96},{16,112},{32,64},{48,80},{64,32},{80,48},{96,0},{112,16},{1... | collective-permute-start | bytes 393224 | tf_op jit(solution)/shard_map/ppermute | solution.py:59
  96.1 7.7 %collective-permute-start.18 = (bf16[128,1024]{1,0:T(8,128)(2,1)S(1)}, bf16[128,1024]{1,0:T(8,128)(2,1)S(1)}, u32[]{:S(2)}, u32[]{:S(2)}) collective-permute-start(bf16[128,1024]{1,0:T(8,128)(2,1)S(1)} %pad_maximum_fusion.10), channel_id=1, source_target_pairs={{0,96},{16,112},{32,64},{48,80},{64,32},{80,48},{96,0},{112,16},{1... | collective-permute-start | bytes 786440 | tf_op jit(solution)/shard_map/ppermute | solution.py:59
  99.5 6.7 %collective-permute-start.20 = (bf16[128,1024]{1,0:T(8,128)(2,1)S(1)}, bf16[128,1024]{1,0:T(8,128)(2,1)S(1)}, u32[]{:S(2)}, u32[]{:S(2)}) collective-permute-start(bf16[128,1024]{1,0:T(8,128)(2,1)S(1)} %pad_maximum_fusion.11), channel_id=1, source_target_pairs={{0,32},{16,48},{32,0},{48,16},{64,96},{80,112},{96,64},{112,80},{1... | collective-permute-start | bytes 786440 | tf_op jit(solution)/shard_map/ppermute | solution.py:59
  120.2 9.0 %collective-permute-start.21 = (bf16[128,1024]{1,0:T(8,128)(2,1)S(1)}, bf16[128,1024]{1,0:T(8,128)(2,1)S(1)}, u32[]{:S(2)}, u32[]{:S(2)}) collective-permute-start(bf16[128,1024]{1,0:T(8,128)(2,1)S(1)} %copy-done.57), channel_id=1, source_target_pairs={{0,96},{16,112},{32,64},{48,80},{64,32},{80,48},{96,0},{112,16},{1... | collective-permute-start | bytes 786440 | tf_op jit(solution)/shard_map/ppermute | solution.py:59
  122.4 6.8 %collective-permute-start.22 = (bf16[128,1024]{1,0:T(8,128)(2,1)S(1)}, bf16[128,1024]{1,0:T(8,128)(2,1)S(1)}, u32[]{:S(2)}, u32[]{:S(2)}) collective-permute-start(bf16[128,1024]{1,0:T(8,128)(2,1)S(1)} %copy-done.56), channel_id=1, source_target_pairs={{0,32},{16,48},{32,0},{48,16},{64,96},{80,112},{96,64},{112,80},{1... | collective-permute-start | bytes 786440 | tf_op jit(solution)/shard_map/ppermute | solution.py:59
  123.2 10.6 %collective-permute-start.25 = (bf16[512,256]{1,0:T(8,128)(2,1)S(1)}, bf16[512,256]{1,0:T(8,128)(2,1)S(1)}, u32[]{:S(2)}, u32[]{:S(2)}) collective-permute-start(bf16[512,256]{1,0:T(8,128)(2,1)S(1)} %bitcast.54), channel_id=1, source_target_pairs={{0,16},{16,0},{32,48},{48,32},{64,80},{80,64},{96,112},{112,96},{1... | collective-permute-start | bytes 786440 | tf_op jit(solution)/shard_map/ppermute | solution.py:59
  129.3 5.0 %collective-permute-start.23 = (bf16[64,1024]{1,0:T(8,128)(2,1)S(1)}, bf16[64,1024]{1,0:T(8,128)(2,1)S(1)}, u32[]{:S(2)}, u32[]{:S(2)}) collective-permute-start(bf16[64,1024]{1,0:T(8,128)(2,1)S(1)} %get-tuple-element.198), channel_id=1, source_target_pairs={{0,32},{16,48},{32,0},{48,16},{64,96},{80,112},{96,64},{112,80},{1... | collective-permute-start | bytes 393224 | tf_op jit(solution)/shard_map/ppermute | solution.py:59
  129.4 6.3 %collective-permute-start.24 = (bf16[64,1024]{1,0:T(8,128)(2,1)S(1)}, bf16[64,1024]{1,0:T(8,128)(2,1)S(1)}, u32[]{:S(2)}, u32[]{:S(2)}) collective-permute-start(bf16[64,1024]{1,0:T(8,128)(2,1)S(1)} %get-tuple-element.197), channel_id=1, source_target_pairs={{0,96},{16,112},{32,64},{48,80},{64,32},{80,48},{96,0},{112,16},{1... | collective-permute-start | bytes 393224 | tf_op jit(solution)/shard_map/ppermute | solution.py:59
  141.2 22.6 %copy-start.50 = (bf16[128,1024]{1,0:T(8,128)(2,1)S(1)}, bf16[128,1024]{1,0:T(8,128)(2,1)}, u32[]{:S(2)}) copy-start(bf16[128,1024]{1,0:T(8,128)(2,1)} %get-tuple-element.122) | copy-start | bytes 786436
  141.2 24.0 %copy-start.49 = (bf16[128,1024]{1,0:T(8,128)(2,1)S(1)}, bf16[128,1024]{1,0:T(8,128)(2,1)}, u32[]{:S(2)}) copy-start(bf16[128,1024]{1,0:T(8,128)(2,1)} %get-tuple-element.123) | copy-start | bytes 786436
  141.2 9.0 %collective-permute-start.26 = (bf16[64,1024]{1,0:T(8,128)(2,1)}, bf16[64,1024]{1,0:T(8,128)(2,1)S(1)}, u32[]{:S(2)}, u32[]{:S(2)}) collective-permute-start(bf16[64,1024]{1,0:T(8,128)(2,1)} %get-tuple-element.120.refs_12_), channel_id=1, source_target_pairs={{0,32},{16,48},{32,0},{48,16},{64,96},{80,112},{96,64},{112,80},{1... | collective-permute-start | bytes 393224 | tf_op jit(solution)/shard_map/ppermute | solution.py:59
  142.2 12.3 %collective-permute-start.28 = (bf16[64,1024]{1,0:T(8,128)(2,1)}, bf16[64,1024]{1,0:T(8,128)(2,1)S(1)}, u32[]{:S(2)}, u32[]{:S(2)}) collective-permute-start(bf16[64,1024]{1,0:T(8,128)(2,1)} %get-tuple-element.121.refs_15_), channel_id=1, source_target_pairs={{0,96},{16,112},{32,64},{48,80},{64,32},{80,48},{96,0},{112,16},{1... | collective-permute-start | bytes 393224 | tf_op jit(solution)/shard_map/ppermute | solution.py:59
  143.9 22.0 %all-to-all-start.1 = ((bf16[8,128,256]{2,1,0:T(8,128)(2,1)}), bf16[8,128,256]{2,1,0:T(8,128)(2,1)S(1)}, u32[]{:S(2)}, u32[]{:S(2)}) async-start(bf16[8,128,256]{2,1,0:T(8,128)(2,1)} %get-tuple-element.125), calls=%async_computation.1 | async-start | bytes 1048576 | tf_op jit(solution)/shard_map/all_to_all | solution.py:679
  150.2 102.9 %all-gather.6.cloned.1.call-start = ((), (), s32[]{:S(2)}) async-start(), calls=%async_computation.5 | async-start | bytes 1474560 | tf_op jit(solution)/shard_map/all_gather | solution.py:95
  151.2 11.5 %collective-permute-start.27 = (bf16[128,1024]{1,0:T(8,128)(2,1)S(1)}, bf16[128,1024]{1,0:T(8,128)(2,1)S(1)}, u32[]{:S(2)}, u32[]{:S(2)}) collective-permute-start(bf16[128,1024]{1,0:T(8,128)(2,1)S(1)} %pad_maximum_fusion.12), channel_id=1, source_target_pairs={{0,96},{16,112},{32,64},{48,80},{64,32},{80,48},{96,0},{112,16},{1... | collective-permute-start | bytes 786440 | tf_op jit(solution)/shard_map/ppermute | solution.py:59
  154.5 9.2 %collective-permute-start.29 = (bf16[128,1024]{1,0:T(8,128)(2,1)S(1)}, bf16[128,1024]{1,0:T(8,128)(2,1)S(1)}, u32[]{:S(2)}, u32[]{:S(2)}) collective-permute-start(bf16[128,1024]{1,0:T(8,128)(2,1)S(1)} %pad_maximum_fusion.13), channel_id=1, source_target_pairs={{0,32},{16,48},{32,0},{48,16},{64,96},{80,112},{96,64},{112,80},{1... | collective-permute-start | bytes 786440 | tf_op jit(solution)/shard_map/ppermute | solution.py:59
  163.8 17.9 %collective-permute-start.30 = (bf16[128,1024]{1,0:T(8,128)(2,1)S(1)}, bf16[128,1024]{1,0:T(8,128)(2,1)S(1)}, u32[]{:S(2)}, u32[]{:S(2)}) collective-permute-start(bf16[128,1024]{1,0:T(8,128)(2,1)S(1)} %copy-done.50), channel_id=1, source_target_pairs={{0,96},{16,112},{32,64},{48,80},{64,32},{80,48},{96,0},{112,16},{1... | collective-permute-start | bytes 786440 | tf_op jit(solution)/shard_map/ppermute | solution.py:59
  165.1 16.5 %collective-permute-start.31 = (bf16[128,1024]{1,0:T(8,128)(2,1)S(1)}, bf16[128,1024]{1,0:T(8,128)(2,1)S(1)}, u32[]{:S(2)}, u32[]{:S(2)}) collective-permute-start(bf16[128,1024]{1,0:T(8,128)(2,1)S(1)} %copy-done.49), channel_id=1, source_target_pairs={{0,32},{16,48},{32,0},{48,16},{64,96},{80,112},{96,64},{112,80},{1... | collective-permute-start | bytes 786440 | tf_op jit(solution)/shard_map/ppermute | solution.py:59
  182.4 3.6 %collective-permute-start.32 = (bf16[512,1152]{1,0:T(8,128)(2,1)}, bf16[512,1152]{1,0:T(8,128)(2,1)S(1)}, u32[]{:S(2)}, u32[]{:S(2)}) collective-permute-start(bf16[512,1152]{1,0:T(8,128)(2,1)} %bitcast.60), channel_id=1, source_target_pairs={{0,1},{1,0},{2,3},{3,2},{4,5},{5,4},{6,7},{7,6},{8,9},{9,8},{10,11... | collective-permute-start | bytes 3538952 | tf_op jit(solution)/shard_map/ppermute | solution.py:59
  183.1 15.8 %collective-permute-start.33 = (bf16[256,1024]{1,0:T(8,128)(2,1)}, bf16[256,1024]{1,0:T(8,128)(2,1)S(1)}, u32[]{:S(2)}, u32[]{:S(2)}) collective-permute-start(bf16[256,1024]{1,0:T(8,128)(2,1)} %get-tuple-element.137), channel_id=1, source_target_pairs={{0,96},{16,112},{32,64},{48,80},{64,32},{80,48},{96,0},{112,16},{1... | collective-permute-start | bytes 1572872 | tf_op jit(solution)/shard_map/ppermute | solution.py:59
  184.7 14.4 %collective-permute-start.34 = (bf16[256,1024]{1,0:T(8,128)(2,1)}, bf16[256,1024]{1,0:T(8,128)(2,1)}, u32[]{:S(2)}, u32[]{:S(2)}) collective-permute-start(bf16[256,1024]{1,0:T(8,128)(2,1)} %get-tuple-element.138), channel_id=1, source_target_pairs={{0,32},{16,48},{32,0},{48,16},{64,96},{80,112},{96,64},{112,80},{1... | collective-permute-start | bytes 1572872 | tf_op jit(solution)/shard_map/ppermute | solution.py:59
  188.2 11.2 %collective-permute-start.35 = (bf16[128,1152]{1,0:T(8,128)(2,1)}, bf16[128,1152]{1,0:T(8,128)(2,1)}, u32[]{:S(2)}, u32[]{:S(2)}) collective-permute-start(bf16[128,1152]{1,0:T(8,128)(2,1)} %pad_maximum_fusion.4), channel_id=1, source_target_pairs={{0,12},{1,13},{2,14},{3,15},{4,8},{5,9},{6,10},{7,11},{8,4},{9,5},... | collective-permute-start | bytes 884744 | tf_op jit(solution)/shard_map/ppermute | solution.py:59
  189.3 10.0 %collective-permute-start.36 = (bf16[128,1152]{1,0:T(8,128)(2,1)}, bf16[128,1152]{1,0:T(8,128)(2,1)}, u32[]{:S(2)}, u32[]{:S(2)}) collective-permute-start(bf16[128,1152]{1,0:T(8,128)(2,1)} %pad_maximum_fusion.5), channel_id=1, source_target_pairs={{0,4},{1,5},{2,6},{3,7},{4,0},{5,1},{6,2},{7,3},{8,12},{9,13},{10,... | collective-permute-start | bytes 884744 | tf_op jit(solution)/shard_map/ppermute | solution.py:59
  201.6 14.3 %collective-permute-start.39 = (bf16[128,1024]{1,0:T(8,128)(2,1)}, bf16[128,1024]{1,0:T(8,128)(2,1)}, u32[]{:S(2)}, u32[]{:S(2)}) collective-permute-start(bf16[128,1024]{1,0:T(8,128)(2,1)} %get-tuple-element.190), channel_id=1, source_target_pairs={{0,32},{16,48},{32,0},{48,16},{64,96},{80,112},{96,64},{112,80},{1... | collective-permute-start | bytes 786440 | tf_op jit(solution)/shard_map/ppermute | solution.py:59
  202.9 12.9 %collective-permute-start.40 = (bf16[128,1024]{1,0:T(8,128)(2,1)}, bf16[128,1024]{1,0:T(8,128)(2,1)}, u32[]{:S(2)}, u32[]{:S(2)}) collective-permute-start(bf16[128,1024]{1,0:T(8,128)(2,1)} %get-tuple-element.189), channel_id=1, source_target_pairs={{0,96},{16,112},{32,64},{48,80},{64,32},{80,48},{96,0},{112,16},{1... | collective-permute-start | bytes 786440 | tf_op jit(solution)/shard_map/ppermute | solution.py:59
  204.8 17.0 %copy-start.22 = (bf16[64,2304]{1,0:T(8,128)(2,1)S(1)}, bf16[64,2304]{1,0:T(8,128)(2,1)}, u32[]{:S(2)}) copy-start(bf16[64,2304]{1,0:T(8,128)(2,1)} %reduce-scatter.2.cloned.1.call-done) | copy-start | bytes 884740
  204.8 11.0 %collective-permute-start.41 = (bf16[64,2304]{1,0:T(8,128)(2,1)}, bf16[64,2304]{1,0:T(8,128)(2,1)S(1)}, u32[]{:S(2)}, u32[]{:S(2)}) collective-permute-start(bf16[64,2304]{1,0:T(8,128)(2,1)} %reduce-scatter.2.cloned.1.call-done), channel_id=1, source_target_pairs={{0,16},{16,0},{32,48},{48,32},{64,80},{80,64},{96,112},{112,96},{1... | collective-permute-start | bytes 884744 | tf_op jit(solution)/shard_map/ppermute | solution.py:59
  208.1 5.2 %collective-permute-start.37 = (bf16[64,1152]{1,0:T(8,128)(2,1)S(1)}, bf16[64,1152]{1,0:T(8,128)(2,1)S(1)}, u32[]{:S(2)}, u32[]{:S(2)}) collective-permute-start(bf16[64,1152]{1,0:T(8,128)(2,1)S(1)} %get-tuple-element.184), channel_id=1, source_target_pairs={{0,4},{1,5},{2,6},{3,7},{4,0},{5,1},{6,2},{7,3},{8,12},{9,13},{10,... | collective-permute-start | bytes 442376 | tf_op jit(solution)/shard_map/ppermute | solution.py:59
  209.3 6.5 %collective-permute-start.38 = (bf16[64,1152]{1,0:T(8,128)(2,1)S(1)}, bf16[64,1152]{1,0:T(8,128)(2,1)S(1)}, u32[]{:S(2)}, u32[]{:S(2)}) collective-permute-start(bf16[64,1152]{1,0:T(8,128)(2,1)S(1)} %get-tuple-element.183), channel_id=1, source_target_pairs={{0,12},{1,13},{2,14},{3,15},{4,8},{5,9},{6,10},{7,11},{8,4},{9,5},... | collective-permute-start | bytes 442376 | tf_op jit(solution)/shard_map/ppermute | solution.py:59
  217.7 5.6 %collective-permute-start.42 = (bf16[64,1152]{1,0:T(8,128)(2,1)}, bf16[64,1152]{1,0:T(8,128)(2,1)}, u32[]{:S(2)}, u32[]{:S(2)}) collective-permute-start(bf16[64,1152]{1,0:T(8,128)(2,1)} %get-tuple-element.150), channel_id=1, source_target_pairs={{0,2},{1,3},{2,0},{3,1},{4,6},{5,7},{6,4},{7,5},{8,10},{9,11},{10,... | collective-permute-start | bytes 442376 | tf_op jit(solution)/shard_map/ppermute | solution.py:59
  218.5 8.1 %collective-permute-start.44 = (bf16[64,1152]{1,0:T(8,128)(2,1)}, bf16[64,1152]{1,0:T(8,128)(2,1)S(1)}, u32[]{:S(2)}, u32[]{:S(2)}) collective-permute-start(bf16[64,1152]{1,0:T(8,128)(2,1)} %get-tuple-element.150), channel_id=1, source_target_pairs={{0,18},{1,19},{2,16},{3,17},{4,22},{5,23},{6,20},{7,21},{8,26},{9,... | collective-permute-start | bytes 442376 | tf_op jit(solution)/shard_map/ppermute | solution.py:74
  219.1 7.6 %collective-permute-start.43 = (bf16[64,1152]{1,0:T(8,128)(2,1)}, bf16[64,1152]{1,0:T(8,128)(2,1)}, u32[]{:S(2)}, u32[]{:S(2)}) collective-permute-start(bf16[64,1152]{1,0:T(8,128)(2,1)} %get-tuple-element.149), channel_id=1, source_target_pairs={{0,16},{16,0},{32,48},{48,32},{64,80},{80,64},{96,112},{112,96},{1... | collective-permute-start | bytes 442376 | tf_op jit(solution)/shard_map/ppermute | solution.py:59
  227.7 9.5 %collective-permute-start.45 = (bf16[64,1152]{1,0:T(8,128)(2,1)S(1)}, bf16[64,1152]{1,0:T(8,128)(2,1)S(1)}, u32[]{:S(2)}, u32[]{:S(2)}) collective-permute-start(bf16[64,1152]{1,0:T(8,128)(2,1)S(1)} %add_convert_fusion.5.refs_1_), channel_id=1, source_target_pairs={{0,32},{16,48},{32,0},{48,16},{64,96},{80,112},{96,64},{112,80},{1... | collective-permute-start | bytes 442376 | tf_op jit(solution)/shard_map/ppermute | solution.py:59
  228.9 14.1 %collective-permute-start.48 = (bf16[128,1024]{1,0:T(8,128)(2,1)S(1)}, bf16[128,1024]{1,0:T(8,128)(2,1)S(1)}, u32[]{:S(2)}, u32[]{:S(2)}) collective-permute-start(bf16[128,1024]{1,0:T(8,128)(2,1)S(1)} %add_convert_fusion.1), channel_id=1, source_target_pairs={{0,16},{16,0},{32,48},{48,32},{64,80},{80,64},{96,112},{112,96},{1... | collective-permute-start | bytes 786440 | tf_op jit(solution)/shard_map/ppermute | solution.py:59
  231.1 11.1 %collective-permute-start.50 = (bf16[64,1152]{1,0:T(8,128)(2,1)S(1)}, bf16[64,1152]{1,0:T(8,128)(2,1)S(1)}, u32[]{:S(2)}, u32[]{:S(2)}) collective-permute-start(bf16[64,1152]{1,0:T(8,128)(2,1)S(1)} %add_convert_fusion.4.refs_4_), channel_id=1, source_target_pairs={{0,96},{16,112},{32,64},{48,80},{64,32},{80,48},{96,0},{112,16},{1... | collective-permute-start | bytes 442376 | tf_op jit(solution)/shard_map/ppermute | solution.py:59
  237.3 9.2 %collective-permute-start.46 = (bf16[64,1024]{1,0:T(8,128)(2,1)S(1)}, bf16[64,1024]{1,0:T(8,128)(2,1)S(1)}, u32[]{:S(2)}, u32[]{:S(2)}) collective-permute-start(bf16[64,1024]{1,0:T(8,128)(2,1)S(1)} %get-tuple-element.193), channel_id=1, source_target_pairs={{0,32},{16,48},{32,0},{48,16},{64,96},{80,112},{96,64},{112,80},{1... | collective-permute-start | bytes 393224 | tf_op jit(solution)/shard_map/ppermute | solution.py:59
  237.3 10.4 %collective-permute-start.47 = (bf16[64,1024]{1,0:T(8,128)(2,1)S(1)}, bf16[64,1024]{1,0:T(8,128)(2,1)S(1)}, u32[]{:S(2)}, u32[]{:S(2)}) collective-permute-start(bf16[64,1024]{1,0:T(8,128)(2,1)S(1)} %get-tuple-element.194), channel_id=1, source_target_pairs={{0,96},{16,112},{32,64},{48,80},{64,32},{80,48},{96,0},{112,16},{1... | collective-permute-start | bytes 393224 | tf_op jit(solution)/shard_map/ppermute | solution.py:59
  237.5 15.5 %collective-permute-start.49 = (bf16[128,1152]{1,0:T(8,128)(2,1)S(1)}, bf16[128,1152]{1,0:T(8,128)(2,1)S(1)}, u32[]{:S(2)}, u32[]{:S(2)}) collective-permute-start(bf16[128,1152]{1,0:T(8,128)(2,1)S(1)} %pad_maximum_fusion.6), channel_id=1, source_target_pairs={{0,96},{16,112},{32,64},{48,80},{64,32},{80,48},{96,0},{112,16},{1... | collective-permute-start | bytes 884744 | tf_op jit(solution)/shard_map/ppermute | solution.py:59
  242.1 10.9 %collective-permute-start.51 = (bf16[128,1152]{1,0:T(8,128)(2,1)S(1)}, bf16[128,1152]{1,0:T(8,128)(2,1)S(1)}, u32[]{:S(2)}, u32[]{:S(2)}) collective-permute-start(bf16[128,1152]{1,0:T(8,128)(2,1)S(1)} %pad_maximum_fusion.7), channel_id=1, source_target_pairs={{0,32},{16,48},{32,0},{48,16},{64,96},{80,112},{96,64},{112,80},{1... | collective-permute-start | bytes 884744 | tf_op jit(solution)/shard_map/ppermute | solution.py:59
  (54 other events, 379.8 us)
Sparse Core Ops, SparseCore 0:
  11.2 66.1 all-gather.3
  119.4 75.2 reduce-scatter.1
  222.7 28.2 all-gather.5

commit v4 on v3

--- a/solution.py
+++ b/solution.py
@@ -169,7 +169,7 @@
     turned, normed, raw, heads, mixed, log_total, gains, weight, value_t, arrived,
 ):
     z, x_hi, y, x_lo, core = at[0], at[1], at[2], at[3], at[4]
-    weights, tokens = (w0, w1, w2, w3, w4, w5), (x0, x1, x2, x3, x4, x5, x6)
+    weights = (w0, w1, w2, w3, w4, w5)
     extra = jnp.zeros((EXTRA, UNIT), jnp.float32)
     for array, step, relative, color in PIECES:
         for other in range(2):
@@ -184,6 +184,7 @@
     gains[0:1, :] = gain
     gains[1:2, :] = jnp.concatenate([extra[2:3], extra[3:4]], axis=1)
     gains[2:3, 0:UNIT] = extra[4:5]
+    table, *tokens = ready(table, x0, x1, x2, x3, x4, x5, x6)
     for array, step, relative, color in TOKEN_PIECES:
         values = tokens[array][step * ROWS : (step + 1) * ROWS, :].astype(jnp.float32)
         place = (2 * (z ^ relative) + (x_hi ^ color)) * ROWS
@@ -300,12 +301,16 @@
     for values in (first_0, first_1, passed, own):
         values.send()
     y, x_lo, core = at[2], at[3], at[4]
-    ordered((p0, p1, p2, p3, p4, p5), proj)
+    normed, mixed_mine, mixed_other, *pieces = ready(
+        normed, mixed_mine, mixed_other, p0, p1, p2, p3, p4, p5
+    )
+    ordered(pieces, proj)
     mixed[:, : 2 * HEAD] = mixed_mine[...]
     mixed[:, 2 * HEAD :] = mixed_other[...]
     lane = lax.broadcasted_iota(jnp.int32, (OWN, HEAD), 1)
     line = lax.broadcasted_iota(jnp.int32, (OWN, HEAD), 0)
     each = HEAD // N_FSDP
+    copies = []
     for start in range(0, D, BLOCK):
         goal = slice(start, start + BLOCK)
         attn = outer_rows(normed[:, goal], back[...]).astype(jnp.bfloat16)
@@ -321,11 +326,13 @@
             share[(*place, slice(None), slice(0, UNIT))] = attn[rows]
             share[(*place, slice(None), slice(UNIT, 2 * UNIT))] = output[rows]
             share[(*place, slice(None), slice(2 * UNIT, SHARE))] = head_gains.astype(jnp.bfloat16)
-    copies = [
-        pltpu.make_async_copy(share.at[i], goal, done.at[i]) for i, goal in ((1, theirs), (0, mine))
-    ]
-    for copy in copies:
-        copy.start()
+        which = (start // BLOCK) ^ y
+        for i, goal in ((1, theirs), (0, mine)):
+            copy = pltpu.make_async_copy(
+                share.at[i, which], goal.at[which], done.at[2 * (start // BLOCK) + i]
+            )
+            copy.start()
+            copies.append(copy)
     for copy in copies:
         copy.wait()
 
@@ -385,18 +392,19 @@
 
 
 def mlp_kernel(
-    n0, n1, n2, n3, n4, n5, c0, c1, c2, c3, c4, c5, weights,
+    n0, n1, n2, n3, n4, n5, c0, c1, c2, c3, c4, c5, weights, down_weights,
     first_0, first_1, passed, own, share, down_0, down_1, down_passed, down_own,
     rows, incoming, both_grad, inner,
 ):
     ordered((n0, n1, n2, n3, n4, n5), rows)
-    ordered((c0, c1, c2, c3, c4, c5), incoming)
     for first in range(0, FF_Z, BLOCK):
         columns, second = slice(first, first + BLOCK), slice(FF_Z + first, FF_Z + first + BLOCK)
-        third = slice(2 * FF_Z + first, 2 * FF_Z + first + BLOCK)
         gate = product(rows[...], weights[:, columns])
         up = product(rows[...], weights[:, second])
-        inner_grad = product(incoming[...], weights[:, third])
+        if first == 0:
+            down_weights, *pieces = ready(down_weights, c0, c1, c2, c3, c4, c5)
+            ordered(pieces, incoming)
+        inner_grad = product(incoming[...], down_weights[:, columns])
         sigmoid = jax.nn.sigmoid(gate)
         swish = gate * sigmoid
         inner[:, columns] = (swish * up).astype(jnp.bfloat16)
@@ -404,11 +412,11 @@
             inner_grad * up * sigmoid * (1.0 + gate * (1.0 - sigmoid))
         ).astype(jnp.bfloat16)
         both_grad[:, second] = (inner_grad * swish).astype(jnp.bfloat16)
-    send_order(contract(both_grad[...], weights[:, : 2 * FF_Z]), first_0, first_1, passed, own)
+    send_order(contract(both_grad[...], weights[...]), first_0, first_1, passed, own)
     for values in (first_0, first_1, passed, own):
         values.send()
     send_order(
-        contract(inner[...], weights[:, 2 * FF_Z :]), down_0, down_1, down_passed, down_own
+        contract(inner[...], down_weights[...]), down_0, down_1, down_passed, down_own
     )
     for values in (down_0, down_1, down_passed, down_own):
         values.send()
@@ -433,9 +441,21 @@
     return jnp.broadcast_to(column, (OWN, HEAD)).T[0:1, :]
 
 
+def last_mlp_kernel(mlp, w_gate, w_up, norm_post, gate, up, down_t, post_grad):
+    for place in range(Z):
+        part = mlp[place].astype(jnp.float32)
+        columns = slice(place * FF_Z, (place + 1) * FF_Z)
+        gate[:, columns] = part[:, :FF_Z]
+        up[:, columns] = part[:, FF_Z : 2 * FF_Z]
+        down_t[:, columns] = part[:, 2 * FF_Z :]
+    for result in (gate, up, down_t):
+        result.send()
+    post_grad[...] = as_row(weighed((gate, w_gate), (up, w_up)) / norm_post[...])
+
+
 def last_kernel(
-    at, p0, p1, p2, p3, p4, p5, mlp, w_query, w_key, w_value, norm, w_gate, w_up, norm_post,
-    query, key, value, output_t, norm_grad, query_gain, key_gain, gate, up, down_t, post_grad,
+    at, p0, p1, p2, p3, p4, p5, w_query, w_key, w_value, norm,
+    query, key, value, output_t, norm_grad, query_gain, key_gain,
 ):
     z, x_hi = at[0], at[1]
     pieces = (p0, p1, p2, p3, p4, p5)
@@ -462,16 +482,13 @@
         result.send()
     query_gain[...] = gain_total[0:1, :each]
     key_gain[...] = gain_total[0:1, each : 2 * each]
-    for place in range(Z):
-        part = mlp[place].astype(jnp.float32)
-        columns = slice(place * FF_Z, (place + 1) * FF_Z)
-        gate[:, columns] = part[:, :FF_Z]
-        up[:, columns] = part[:, FF_Z : 2 * FF_Z]
-        down_t[:, columns] = part[:, 2 * FF_Z :]
-    for result in (gate, up, down_t):
-        result.send()
     norm_grad[...] = as_row(weighed((query, w_query), (key, w_key), (value, w_value)) / norm[...])
-    post_grad[...] = as_row(weighed((gate, w_gate), (up, w_up)) / norm_post[...])
+
+
+def ready(*inputs):
+    for _, copy in inputs:
+        copy.wait()
+    return [place for place, _ in inputs]
 
 
 class Writing:
@@ -491,7 +508,7 @@
         self.copies.append(copy)
 
 
-def kernel_call(kernel, inputs, outs, scratch=(), flops=0, cuts=None, raw_outs=0):
+def kernel_call(kernel, inputs, outs, scratch=(), flops=0, cuts=None, raw_outs=0, late=()):
     cuts = cuts or {}
     n_in, n_out, n_sent = len(inputs), len(outs), 24
 
@@ -510,12 +527,14 @@
         args, copies = list(ins), []
         for i, place in zip(copied, places):
             source = ins[i].at[:, pl.ds(*cuts[i])] if i in cuts else ins[i]
-            copies.append(pltpu.make_async_copy(source, place, arrived.at[i]))
-            args[i] = place
-        for copy in copies:
+            copy = pltpu.make_async_copy(source, place, arrived.at[i])
+            copies.append((i in late, copy))
+            args[i] = (place, copy) if i in late else place
+        for _, copy in copies:
             copy.start()
-        for copy in copies:
-            copy.wait()
+        for waits_later, copy in copies:
+            if not waits_later:
+                copy.wait()
         semaphores = iter([sent.at[i] for i in range(n_sent)])
         writes = [Writing(p, g, semaphores) for p, g in zip(out_places, results[raw_outs:])]
         kernel(*args, *results[:raw_outs], *writes, *rest)
@@ -632,6 +651,7 @@
         scratch=(((HEAD, LENGTH), bf16), pltpu.SemaphoreType.DMA((8,))),
         flops=4 * 10**9,
         raw_outs=1,
+        late=range(7, 15),
     )
 
     mixed_tokens = lax.all_to_all(
@@ -653,7 +673,7 @@
     sent = (((ROWS, D), bf16), ((ROWS, D), bf16), ((ROWS, D), f32), ((ROWS, D), f32))
     first_0, first_1, passed, own, mlp_share, down_0, down_1, down_passed, down_own = kernel_call(
         mlp_kernel,
-        (*normed_post_z, *cotangent_z, later),
+        (*normed_post_z, *cotangent_z, later, later),
         (*sent, ((D, 3 * FF_Z), bf16), *sent),
         scratch=(
             ((Z * ROWS, D), bf16),
@@ -662,7 +682,8 @@
             ((Z * ROWS, FF_Z), bf16),
         ),
         flops=8 * 10**9,
-        cuts={12: (2 * D, 3 * FF_Z)},
+        cuts={12: (2 * D, 2 * FF_Z), 13: (2 * D + 2 * FF_Z, FF_Z)},
+        late=(6, 7, 8, 9, 10, 11, 13),
     )
     turned = after(turned, first_0).reshape(2, Z * ROWS, 2 * HEAD)
     mixed_mine, mixed_other = turned[0], swap_x_hi(turned[1])
@@ -706,10 +727,11 @@
             ((Z * ROWS, UNIT), bf16),
             ((2, Z, 2, OWN, SHARE), bf16),
             ((LENGTH, UNIT), bf16),
-            pltpu.SemaphoreType.DMA((2,)),
+            pltpu.SemaphoreType.DMA((8,)),
         ),
         flops=8 * 10**9,
         raw_outs=2,
+        late=range(9, 18),
     )
     share, share_sent, dx_0, dx_1 = after((share, share_sent, dx_0, dx_1), down_got)
     share = share.reshape(D // 2, SHARE)
@@ -728,7 +750,6 @@
         swap_y_b(share_pair((3, 0), (2, 0))),
         swap_y_a(share_pair((1, 1), (2, 1))),
     )
-    dx_got, share_got = lax.optimization_barrier((dx_got, share_got))
 
     def second(got, passed_0, passed_1, swap_a, swap_b):
         n = got[0].shape[0] // 2
@@ -737,20 +758,19 @@
         return *got, last_0, last_1
 
     share_parts = second(share_got, share_block(1, 0), share_block(3, 1), swap_y_a, swap_y_b)
-    dx_parts = second(dx_got, *halves(dx_passed), swap_z_a, swap_z_b)
     mlp_other = swap_x_hi(mlp_share)
-    share_parts, dx_parts, mlp_other = lax.optimization_barrier((share_parts, dx_parts, mlp_other))
+    share_parts, dx_got, mlp_other = lax.optimization_barrier((share_parts, dx_got, mlp_other))
     mlp_pieces = gather_z((wide(mlp_share) + wide(mlp_other)).astype(bf16))
     share_0, share_1 = total4(share_block(0, 0), share_block(0, 1), *share_parts)
     share_0, share_1 = share_0.astype(bf16), share_1.astype(bf16)
-    normed_grad, other_grad = total4(*halves(dx_own), *dx_parts)
-    other_grad = other_grad.astype(bf16)
     share_0, share_1 = lax.optimization_barrier((share_0, share_1))
     attn_share = (share_0.astype(f32) + swap_x_lo(share_1).astype(f32)).astype(bf16)
     other_attn = swap_x_hi(share_0).astype(f32) + swap_x_both(share_1).astype(f32)
     other_attn = other_attn.astype(bf16)
-    attn_share, other_attn = lax.optimization_barrier((attn_share, other_attn))
-    other_grad = swap_x_hi(after(other_grad, attn_share))
+    dx_parts = second(dx_got, *halves(dx_passed), swap_z_a, swap_z_b)
+    attn_share, other_attn, dx_parts = lax.optimization_barrier((attn_share, other_attn, dx_parts))
+    normed_grad, other_grad = total4(*halves(dx_own), *dx_parts)
+    other_grad = swap_x_hi(other_grad.astype(bf16))
     normed_grad = (normed_grad + other_grad.astype(f32)) * gains[0:1]
     widened = sequence.astype(f32)
     inverse = inverse_norm(widened)
@@ -760,21 +780,21 @@
     )
 
     last_pieces = gather4(attn_share, other_attn, swap_z_a, swap_z_b)
-    down_got = after(down_got, last_pieces[1])
+    down_got = after(down_got, other_grad)
     down_parts = second(down_got, *halves(down_passed), swap_z_a, swap_z_b)
     result = hidden + jnp.concatenate(total4(*halves(down_own), *down_parts), axis=0)
     result = result.astype(bf16)
 
-    last_pieces = after(last_pieces, mlp_pieces)
-    (
-        query_total, key_total, value_total, output_total, input_gain, query_gain, key_gain,
-        gate_total, up_total, down_total, post_gain,
-    ) = kernel_call(
+    gate_total, up_total, down_total, post_gain = kernel_call(
+        last_mlp_kernel,
+        (mlp_pieces, w_gate, w_up, norm_post.astype(f32).reshape(OWN, 1)),
+        (((OWN, FF), f32), ((OWN, FF), f32), ((OWN, FF), f32), ((1, OWN), f32)),
+    )
+    last_pieces = after(last_pieces, post_gain)
+    query_total, key_total, value_total, output_total, input_gain, query_gain, key_gain = kernel_call(
         last_kernel,
         (
-            at, *last_pieces, mlp_pieces,
-            w_query, w_key, w_value, norm_input.astype(f32).reshape(OWN, 1),
-            w_gate, w_up, norm_post.astype(f32).reshape(OWN, 1),
+            at, *last_pieces, w_query, w_key, w_value, norm_input.astype(f32).reshape(OWN, 1),
         ),
         (
             ((OWN, 2 * D), f32),
@@ -784,10 +804,6 @@
             ((1, OWN), f32),
             ((1, HEAD // N_FSDP), f32),
             ((1, HEAD // N_FSDP), f32),
-            ((OWN, FF), f32),
-            ((OWN, FF), f32),
-            ((OWN, FF), f32),
-            ((1, OWN), f32),
         ),
     )
     return (

time: 271 us -> 267 us (0.985)
  waiting for transfers between devices: 68.8 us -> 62 us
  starting transfers between devices: 91 us -> 95.4 us
    ppermute x51, waiting for transfers between devices: 64.9 us -> 59.4 us  [exchange(): return lax.ppermute(values, axis, [(i, i ^ bits) for i in range(size)])]
    ppermute x51, starting transfers between devices: 75.6 us -> 79.4 us  [exchange(): return lax.ppermute(values, axis, [(i, i ^ bits) for i in range(size)])]
    unnamed x124 -> x128, local copies, waits for them, and re-layouts: 7.73 us -> 8.41 us
    pallas_call x6 -> x7, Pallas kernels: 53.1 us -> 53.3 us  [kernel_call(): pl.pallas_call(body, out_shape=[jax.ShapeDtypeStruct(shape, dtype) for sh...]
  transfers between devices with their start and end apart: 57 -> 57, of which waited for: 27 -> 24; matrix products, arithmetic and copies ran while one was open for 10% -> 9% of each run, Pallas kernels for 13% -> 14%
where the time goes in v4:
time: 267 us; the launch traced here: 262 us
  starting transfers between devices  95.4 us (36%)
  waiting for transfers between devices  62 us (23%)
  Pallas kernels  53.3 us (20%)
  other arithmetic  20.4 us (8%)
  local copies, waits for them, and re-layouts  16.4 us (6%)
  between operations  14.9 us (6%)
    ppermute x51, starting transfers between devices, exchange(): return lax.ppermute(values, axis, [(i, i ^ bits) for i in range(size)])  79.4 us
    ppermute x51, waiting for transfers between devices, exchange(): return lax.ppermute(values, axis, [(i, i ^ bits) for i in range(size)])  59.4 us
    pallas_call x7, Pallas kernels, kernel_call(): pl.pallas_call(body, out_shape=[jax.ShapeDtypeStruct(shape, dtype) for sh...  53.3 us
    unnamed x128, local copies, waits for them, and re-layouts  8.41 us
    all_to_all x1, starting transfers between devices, per_device(): lax.all_to_all(mixed.reshape(N_SEQ, ROWS, 2 * HEAD), 'seq', split_axis=0,...  8.33 us
  transfers between devices with their start and end apart: 57, of which 24 were waited for; matrix products, arithmetic and copies ran while one was open for 9% of the time, Pallas kernels for 14%

profile of v4, /device:TPU:0, one launch (start us, length us, event | category | flops | bytes accessed | tf_op | source)
XLA Modules:
  0.0 262.3 jit_solution(1928604563639188812)
XLA Ops:
  9.2 1.8 pad_maximum_fusion
  13.8 1.7 collective-permute-start.2
  15.9 2.0 collective-permute-start.7
  17.9 3.0 %collective-permute-start.9 = (bf16[128,1024]{1,0:T(8,128)(2,1)S(1)}, bf16[128,1024]{1,0:T(8,128)(2,1)S(1)}, u32[]{:S(2)}, u32[]{:S(2)}) collective-permute-start(bf16[128,1024]{1,0:T(8,128)(2,1)S(1)} %bitcast.42), channel_id=1, source_target_pairs={{0,16},{16,0},{32,48},{48,32},{64,80},{80,64},{96,112},{112,96},{1... | collective-permute-start | bytes 786440 | tf_op jit(solution)/shard_map/ppermute | solution.py:59
  21.0 1.7 collective-permute-start.3
  22.7 2.2 collective-permute-start.5
  24.9 3.8 %collective-permute-start.8 = (bf16[256,1024]{1,0:T(8,128)(2,1)S(1)}, bf16[256,1024]{1,0:T(8,128)(2,1)S(1)}, u32[]{:S(2)}, u32[]{:S(2)}) collective-permute-start(bf16[256,1024]{1,0:T(8,128)(2,1)S(1)} %pad_maximum_fusion.1), channel_id=1, source_target_pairs={{0,96},{16,112},{32,64},{48,80},{64,32},{80,48},{96,0},{112,16},{1... | collective-permute-start | bytes 1572872 | tf_op jit(solution)/shard_map/ppermute | solution.py:59
  28.7 2.6 collective-permute-done.9.refs_10_
  31.3 1.7 collective-permute-start.10
  33.0 3.4 %collective-permute-start.4 = (bf16[320,512]{1,0:T(8,128)(2,1)S(1)}, bf16[320,512]{1,0:T(8,128)(2,1)S(1)}, u32[]{:S(2)}, u32[]{:S(2)}) collective-permute-start(bf16[320,512]{1,0:T(8,128)(2,1)S(1)} %pad_maximum_fusion.2), channel_id=1, source_target_pairs={{0,12},{1,13},{2,14},{3,15},{4,8},{5,9},{6,10},{7,11},{8,4},{9,5},... | collective-permute-start | bytes 983048 | tf_op jit(solution)/shard_map/ppermute | solution.py:59
  36.5 3.0 %collective-permute-start.11 = (bf16[128,1024]{1,0:T(8,128)(2,1)S(1)}, bf16[128,1024]{1,0:T(8,128)(2,1)}, u32[]{:S(2)}, u32[]{:S(2)}) collective-permute-start(bf16[128,1024]{1,0:T(8,128)(2,1)S(1)} %collective-permute-done.9.refs_10_), channel_id=1, source_target_pairs={{0,96},{16,112},{32,64},{48,80},{64,32},{80,48},{96,0},{112,16},{1... | collective-permute-start | bytes 786440 | tf_op jit(solution)/shard_map/ppermute | solution.py:59
  40.2 2.9 %collective-permute-start.12 = (bf16[128,1024]{1,0:T(8,128)(2,1)S(1)}, bf16[128,1024]{1,0:T(8,128)(2,1)}, u32[]{:S(2)}, u32[]{:S(2)}) collective-permute-start(bf16[128,1024]{1,0:T(8,128)(2,1)S(1)} %collective-permute-done.9.refs_10_), channel_id=1, source_target_pairs={{0,64},{16,80},{32,96},{48,112},{64,0},{80,16},{96,32},{112,48},{1... | collective-permute-start | bytes 786440 | tf_op jit(solution)/shard_map/ppermute | solution.py:59
  43.7 1.2 convert_reduce_fusion
  44.9 6.0 %collective-permute-done.11.refs_12_ = bf16[128,1024]{1,0:T(8,128)(2,1)} collective-permute-done((bf16[128,1024]{1,0:T(8,128)(2,1)S(1)}, bf16[128,1024]{1,0:T(8,128)(2,1)}, u32[]{:S(2)}, u32[]{:S(2)}) %collective-permute-start.11) | collective-permute-done | bytes 262176 | tf_op jit(solution)/shard_map/ppermute | solution.py:59
  50.9 1.4 collective-permute-done.6.refs_6_
  53.2 10.6 %shard_map.246 = (bf16[2,4,128,256]{3,2,1,0:T(8,128)(2,1)}, bf16[1024,1024]{1,0:T(8,128)(2,1)}, f32[1024,384]{1,0:T(8,128)}, bf16[1024,512]{1,0:T(8,128)(2,1)}, ...) custom-call(s32[5]{0:T(128)} %stack.23.refs_0_, ...), custom_call_target="tpu_custom_call" | custom-call | flops 4000000000 | bytes 8388608 | tf_op jit(solution)/shard_map/pallas_call | solution.py:549
  64.6 8.3 %all-to-all-start = ((bf16[8,128,256]{2,1,0:T(8,128)(2,1)}), bf16[8,128,256]{2,1,0:T(8,128)(2,1)S(1)}, u32[]{:S(2)}, u32[]{:S(2)}) async-start(bf16[8,128,256]{2,1,0:T(8,128)(2,1)} %bitcast.51), calls=%async_computation | async-start | bytes 1048576 | tf_op jit(solution)/shard_map/all_to_all | solution.py:657
  73.0 3.2 %collective-permute-start.15 = (bf16[64,1024]{1,0:T(8,128)(2,1)S(1)}, bf16[64,1024]{1,0:T(8,128)(2,1)S(1)}, u32[]{:S(2)}, u32[]{:S(2)}) collective-permute-start(bf16[64,1024]{1,0:T(8,128)(2,1)S(1)} %get-tuple-element.193.refs_9_), channel_id=1, source_target_pairs={{0,96},{16,112},{32,64},{48,80},{64,32},{80,48},{96,0},{112,16},{1... | collective-permute-start | bytes 393224 | tf_op jit(solution)/shard_map/ppermute | solution.py:59
  76.4 4.8 %collective-permute-done.15.refs_10_ = bf16[64,1024]{1,0:T(8,128)(2,1)S(1)} collective-permute-done((bf16[64,1024]{1,0:T(8,128)(2,1)S(1)}, bf16[64,1024]{1,0:T(8,128)(2,1)S(1)}, u32[]{:S(2)}, u32[]{:S(2)}) %collective-permute-start.15) | collective-permute-done | bytes 131104 | tf_op jit(solution)/shard_map/ppermute | solution.py:59
  81.8 2.2 all-to-all-done.refs_0_
  84.8 5.1 %shard_map.247 = (f32[128,1024]{1,0:T(8,128)}, bf16[64,1024]{1,0:T(8,128)(2,1)}, bf16[64,1024]{1,0:T(8,128)(2,1)}) custom-call(bf16[8,128,256]{2,1,0:T(8,128)(2,1)} %copy-done.4, bf16[128,1024]{1,0:T(8,128)(2,1)} %bitcast.40, f32[8,1024]{1,0:T(8,128)} %get-tuple-element.97.refs_2_.refs_7_, ...), custom_call_target="tpu_custom_call" | custom-call | flops 1000000000 | bytes 8388608 | tf_op jit(solution)/shard_map/pallas_call | solution.py:549
  90.0 2.8 %collective-permute-start.19 = (bf16[64,1024]{1,0:T(8,128)(2,1)}, bf16[64,1024]{1,0:T(8,128)(2,1)S(1)}, u32[]{:S(2)}, u32[]{:S(2)}) collective-permute-start(bf16[64,1024]{1,0:T(8,128)(2,1)} %get-tuple-element.103.refs_3_), channel_id=1, source_target_pairs={{0,96},{16,112},{32,64},{48,80},{64,32},{80,48},{96,0},{112,16},{1... | collective-permute-start | bytes 393224 | tf_op jit(solution)/shard_map/ppermute | solution.py:59
  92.8 2.4 collective-permute-done.17.refs_1_
  96.2 1.4 collective-permute-start.18
  99.8 4.1 %collective-permute-done.18.refs_2_ = bf16[128,1024]{1,0:T(8,128)(2,1)S(1)} collective-permute-done((bf16[128,1024]{1,0:T(8,128)(2,1)S(1)}, bf16[128,1024]{1,0:T(8,128)(2,1)S(1)}, u32[]{:S(2)}, u32[]{:S(2)}) %collective-permute-start.18) | collective-permute-done | bytes 262176 | tf_op jit(solution)/shard_map/ppermute | solution.py:59
  103.8 1.4 collective-permute-done.20.refs_5_
  106.0 12.1 %shard_map.248 = (bf16[128,1024]{1,0:T(8,128)(2,1)}, bf16[128,1024]{1,0:T(8,128)(2,1)}, f32[128,1024]{1,0:T(8,128)}, f32[128,1024]{1,0:T(8,128)}, bf16[1024,2304...) custom-call(bf16[64,1024]{1,0:T(8,128)(2,1)} %get-tuple-element.102., ...), custom_call_target="tpu_custom_call" | custom-call | flops 8000000000 | bytes 8388608 | tf_op jit(solution)/shard_map/pallas_call | solution.py:549
  119.1 3.0 %collective-permute-start.21 = (bf16[128,1024]{1,0:T(8,128)(2,1)S(1)}, bf16[128,1024]{1,0:T(8,128)(2,1)S(1)}, u32[]{:S(2)}, u32[]{:S(2)}) collective-permute-start(bf16[128,1024]{1,0:T(8,128)(2,1)S(1)} %copy-done.59), channel_id=1, source_target_pairs={{0,96},{16,112},{32,64},{48,80},{64,32},{80,48},{96,0},{112,16},{1... | collective-permute-start | bytes 786440 | tf_op jit(solution)/shard_map/ppermute | solution.py:59
  122.8 2.7 %collective-permute-start.25 = (bf16[512,256]{1,0:T(8,128)(2,1)S(1)}, bf16[512,256]{1,0:T(8,128)(2,1)S(1)}, u32[]{:S(2)}, u32[]{:S(2)}) collective-permute-start(bf16[512,256]{1,0:T(8,128)(2,1)S(1)} %bitcast.54), channel_id=1, source_target_pairs={{0,16},{16,0},{32,48},{48,32},{64,80},{80,64},{96,112},{112,96},{1... | collective-permute-start | bytes 786440 | tf_op jit(solution)/shard_map/ppermute | solution.py:59
  125.5 2.1 collective-permute-done.21
  129.0 2.3 collective-permute-start.24
  132.6 1.2 collective-permute-done.25.refs_11_
  133.8 1.3 collective-permute-done.24.refs_4_
  135.8 4.8 %shard_map.249 = (f32[128,1024]{1,0:T(8,128)}, bf16[64,1024]{1,0:T(8,128)(2,1)}, bf16[64,1024]{1,0:T(8,128)(2,1)}, bf16[8,128,256]{2,1,0:T(8,128)(2,1)}) custom-call(f32[128,1024]{1,0:T(8,128)} %get-tuple-element.107.refs_0_, bf16[64,1024]{1,0:T(8,128)(2,1)} %slice.190.refs_1_, bf16[64,1024]{1,0:T(8,128)(2,1)} %slice.191.refs_2_, ...), custom_call_target="tpu_custom_call" | custom-call | flops 1000000000 | bytes 8388608 | tf_op jit(solution)/shard_map/pallas_call | solution.py:549
  141.4 2.4 collective-permute-start.28
  143.8 5.1 %all-to-all-start.1 = ((bf16[8,128,256]{2,1,0:T(8,128)(2,1)}), bf16[8,128,256]{2,1,0:T(8,128)(2,1)S(1)}, u32[]{:S(2)}, u32[]{:S(2)}) async-start(bf16[8,128,256]{2,1,0:T(8,128)(2,1)} %get-tuple-element.122), calls=%async_computation.1 | async-start | bytes 1048576 | tf_op jit(solution)/shard_map/all_to_all | solution.py:700
  149.9 3.3 %collective-permute-start.27 = (bf16[128,1024]{1,0:T(8,128)(2,1)S(1)}, bf16[128,1024]{1,0:T(8,128)(2,1)S(1)}, u32[]{:S(2)}, u32[]{:S(2)}) collective-permute-start(bf16[128,1024]{1,0:T(8,128)(2,1)S(1)} %pad_maximum_fusion.12), channel_id=1, source_target_pairs={{0,96},{16,112},{32,64},{48,80},{64,32},{80,48},{96,0},{112,16},{1... | collective-permute-start | bytes 786440 | tf_op jit(solution)/shard_map/ppermute | solution.py:59
  153.6 8.3 %collective-permute-done.27.refs_14_ = bf16[128,1024]{1,0:T(8,128)(2,1)S(1)} collective-permute-done((bf16[128,1024]{1,0:T(8,128)(2,1)S(1)}, bf16[128,1024]{1,0:T(8,128)(2,1)S(1)}, u32[]{:S(2)}, u32[]{:S(2)}) %collective-permute-start.27) | collective-permute-done | bytes 262176 | tf_op jit(solution)/shard_map/ppermute | solution.py:59
  161.9 1.6 collective-permute-done.29.refs_17_
  163.5 1.2 collective-permute-start.30
  165.9 13.7 %shard_map.250 = (bf16[4,2,64,1152]{3,2,1,0:T(8,128)(2,1)}, bf16[4,2,64,1152]{3,2,1,0:T(8,128)(2,1)}, bf16[256,1024]{1,0:T(8,128)(2,1)}, bf16[256,1024]{1,0:T(8,...) custom-call(s32[5]{0:T(128)} %stack.23.refs_0_, bf16[1024,512]{1,0:T(8,128)(2,1)} %get-tuple-element.121.refs_1_, ...), custom_call_target="tpu_custom_call" | custom-call | flops 8000000000 | bytes 8388608 | tf_op jit(solution)/shard_map/pallas_call | solution.py:549
  181.1 2.4 collective-permute-done.32
  183.4 1.4 add_convert_fusion.11
  186.7 2.3 collective-permute-start.34
  190.8 1.4 collective-permute-start.38
  192.6 2.4 collective-permute-start.39
  195.0 1.9 collective-permute-done.33
  198.1 1.5 collective-permute-start.35
  199.5 2.3 collective-permute-start.36
  202.7 2.3 collective-permute-done.37
  205.9 1.9 add_convert_fusion.6
  207.8 2.4 collective-permute-start.42
  210.2 1.8 collective-permute-start.41
  214.0 2.1 collective-permute-start.44
  219.6 1.9 collective-permute-done.44
  222.8 3.0 %collective-permute-start.45 = (bf16[128,1024]{1,0:T(8,128)(2,1)S(1)}, bf16[128,1024]{1,0:T(8,128)(2,1)S(1)}, u32[]{:S(2)}, u32[]{:S(2)}) collective-permute-start(bf16[128,1024]{1,0:T(8,128)(2,1)S(1)} %add_convert_fusion.1), channel_id=1, source_target_pairs={{0,16},{16,0},{32,48},{48,32},{64,80},{80,64},{96,112},{112,96},{1... | collective-permute-start | bytes 786440 | tf_op jit(solution)/shard_map/ppermute | solution.py:59
  225.8 1.6 collective-permute-start.50
  227.4 1.8 collective-permute-start.49
  229.2 6.9 %collective-permute-done.50.refs_5_ = bf16[64,1152]{1,0:T(8,128)(2,1)S(1)} collective-permute-done((bf16[64,1152]{1,0:T(8,128)(2,1)S(1)}, bf16[64,1152]{1,0:T(8,128)(2,1)S(1)}, u32[]{:S(2)}, u32[]{:S(2)}) %collective-permute-start.50) | collective-permute-done | bytes 147488 | tf_op jit(solution)/shard_map/ppermute | solution.py:59
  236.8 1.4 collective-permute-start.51
  239.0 2.3 collective-permute-start.47
  242.7 4.0 %collective-permute-done.46 = bf16[64,1024]{1,0:T(8,128)(2,1)S(1)} collective-permute-done((bf16[64,1024]{1,0:T(8,128)(2,1)S(1)}, bf16[64,1024]{1,0:T(8,128)(2,1)S(1)}, u32[]{:S(2)}, u32[]{:S(2)}) %collective-permute-start.46) | collective-permute-done | bytes 131104 | tf_op jit(solution)/shard_map/ppermute | solution.py:59
  247.8 3.3 %shard_map.251 = (f32[64,3072]{1,0:T(8,128)}, f32[64,3072]{1,0:T(8,128)}, f32[64,3072]{1,0:T(8,128)}, f32[1,64]{1,0:T(1,128)}) custom-call(bf16[4,64,2304]{2,1,0:T(8,128)(2,1)} %bitcast.47, bf16[64,3072]{1,0:T(8,128)(2,1)} %refs_1_.1, bf16[64,3072]{1,0:T(8,128)(2,1)} %refs_2_.1, f32[64,1]{1,0:T(8,128)} %copy.32.refs_3_), custom_call_target="tpu_custom_call" | custom-call | bytes 8388608 | tf_op jit(solution)/shard_map/pallas_call | solution.py:549
  251.9 3.7 %shard_map.252 = (f32[64,2048]{1,0:T(8,128)}, f32[64,1024]{1,0:T(8,128)}, f32[64,1024]{1,0:T(8,128)}, f32[64,2048]{1,0:T(8,128)}, f32[1,64]{1,0:T(1,128)}, /*index=5*/f32[1,8]{1,0:T(1,128)}, f32[1,8]{1,0:T(1,128)}) custom-call(s32[5]{0:T(128)} %stack.23.refs_0_, bf16[64,1152]{1,0:T(8,128)(2,1)} %copy-done.6, bf16[64,1152]{1,0:T(8,128)(2,1)} %copy-done.13, ...), custom_call_target="tpu_custom_call" | custom-call | bytes 8388608 | tf_op jit(solution)/shard_map/pallas_call | solution.py:549
  (251 shorter events, 41.9 us)
Async XLA Ops:
  7.2 76.8 %all-gather.4.cloned.1.call-start = ((), (), s32[]{:S(2)}) async-start(), calls=%async_computation.3 | async-start | bytes 9469952 | tf_op jit(solution)/shard_map/all_gather | solution.py:636
  13.7 7.3 %collective-permute-start = (bf16[80,512]{1,0:T(8,128)(2,1)S(1)}, bf16[80,512]{1,0:T(8,128)(2,1)S(1)}, u32[]{:S(2)}, u32[]{:S(2)}) collective-permute-start(bf16[80,512]{1,0:T(8,128)(2,1)S(1)} %fusion.11), channel_id=1, source_target_pairs={{0,1},{1,0},{2,3},{3,2},{4,5},{5,4},{6,7},{7,6},{8,9},{9,8},{10,11... | collective-permute-start | bytes 245768 | tf_op jit(solution)/shard_map/ppermute | solution.py:59
  13.8 7.2 %collective-permute-start.2 = (bf16[80,512]{1,0:T(8,128)(2,1)S(1)}, bf16[80,512]{1,0:T(8,128)(2,1)S(1)}, u32[]{:S(2)}, u32[]{:S(2)}) collective-permute-start(bf16[80,512]{1,0:T(8,128)(2,1)S(1)} %fusion.11), channel_id=1, source_target_pairs={{0,3},{1,2},{2,1},{3,0},{4,7},{5,6},{6,5},{7,4},{8,11},{9,10},{10,... | collective-permute-start | bytes 245768 | tf_op jit(solution)/shard_map/ppermute | solution.py:59
  15.5 5.5 %collective-permute-start.1 = (bf16[80,512]{1,0:T(8,128)(2,1)S(1)}, bf16[80,512]{1,0:T(8,128)(2,1)S(1)}, u32[]{:S(2)}, u32[]{:S(2)}) collective-permute-start(bf16[80,512]{1,0:T(8,128)(2,1)S(1)} %fusion.11), channel_id=1, source_target_pairs={{0,2},{1,3},{2,0},{3,1},{4,6},{5,7},{6,4},{7,5},{8,10},{9,11},{10,... | collective-permute-start | bytes 245768 | tf_op jit(solution)/shard_map/ppermute | solution.py:59
  15.9 9.0 %collective-permute-start.7 = (bf16[128,1024]{1,0:T(8,128)(2,1)S(1)}, bf16[128,1024]{1,0:T(8,128)(2,1)S(1)}, u32[]{:S(2)}, u32[]{:S(2)}) collective-permute-start(bf16[128,1024]{1,0:T(8,128)(2,1)S(1)} %bitcast.41), channel_id=1, source_target_pairs={{0,32},{16,48},{32,0},{48,16},{64,96},{80,112},{96,64},{112,80},{1... | collective-permute-start | bytes 786440 | tf_op jit(solution)/shard_map/ppermute | solution.py:59
  17.9 13.4 %collective-permute-start.9 = (bf16[128,1024]{1,0:T(8,128)(2,1)S(1)}, bf16[128,1024]{1,0:T(8,128)(2,1)S(1)}, u32[]{:S(2)}, u32[]{:S(2)}) collective-permute-start(bf16[128,1024]{1,0:T(8,128)(2,1)S(1)} %bitcast.42), channel_id=1, source_target_pairs={{0,16},{16,0},{32,48},{48,32},{64,80},{80,64},{96,112},{112,96},{1... | collective-permute-start | bytes 786440 | tf_op jit(solution)/shard_map/ppermute | solution.py:59
  21.0 22.7 %copy-start.42 = (s32[1,1024]{1,0:T(1,128)S(1)}, s32[1,1024]{1,0:T(1,128)}, u32[]{:S(2)}) copy-start(s32[1,1024]{1,0:T(1,128)} %param.16) | copy-start | bytes 12292
  21.0 12.0 %collective-permute-start.3 = (bf16[160,512]{1,0:T(8,128)(2,1)S(1)}, bf16[160,512]{1,0:T(8,128)(2,1)S(1)}, u32[]{:S(2)}, u32[]{:S(2)}) collective-permute-start(bf16[160,512]{1,0:T(8,128)(2,1)S(1)} %pad_maximum_fusion.14.refs_1_), channel_id=1, source_target_pairs={{0,4},{1,5},{2,6},{3,7},{4,0},{5,1},{6,2},{7,3},{8,12},{9,13},{10,... | collective-permute-start | bytes 491528 | tf_op jit(solution)/shard_map/ppermute | solution.py:59
  22.7 13.7 %collective-permute-start.5 = (bf16[160,512]{1,0:T(8,128)(2,1)S(1)}, bf16[160,512]{1,0:T(8,128)(2,1)S(1)}, u32[]{:S(2)}, u32[]{:S(2)}) collective-permute-start(bf16[160,512]{1,0:T(8,128)(2,1)S(1)} %pad_maximum_fusion.15.refs_4_), channel_id=1, source_target_pairs={{0,12},{1,13},{2,14},{3,15},{4,8},{5,9},{6,10},{7,11},{8,4},{9,5},... | collective-permute-start | bytes 491528 | tf_op jit(solution)/shard_map/ppermute | solution.py:59
  24.9 27.4 %collective-permute-start.8 = (bf16[256,1024]{1,0:T(8,128)(2,1)S(1)}, bf16[256,1024]{1,0:T(8,128)(2,1)S(1)}, u32[]{:S(2)}, u32[]{:S(2)}) collective-permute-start(bf16[256,1024]{1,0:T(8,128)(2,1)S(1)} %pad_maximum_fusion.1), channel_id=1, source_target_pairs={{0,96},{16,112},{32,64},{48,80},{64,32},{80,48},{96,0},{112,16},{1... | collective-permute-start | bytes 1572872 | tf_op jit(solution)/shard_map/ppermute | solution.py:59
  31.3 21.0 %copy-start.50 = (bf16[128,1024]{1,0:T(8,128)(2,1)}, bf16[128,1024]{1,0:T(8,128)(2,1)S(1)}, u32[]{:S(2)}) copy-start(bf16[128,1024]{1,0:T(8,128)(2,1)S(1)} %collective-permute-done.9.refs_10_) | copy-start | bytes 786436
  31.3 8.2 %collective-permute-start.10 = (bf16[128,1024]{1,0:T(8,128)(2,1)S(1)}, bf16[128,1024]{1,0:T(8,128)(2,1)S(1)}, u32[]{:S(2)}, u32[]{:S(2)}) collective-permute-start(bf16[128,1024]{1,0:T(8,128)(2,1)S(1)} %collective-permute-done.9.refs_10_), channel_id=1, source_target_pairs={{0,32},{16,48},{32,0},{48,16},{64,96},{80,112},{96,64},{112,80},{1... | collective-permute-start | bytes 786440 | tf_op jit(solution)/shard_map/ppermute | solution.py:59
  33.0 17.9 %collective-permute-start.4 = (bf16[320,512]{1,0:T(8,128)(2,1)S(1)}, bf16[320,512]{1,0:T(8,128)(2,1)S(1)}, u32[]{:S(2)}, u32[]{:S(2)}) collective-permute-start(bf16[320,512]{1,0:T(8,128)(2,1)S(1)} %pad_maximum_fusion.2), channel_id=1, source_target_pairs={{0,12},{1,13},{2,14},{3,15},{4,8},{5,9},{6,10},{7,11},{8,4},{9,5},... | collective-permute-start | bytes 983048 | tf_op jit(solution)/shard_map/ppermute | solution.py:59
  36.4 15.9 %collective-permute-start.6 = (bf16[320,512]{1,0:T(8,128)(2,1)S(1)}, bf16[320,512]{1,0:T(8,128)(2,1)S(1)}, u32[]{:S(2)}, u32[]{:S(2)}) collective-permute-start(bf16[320,512]{1,0:T(8,128)(2,1)S(1)} %pad_maximum_fusion.3), channel_id=1, source_target_pairs={{0,4},{1,5},{2,6},{3,7},{4,0},{5,1},{6,2},{7,3},{8,12},{9,13},{10,... | collective-permute-start | bytes 983048 | tf_op jit(solution)/shard_map/ppermute | solution.py:59
  36.5 14.4 %collective-permute-start.11 = (bf16[128,1024]{1,0:T(8,128)(2,1)S(1)}, bf16[128,1024]{1,0:T(8,128)(2,1)}, u32[]{:S(2)}, u32[]{:S(2)}) collective-permute-start(bf16[128,1024]{1,0:T(8,128)(2,1)S(1)} %collective-permute-done.9.refs_10_), channel_id=1, source_target_pairs={{0,96},{16,112},{32,64},{48,80},{64,32},{80,48},{96,0},{112,16},{1... | collective-permute-start | bytes 786440 | tf_op jit(solution)/shard_map/ppermute | solution.py:59
  40.2 10.7 %collective-permute-start.12 = (bf16[128,1024]{1,0:T(8,128)(2,1)S(1)}, bf16[128,1024]{1,0:T(8,128)(2,1)}, u32[]{:S(2)}, u32[]{:S(2)}) collective-permute-start(bf16[128,1024]{1,0:T(8,128)(2,1)S(1)} %collective-permute-done.9.refs_10_), channel_id=1, source_target_pairs={{0,64},{16,80},{32,96},{48,112},{64,0},{80,16},{96,32},{112,48},{1... | collective-permute-start | bytes 786440 | tf_op jit(solution)/shard_map/ppermute | solution.py:59
  63.9 26.0 %copy-start.21 = (bf16[64,1024]{1,0:T(8,128)(2,1)}, bf16[64,1024]{1,0:T(8,128)(2,1)S(1)}, u32[]{:S(2)}) copy-start(bf16[64,1024]{1,0:T(8,128)(2,1)S(1)} %get-tuple-element.193.refs_9_) | copy-start | bytes 393220
  63.9 26.0 %copy-start.22 = (bf16[64,1024]{1,0:T(8,128)(2,1)}, bf16[64,1024]{1,0:T(8,128)(2,1)S(1)}, u32[]{:S(2)}) copy-start(bf16[64,1024]{1,0:T(8,128)(2,1)S(1)} %get-tuple-element.194.refs_6_) | copy-start | bytes 393220
  63.9 12.3 %collective-permute-start.13 = (bf16[64,1024]{1,0:T(8,128)(2,1)S(1)}, bf16[64,1024]{1,0:T(8,128)(2,1)S(1)}, u32[]{:S(2)}, u32[]{:S(2)}) collective-permute-start(bf16[64,1024]{1,0:T(8,128)(2,1)S(1)} %get-tuple-element.194.refs_6_), channel_id=1, source_target_pairs={{0,32},{16,48},{32,0},{48,16},{64,96},{80,112},{96,64},{112,80},{1... | collective-permute-start | bytes 393224 | tf_op jit(solution)/shard_map/ppermute | solution.py:59
  64.6 19.4 %all-to-all-start = ((bf16[8,128,256]{2,1,0:T(8,128)(2,1)}), bf16[8,128,256]{2,1,0:T(8,128)(2,1)S(1)}, u32[]{:S(2)}, u32[]{:S(2)}) async-start(bf16[8,128,256]{2,1,0:T(8,128)(2,1)} %bitcast.51), calls=%async_computation | async-start | bytes 1048576 | tf_op jit(solution)/shard_map/all_to_all | solution.py:657
  72.9 119.7 %reduce-scatter.2.cloned.1.call-start = ((), (), s32[]{:S(2)}) async-start(), calls=%async_computation.4 | async-start | bytes 5013504 | tf_op jit(solution)/shard_map/reduce_scatter | solution.py:692
  73.0 8.3 %collective-permute-start.15 = (bf16[64,1024]{1,0:T(8,128)(2,1)S(1)}, bf16[64,1024]{1,0:T(8,128)(2,1)S(1)}, u32[]{:S(2)}, u32[]{:S(2)}) collective-permute-start(bf16[64,1024]{1,0:T(8,128)(2,1)S(1)} %get-tuple-element.193.refs_9_), channel_id=1, source_target_pairs={{0,96},{16,112},{32,64},{48,80},{64,32},{80,48},{96,0},{112,16},{1... | collective-permute-start | bytes 393224 | tf_op jit(solution)/shard_map/ppermute | solution.py:59
  76.2 13.7 %collective-permute-start.14 = (bf16[128,1024]{1,0:T(8,128)(2,1)S(1)}, bf16[128,1024]{1,0:T(8,128)(2,1)S(1)}, u32[]{:S(2)}, u32[]{:S(2)}) collective-permute-start(bf16[128,1024]{1,0:T(8,128)(2,1)S(1)} %pad_maximum_fusion.8), channel_id=1, source_target_pairs={{0,96},{16,112},{32,64},{48,80},{64,32},{80,48},{96,0},{112,16},{1... | collective-permute-start | bytes 786440 | tf_op jit(solution)/shard_map/ppermute | solution.py:59
  81.3 8.7 %collective-permute-start.16 = (bf16[128,1024]{1,0:T(8,128)(2,1)S(1)}, bf16[128,1024]{1,0:T(8,128)(2,1)S(1)}, u32[]{:S(2)}, u32[]{:S(2)}) collective-permute-start(bf16[128,1024]{1,0:T(8,128)(2,1)S(1)} %pad_maximum_fusion.9), channel_id=1, source_target_pairs={{0,32},{16,48},{32,0},{48,16},{64,96},{80,112},{96,64},{112,80},{1... | collective-permute-start | bytes 786440 | tf_op jit(solution)/shard_map/ppermute | solution.py:59
  89.9 5.3 %collective-permute-start.17 = (bf16[64,1024]{1,0:T(8,128)(2,1)}, bf16[64,1024]{1,0:T(8,128)(2,1)S(1)}, u32[]{:S(2)}, u32[]{:S(2)}) collective-permute-start(bf16[64,1024]{1,0:T(8,128)(2,1)} %get-tuple-element.102.refs_0_), channel_id=1, source_target_pairs={{0,32},{16,48},{32,0},{48,16},{64,96},{80,112},{96,64},{112,80},{1... | collective-permute-start | bytes 393224 | tf_op jit(solution)/shard_map/ppermute | solution.py:59
  90.0 7.6 %collective-permute-start.19 = (bf16[64,1024]{1,0:T(8,128)(2,1)}, bf16[64,1024]{1,0:T(8,128)(2,1)S(1)}, u32[]{:S(2)}, u32[]{:S(2)}) collective-permute-start(bf16[64,1024]{1,0:T(8,128)(2,1)} %get-tuple-element.103.refs_3_), channel_id=1, source_target_pairs={{0,96},{16,112},{32,64},{48,80},{64,32},{80,48},{96,0},{112,16},{1... | collective-permute-start | bytes 393224 | tf_op jit(solution)/shard_map/ppermute | solution.py:59
  96.2 7.7 %collective-permute-start.18 = (bf16[128,1024]{1,0:T(8,128)(2,1)S(1)}, bf16[128,1024]{1,0:T(8,128)(2,1)S(1)}, u32[]{:S(2)}, u32[]{:S(2)}) collective-permute-start(bf16[128,1024]{1,0:T(8,128)(2,1)S(1)} %pad_maximum_fusion.10), channel_id=1, source_target_pairs={{0,96},{16,112},{32,64},{48,80},{64,32},{80,48},{96,0},{112,16},{1... | collective-permute-start | bytes 786440 | tf_op jit(solution)/shard_map/ppermute | solution.py:59
  98.6 6.7 %collective-permute-start.20 = (bf16[128,1024]{1,0:T(8,128)(2,1)S(1)}, bf16[128,1024]{1,0:T(8,128)(2,1)S(1)}, u32[]{:S(2)}, u32[]{:S(2)}) collective-permute-start(bf16[128,1024]{1,0:T(8,128)(2,1)S(1)} %pad_maximum_fusion.11), channel_id=1, source_target_pairs={{0,32},{16,48},{32,0},{48,16},{64,96},{80,112},{96,64},{112,80},{1... | collective-permute-start | bytes 786440 | tf_op jit(solution)/shard_map/ppermute | solution.py:59
  119.1 8.5 %collective-permute-start.21 = (bf16[128,1024]{1,0:T(8,128)(2,1)S(1)}, bf16[128,1024]{1,0:T(8,128)(2,1)S(1)}, u32[]{:S(2)}, u32[]{:S(2)}) collective-permute-start(bf16[128,1024]{1,0:T(8,128)(2,1)S(1)} %copy-done.59), channel_id=1, source_target_pairs={{0,96},{16,112},{32,64},{48,80},{64,32},{80,48},{96,0},{112,16},{1... | collective-permute-start | bytes 786440 | tf_op jit(solution)/shard_map/ppermute | solution.py:59
  122.0 6.5 %collective-permute-start.22 = (bf16[128,1024]{1,0:T(8,128)(2,1)S(1)}, bf16[128,1024]{1,0:T(8,128)(2,1)S(1)}, u32[]{:S(2)}, u32[]{:S(2)}) collective-permute-start(bf16[128,1024]{1,0:T(8,128)(2,1)S(1)} %copy-done.58), channel_id=1, source_target_pairs={{0,32},{16,48},{32,0},{48,16},{64,96},{80,112},{96,64},{112,80},{1... | collective-permute-start | bytes 786440 | tf_op jit(solution)/shard_map/ppermute | solution.py:59
  122.8 11.0 %collective-permute-start.25 = (bf16[512,256]{1,0:T(8,128)(2,1)S(1)}, bf16[512,256]{1,0:T(8,128)(2,1)S(1)}, u32[]{:S(2)}, u32[]{:S(2)}) collective-permute-start(bf16[512,256]{1,0:T(8,128)(2,1)S(1)} %bitcast.54), channel_id=1, source_target_pairs={{0,16},{16,0},{32,48},{48,32},{64,80},{80,64},{96,112},{112,96},{1... | collective-permute-start | bytes 786440 | tf_op jit(solution)/shard_map/ppermute | solution.py:59
  128.6 5.2 %collective-permute-start.23 = (bf16[64,1024]{1,0:T(8,128)(2,1)S(1)}, bf16[64,1024]{1,0:T(8,128)(2,1)S(1)}, u32[]{:S(2)}, u32[]{:S(2)}) collective-permute-start(bf16[64,1024]{1,0:T(8,128)(2,1)S(1)} %get-tuple-element.192), channel_id=1, source_target_pairs={{0,32},{16,48},{32,0},{48,16},{64,96},{80,112},{96,64},{112,80},{1... | collective-permute-start | bytes 393224 | tf_op jit(solution)/shard_map/ppermute | solution.py:59
  129.0 6.2 %collective-permute-start.24 = (bf16[64,1024]{1,0:T(8,128)(2,1)S(1)}, bf16[64,1024]{1,0:T(8,128)(2,1)S(1)}, u32[]{:S(2)}, u32[]{:S(2)}) collective-permute-start(bf16[64,1024]{1,0:T(8,128)(2,1)S(1)} %get-tuple-element.191), channel_id=1, source_target_pairs={{0,96},{16,112},{32,64},{48,80},{64,32},{80,48},{96,0},{112,16},{1... | collective-permute-start | bytes 393224 | tf_op jit(solution)/shard_map/ppermute | solution.py:59
  140.6 22.8 %copy-start.52 = (bf16[128,1024]{1,0:T(8,128)(2,1)S(1)}, bf16[128,1024]{1,0:T(8,128)(2,1)}, u32[]{:S(2)}) copy-start(bf16[128,1024]{1,0:T(8,128)(2,1)} %get-tuple-element.119) | copy-start | bytes 786436
  140.6 24.0 %copy-start.51 = (bf16[128,1024]{1,0:T(8,128)(2,1)S(1)}, bf16[128,1024]{1,0:T(8,128)(2,1)}, u32[]{:S(2)}) copy-start(bf16[128,1024]{1,0:T(8,128)(2,1)} %get-tuple-element.120) | copy-start | bytes 786436
  140.7 8.3 %collective-permute-start.26 = (bf16[64,1024]{1,0:T(8,128)(2,1)}, bf16[64,1024]{1,0:T(8,128)(2,1)S(1)}, u32[]{:S(2)}, u32[]{:S(2)}) collective-permute-start(bf16[64,1024]{1,0:T(8,128)(2,1)} %get-tuple-element.117.refs_12_), channel_id=1, source_target_pairs={{0,32},{16,48},{32,0},{48,16},{64,96},{80,112},{96,64},{112,80},{1... | collective-permute-start | bytes 393224 | tf_op jit(solution)/shard_map/ppermute | solution.py:59
  141.4 11.8 %collective-permute-start.28 = (bf16[64,1024]{1,0:T(8,128)(2,1)}, bf16[64,1024]{1,0:T(8,128)(2,1)S(1)}, u32[]{:S(2)}, u32[]{:S(2)}) collective-permute-start(bf16[64,1024]{1,0:T(8,128)(2,1)} %get-tuple-element.118.refs_15_), channel_id=1, source_target_pairs={{0,96},{16,112},{32,64},{48,80},{64,32},{80,48},{96,0},{112,16},{1... | collective-permute-start | bytes 393224 | tf_op jit(solution)/shard_map/ppermute | solution.py:59
  143.8 21.3 %all-to-all-start.1 = ((bf16[8,128,256]{2,1,0:T(8,128)(2,1)}), bf16[8,128,256]{2,1,0:T(8,128)(2,1)S(1)}, u32[]{:S(2)}, u32[]{:S(2)}) async-start(bf16[8,128,256]{2,1,0:T(8,128)(2,1)} %get-tuple-element.122), calls=%async_computation.1 | async-start | bytes 1048576 | tf_op jit(solution)/shard_map/all_to_all | solution.py:700
  148.9 98.9 %all-gather.6.cloned.1.call-start = ((), (), s32[]{:S(2)}) async-start(), calls=%async_computation.5 | async-start | bytes 1474560 | tf_op jit(solution)/shard_map/all_gather | solution.py:95
  149.9 11.9 %collective-permute-start.27 = (bf16[128,1024]{1,0:T(8,128)(2,1)S(1)}, bf16[128,1024]{1,0:T(8,128)(2,1)S(1)}, u32[]{:S(2)}, u32[]{:S(2)}) collective-permute-start(bf16[128,1024]{1,0:T(8,128)(2,1)S(1)} %pad_maximum_fusion.12), channel_id=1, source_target_pairs={{0,96},{16,112},{32,64},{48,80},{64,32},{80,48},{96,0},{112,16},{1... | collective-permute-start | bytes 786440 | tf_op jit(solution)/shard_map/ppermute | solution.py:59
  153.2 10.2 %collective-permute-start.29 = (bf16[128,1024]{1,0:T(8,128)(2,1)S(1)}, bf16[128,1024]{1,0:T(8,128)(2,1)S(1)}, u32[]{:S(2)}, u32[]{:S(2)}) collective-permute-start(bf16[128,1024]{1,0:T(8,128)(2,1)S(1)} %pad_maximum_fusion.13), channel_id=1, source_target_pairs={{0,32},{16,48},{32,0},{48,16},{64,96},{80,112},{96,64},{112,80},{1... | collective-permute-start | bytes 786440 | tf_op jit(solution)/shard_map/ppermute | solution.py:59
  163.5 16.1 %collective-permute-start.30 = (bf16[128,1024]{1,0:T(8,128)(2,1)S(1)}, bf16[128,1024]{1,0:T(8,128)(2,1)S(1)}, u32[]{:S(2)}, u32[]{:S(2)}) collective-permute-start(bf16[128,1024]{1,0:T(8,128)(2,1)S(1)} %copy-done.52), channel_id=1, source_target_pairs={{0,96},{16,112},{32,64},{48,80},{64,32},{80,48},{96,0},{112,16},{1... | collective-permute-start | bytes 786440 | tf_op jit(solution)/shard_map/ppermute | solution.py:59
  164.7 14.9 %collective-permute-start.31 = (bf16[128,1024]{1,0:T(8,128)(2,1)S(1)}, bf16[128,1024]{1,0:T(8,128)(2,1)S(1)}, u32[]{:S(2)}, u32[]{:S(2)}) collective-permute-start(bf16[128,1024]{1,0:T(8,128)(2,1)S(1)} %copy-done.51), channel_id=1, source_target_pairs={{0,32},{16,48},{32,0},{48,16},{64,96},{80,112},{96,64},{112,80},{1... | collective-permute-start | bytes 786440 | tf_op jit(solution)/shard_map/ppermute | solution.py:59
  180.4 3.1 %collective-permute-start.32 = (bf16[512,1152]{1,0:T(8,128)(2,1)}, bf16[512,1152]{1,0:T(8,128)(2,1)S(1)}, u32[]{:S(2)}, u32[]{:S(2)}) collective-permute-start(bf16[512,1152]{1,0:T(8,128)(2,1)} %bitcast.60), channel_id=1, source_target_pairs={{0,1},{1,0},{2,3},{3,2},{4,5},{5,4},{6,7},{7,6},{8,9},{9,8},{10,11... | collective-permute-start | bytes 3538952 | tf_op jit(solution)/shard_map/ppermute | solution.py:59
  185.6 11.4 %collective-permute-start.33 = (bf16[128,1152]{1,0:T(8,128)(2,1)}, bf16[128,1152]{1,0:T(8,128)(2,1)}, u32[]{:S(2)}, u32[]{:S(2)}) collective-permute-start(bf16[128,1152]{1,0:T(8,128)(2,1)} %pad_maximum_fusion.4), channel_id=1, source_target_pairs={{0,12},{1,13},{2,14},{3,15},{4,8},{5,9},{6,10},{7,11},{8,4},{9,5},... | collective-permute-start | bytes 884744 | tf_op jit(solution)/shard_map/ppermute | solution.py:59
  186.7 10.3 %collective-permute-start.34 = (bf16[128,1152]{1,0:T(8,128)(2,1)}, bf16[128,1152]{1,0:T(8,128)(2,1)}, u32[]{:S(2)}, u32[]{:S(2)}) collective-permute-start(bf16[128,1152]{1,0:T(8,128)(2,1)} %pad_maximum_fusion.5), channel_id=1, source_target_pairs={{0,4},{1,5},{2,6},{3,7},{4,0},{5,1},{6,2},{7,3},{8,12},{9,13},{10,... | collective-permute-start | bytes 884744 | tf_op jit(solution)/shard_map/ppermute | solution.py:59
  189.8 15.2 %collective-permute-start.37 = (bf16[256,1024]{1,0:T(8,128)(2,1)}, bf16[256,1024]{1,0:T(8,128)(2,1)S(1)}, u32[]{:S(2)}, u32[]{:S(2)}) collective-permute-start(bf16[256,1024]{1,0:T(8,128)(2,1)} %get-tuple-element.135), channel_id=1, source_target_pairs={{0,96},{16,112},{32,64},{48,80},{64,32},{80,48},{96,0},{112,16},{1... | collective-permute-start | bytes 1572872 | tf_op jit(solution)/shard_map/ppermute | solution.py:59
  190.8 14.2 %collective-permute-start.38 = (bf16[256,1024]{1,0:T(8,128)(2,1)}, bf16[256,1024]{1,0:T(8,128)(2,1)}, u32[]{:S(2)}, u32[]{:S(2)}) collective-permute-start(bf16[256,1024]{1,0:T(8,128)(2,1)} %get-tuple-element.136), channel_id=1, source_target_pairs={{0,32},{16,48},{32,0},{48,16},{64,96},{80,112},{96,64},{112,80},{1... | collective-permute-start | bytes 1572872 | tf_op jit(solution)/shard_map/ppermute | solution.py:59
  192.6 19.4 %copy-start.9 = (f32[256,1024]{1,0:T(8,128)S(1)}, f32[256,1024]{1,0:T(8,128)}, u32[]{:S(2)}) copy-start(f32[256,1024]{1,0:T(8,128)} %get-tuple-element.146) | copy-start | bytes 3145732
  192.6 13.3 %collective-permute-start.39 = (bf16[64,2304]{1,0:T(8,128)(2,1)}, bf16[64,2304]{1,0:T(8,128)(2,1)S(1)}, u32[]{:S(2)}, u32[]{:S(2)}) collective-permute-start(bf16[64,2304]{1,0:T(8,128)(2,1)} %reduce-scatter.2.cloned.1.call-done), channel_id=1, source_target_pairs={{0,16},{16,0},{32,48},{48,32},{64,80},{80,64},{96,112},{112,96},{1... | collective-permute-start | bytes 884744 | tf_op jit(solution)/shard_map/ppermute | solution.py:59
  198.1 6.9 %collective-permute-start.35 = (bf16[64,1152]{1,0:T(8,128)(2,1)S(1)}, bf16[64,1152]{1,0:T(8,128)(2,1)S(1)}, u32[]{:S(2)}, u32[]{:S(2)}) collective-permute-start(bf16[64,1152]{1,0:T(8,128)(2,1)S(1)} %get-tuple-element.178), channel_id=1, source_target_pairs={{0,4},{1,5},{2,6},{3,7},{4,0},{5,1},{6,2},{7,3},{8,12},{9,13},{10,... | collective-permute-start | bytes 442376 | tf_op jit(solution)/shard_map/ppermute | solution.py:59
  199.5 6.4 %collective-permute-start.36 = (bf16[64,1152]{1,0:T(8,128)(2,1)S(1)}, bf16[64,1152]{1,0:T(8,128)(2,1)S(1)}, u32[]{:S(2)}, u32[]{:S(2)}) collective-permute-start(bf16[64,1152]{1,0:T(8,128)(2,1)S(1)} %get-tuple-element.177), channel_id=1, source_target_pairs={{0,12},{1,13},{2,14},{3,15},{4,8},{5,9},{6,10},{7,11},{8,4},{9,5},... | collective-permute-start | bytes 442376 | tf_op jit(solution)/shard_map/ppermute | solution.py:59
  207.8 9.1 %collective-permute-start.40 = (bf16[64,1152]{1,0:T(8,128)(2,1)}, bf16[64,1152]{1,0:T(8,128)(2,1)}, u32[]{:S(2)}, u32[]{:S(2)}) collective-permute-start(bf16[64,1152]{1,0:T(8,128)(2,1)} %get-tuple-element.143), channel_id=1, source_target_pairs={{0,2},{1,3},{2,0},{3,1},{4,6},{5,7},{6,4},{7,5},{8,10},{9,11},{10,... | collective-permute-start | bytes 442376 | tf_op jit(solution)/shard_map/ppermute | solution.py:59
  207.8 10.1 %collective-permute-start.42 = (bf16[64,1152]{1,0:T(8,128)(2,1)}, bf16[64,1152]{1,0:T(8,128)(2,1)S(1)}, u32[]{:S(2)}, u32[]{:S(2)}) collective-permute-start(bf16[64,1152]{1,0:T(8,128)(2,1)} %get-tuple-element.143), channel_id=1, source_target_pairs={{0,18},{1,19},{2,16},{3,17},{4,22},{5,23},{6,20},{7,21},{8,26},{9,... | collective-permute-start | bytes 442376 | tf_op jit(solution)/shard_map/ppermute | solution.py:74
  210.2 7.7 %collective-permute-start.41 = (bf16[64,1152]{1,0:T(8,128)(2,1)}, bf16[64,1152]{1,0:T(8,128)(2,1)}, u32[]{:S(2)}, u32[]{:S(2)}) collective-permute-start(bf16[64,1152]{1,0:T(8,128)(2,1)} %get-tuple-element.142), channel_id=1, source_target_pairs={{0,16},{16,0},{32,48},{48,32},{64,80},{80,64},{96,112},{112,96},{1... | collective-permute-start | bytes 442376 | tf_op jit(solution)/shard_map/ppermute | solution.py:59
  213.1 6.5 %collective-permute-start.43 = (bf16[128,1024]{1,0:T(8,128)(2,1)S(1)}, bf16[128,1024]{1,0:T(8,128)(2,1)S(1)}, u32[]{:S(2)}, u32[]{:S(2)}) collective-permute-start(bf16[128,1024]{1,0:T(8,128)(2,1)S(1)} %get-tuple-element.184), channel_id=1, source_target_pairs={{0,32},{16,48},{32,0},{48,16},{64,96},{80,112},{96,64},{112,80},{1... | collective-permute-start | bytes 786440 | tf_op jit(solution)/shard_map/ppermute | solution.py:59
  214.0 7.6 %collective-permute-start.44 = (bf16[128,1024]{1,0:T(8,128)(2,1)S(1)}, bf16[128,1024]{1,0:T(8,128)(2,1)S(1)}, u32[]{:S(2)}, u32[]{:S(2)}) collective-permute-start(bf16[128,1024]{1,0:T(8,128)(2,1)S(1)} %get-tuple-element.183), channel_id=1, source_target_pairs={{0,96},{16,112},{32,64},{48,80},{64,32},{80,48},{96,0},{112,16},{1... | collective-permute-start | bytes 786440 | tf_op jit(solution)/shard_map/ppermute | solution.py:59
  221.5 5.8 %collective-permute-start.48 = (bf16[64,1152]{1,0:T(8,128)(2,1)S(1)}, bf16[64,1152]{1,0:T(8,128)(2,1)S(1)}, u32[]{:S(2)}, u32[]{:S(2)}) collective-permute-start(bf16[64,1152]{1,0:T(8,128)(2,1)S(1)} %add_convert_fusion.5.refs_1_), channel_id=1, source_target_pairs={{0,32},{16,48},{32,0},{48,16},{64,96},{80,112},{96,64},{112,80},{1... | collective-permute-start | bytes 442376 | tf_op jit(solution)/shard_map/ppermute | solution.py:59
  222.8 15.4 %collective-permute-start.45 = (bf16[128,1024]{1,0:T(8,128)(2,1)S(1)}, bf16[128,1024]{1,0:T(8,128)(2,1)S(1)}, u32[]{:S(2)}, u32[]{:S(2)}) collective-permute-start(bf16[128,1024]{1,0:T(8,128)(2,1)S(1)} %add_convert_fusion.1), channel_id=1, source_target_pairs={{0,16},{16,0},{32,48},{48,32},{64,80},{80,64},{96,112},{112,96},{1... | collective-permute-start | bytes 786440 | tf_op jit(solution)/shard_map/ppermute | solution.py:59
  225.8 10.2 %collective-permute-start.50 = (bf16[64,1152]{1,0:T(8,128)(2,1)S(1)}, bf16[64,1152]{1,0:T(8,128)(2,1)S(1)}, u32[]{:S(2)}, u32[]{:S(2)}) collective-permute-start(bf16[64,1152]{1,0:T(8,128)(2,1)S(1)} %add_convert_fusion.4.refs_4_), channel_id=1, source_target_pairs={{0,96},{16,112},{32,64},{48,80},{64,32},{80,48},{96,0},{112,16},{1... | collective-permute-start | bytes 442376 | tf_op jit(solution)/shard_map/ppermute | solution.py:59
  227.4 23.7 %collective-permute-start.49 = (bf16[128,1152]{1,0:T(8,128)(2,1)S(1)}, bf16[128,1152]{1,0:T(8,128)(2,1)S(1)}, u32[]{:S(2)}, u32[]{:S(2)}) collective-permute-start(bf16[128,1152]{1,0:T(8,128)(2,1)S(1)} %pad_maximum_fusion.6), channel_id=1, source_target_pairs={{0,96},{16,112},{32,64},{48,80},{64,32},{80,48},{96,0},{112,16},{1... | collective-permute-start | bytes 884744 | tf_op jit(solution)/shard_map/ppermute | solution.py:59
  236.8 14.3 %collective-permute-start.51 = (bf16[128,1152]{1,0:T(8,128)(2,1)}, bf16[128,1152]{1,0:T(8,128)(2,1)S(1)}, u32[]{:S(2)}, u32[]{:S(2)}) collective-permute-start(bf16[128,1152]{1,0:T(8,128)(2,1)} %pad_maximum_fusion.7), channel_id=1, source_target_pairs={{0,32},{16,48},{32,0},{48,16},{64,96},{80,112},{96,64},{112,80},{1... | collective-permute-start | bytes 884744 | tf_op jit(solution)/shard_map/ppermute | solution.py:59
  238.3 8.5 %collective-permute-start.46 = (bf16[64,1024]{1,0:T(8,128)(2,1)S(1)}, bf16[64,1024]{1,0:T(8,128)(2,1)S(1)}, u32[]{:S(2)}, u32[]{:S(2)}) collective-permute-start(bf16[64,1024]{1,0:T(8,128)(2,1)S(1)} %get-tuple-element.187), channel_id=1, source_target_pairs={{0,32},{16,48},{32,0},{48,16},{64,96},{80,112},{96,64},{112,80},{1... | collective-permute-start | bytes 393224 | tf_op jit(solution)/shard_map/ppermute | solution.py:59
  239.0 7.9 %collective-permute-start.47 = (bf16[64,1024]{1,0:T(8,128)(2,1)S(1)}, bf16[64,1024]{1,0:T(8,128)(2,1)S(1)}, u32[]{:S(2)}, u32[]{:S(2)}) collective-permute-start(bf16[64,1024]{1,0:T(8,128)(2,1)S(1)} %get-tuple-element.188), channel_id=1, source_target_pairs={{0,96},{16,112},{32,64},{48,80},{64,32},{80,48},{96,0},{112,16},{1... | collective-permute-start | bytes 393224 | tf_op jit(solution)/shard_map/ppermute | solution.py:59
  (56 other events, 425.1 us)
Sparse Core Ops, SparseCore 0:
  11.2 66.4 all-gather.3
  118.3 74.2 reduce-scatter.1
  217.0 28.5 all-gather.5
